TPU v7x, 32 devices: a whole 2x2x4 slice. The times are simulated.
32 devices in a mesh: batch: 4 (over z), ha: 2 (over core), wa: 4 (over y, x).
Axes of the slice: x: 2, y: 2, z: 4, core: 2. Of those that a mesh axis runs over, the one named last changes fastest.
Arguments:
- clip_features: bfloat16 [128, 16, 16, 832], P('batch', 'ha', 'wa'), may hold values from -6 to 6
- frame_counts: int32 [8], P('batch'), may hold values from 2 to 16, as said below
- w_reduce: bfloat16 [2, 832, 448], replicated, may hold values from -0.21875 to 0.21875
- w_mid: bfloat16 [2, 27, 160, 320], replicated, may hold values from -0.09375 to 0.09375
- w_small: bfloat16 [2, 27, 32, 128], replicated, may hold values from -0.21875 to 0.21875
- w_pool: bfloat16 [2, 832, 128], replicated, may hold values from -0.21875 to 0.21875
- norm_gain: float32 [2, 1024], replicated, may hold values from 0.5 to 1.5
- norm_bias: float32 [2, 1024], replicated, may hold values from -3 to 3
- out_grad: bfloat16 [64, 8, 8, 832], P('batch', 'ha', 'wa'), may hold values from -6 to 6
Outputs:
- block_output: bfloat16 [64, 8, 8, 832], P('batch', 'ha', 'wa')
- input_grad: bfloat16 [128, 16, 16, 832], P('batch', 'ha', 'wa')
- reduce_grad: float32 [2, 832, 448], replicated
- mid_grad: float32 [2, 27, 160, 320], replicated
- small_grad: float32 [2, 27, 32, 128], replicated
- pool_grad: float32 [2, 832, 128], replicated
- gain_grad: float32 [2, 1024], replicated
- bias_grad: float32 [2, 1024], replicated
Inputs may be any that keep to these rules, and one draw needn't show every extreme that they name: `frame_counts`: even; some clip has 16 frames and some 2.
All inputs are finite; a program needn't handle non-finite values.
Results may differ from a plain program's by a relative error of at most 0.015.
Values may be sent and summed in bfloat16 or wider, within the bound.
A program may use at most 192 MiB of HBM per device.

v0:
```python
import jax
import jax.numpy as jnp
from jax import lax
from jax.sharding import PartitionSpec as P

HEIGHT = 14


EPSILON = 1e-05


def padded_2(block, sides, width):
    for axis, dim in sides:
        count = lax.axis_size(axis)
        forward = [(i, i + 1) for i in range(count - 1)]
        backward = [(target, source) for source, target in forward]
        low = lax.ppermute(
            lax.slice_in_dim(block, block.shape[dim] - width, None, axis=dim), axis, forward
        )
        high = lax.ppermute(lax.slice_in_dim(block, 0, width, axis=dim), axis, backward)
        block = jnp.concatenate([low, block, high], axis=dim)
    return block


def validity(frame_counts, slot_len, tile_rows, tile_cols, height):
    grid_shape = (frame_counts.shape[0], slot_len, tile_rows, tile_cols, 1)
    frame_at = lax.broadcasted_iota(jnp.int32, grid_shape, 1)
    row_at = lax.broadcasted_iota(jnp.int32, grid_shape, 2) + lax.axis_index("ha") * tile_rows
    col_at = lax.broadcasted_iota(jnp.int32, grid_shape, 3) + lax.axis_index("wa") * tile_cols
    inside = (
        (frame_at < frame_counts[:, None, None, None, None]) & (row_at < height) & (col_at < height)
    )
    return inside.astype(jnp.float32)


def pad_frames(extended):
    return jnp.pad(extended, ((0, 0), (1, 1), (0, 0), (0, 0), (0, 0)))


def window_slice(padded, offset, extent):
    slot_len, tile_rows, tile_cols = extent
    off_time, off_row, off_col = (offset // 9, offset // 3 % 3, offset % 3)
    window = padded[
        :,
        off_time : off_time + slot_len,
        off_row : off_row + tile_rows,
        off_col : off_col + tile_cols,
        :,
    ]
    return window.reshape(-1, padded.shape[-1])


def conv_forward(padded, kernel, extent):
    summed = jnp.dot(window_slice(padded, 0, extent), kernel[0], preferred_element_type=jnp.float32)
    for offset in range(1, 27):
        summed = summed + jnp.dot(
            window_slice(padded, offset, extent), kernel[offset], preferred_element_type=jnp.float32
        )
    return summed


def conv_input_grad(padded, kernel, extent):
    summed = jnp.einsum(
        "vo,io->vi", window_slice(padded, 26, extent), kernel[0], preferred_element_type=jnp.float32
    )
    for offset in range(1, 27):
        summed = summed + jnp.einsum(
            "vo,io->vi",
            window_slice(padded, 26 - offset, extent),
            kernel[offset],
            preferred_element_type=jnp.float32,
        )
    return summed


def conv_kernel_grad(padded, grad_low, extent):
    return jnp.stack(
        [
            jnp.einsum(
                "vi,vo->io",
                window_slice(padded, offset, extent),
                grad_low,
                preferred_element_type=jnp.float32,
            )
            for offset in range(27)
        ]
    )


def box_sum(padded, extent):
    summed = window_slice(padded, 0, extent).astype(jnp.float32)
    for offset in range(1, 27):
        summed = summed + window_slice(padded, offset, extent).astype(jnp.float32)
    return summed


def norm_sums(partial_value):
    return lax.psum((partial_value[0], partial_value[1], partial_value[2]), ("batch", "ha", "wa"))


def slope_totals(partial_value):
    return lax.psum((partial_value[0], partial_value[1]), ("batch", "ha", "wa"))


def norm_forward(volume, flat_inside, gain_vec, bias_vec):
    total_sum, square_sum, count_sum = norm_sums(
        (
            jnp.sum(volume * flat_inside, axis=0),
            jnp.sum(volume * volume * flat_inside, axis=0),
            jnp.sum(flat_inside),
        )
    )
    average = total_sum / count_sum
    variance = square_sum / count_sum - average * average
    inv_std = lax.rsqrt(variance + EPSILON)
    normed = (volume - average) * inv_std
    affine = normed * gain_vec + bias_vec
    return (jax.nn.softplus(affine) * flat_inside, (normed, affine, inv_std, count_sum))


def norm_backward(out_slope, flat_inside, stored, gain_vec):
    normed, affine, inv_std, count_sum = stored
    affine_grad = out_slope * flat_inside * jax.nn.sigmoid(affine)
    bias_grad, gain_grad = slope_totals(
        (jnp.sum(affine_grad, axis=0), jnp.sum(affine_grad * normed, axis=0))
    )
    pre_grad = (
        gain_vec
        * inv_std
        * (affine_grad - (bias_grad + normed * gain_grad) / count_sum)
        * flat_inside
    )
    return (pre_grad, gain_grad, bias_grad)


def layer_forward(features, inside, params):
    w_reduce, w_mid, w_small, w_pool, gain_vec, bias_vec = params
    clip_count, slot_len, tile_rows, tile_cols, channels = features.shape
    extent = (slot_len, tile_rows, tile_cols)
    flat_inside = inside.reshape(-1, 1)
    reduce_width = w_reduce.shape[1]
    mid_in = w_mid.shape[1]
    small_in = w_small.shape[1]
    first_width = reduce_width - mid_in - small_in
    block_in = (features.astype(jnp.float32) * inside).astype(jnp.bfloat16)
    flat_in = block_in.reshape(-1, channels)
    reduced = jnp.dot(flat_in, w_reduce, preferred_element_type=jnp.float32)
    first_out, first_stored = norm_forward(
        reduced, flat_inside, gain_vec[:reduce_width], bias_vec[:reduce_width]
    )
    narrow = first_out[:, first_width:].astype(jnp.bfloat16)
    projected = jnp.dot(flat_in, w_pool, preferred_element_type=jnp.float32).astype(jnp.bfloat16)
    joined = jnp.concatenate([narrow, projected], axis=1).reshape(
        clip_count, slot_len, tile_rows, tile_cols, -1
    )
    extended = pad_frames(padded_2(joined, (("ha", 2), ("wa", 3)), 1))
    mid_pad = extended[..., :mid_in]
    small_pad = extended[..., mid_in : mid_in + small_in]
    projected_pad = extended[..., mid_in + small_in :]
    second = jnp.concatenate(
        [
            conv_forward(mid_pad, w_mid, extent),
            conv_forward(small_pad, w_small, extent),
            box_sum(projected_pad, extent) / 27.0,
        ],
        axis=1,
    )
    second_out, second_stored = norm_forward(
        second, flat_inside, gain_vec[reduce_width:], bias_vec[reduce_width:]
    )
    output = jnp.concatenate([first_out[:, :first_width], second_out], axis=1)
    stored = (block_in, mid_pad, small_pad, first_stored, second_stored)
    return (output.reshape(clip_count, slot_len, tile_rows, tile_cols, -1), stored)


def layer_backward(slope_out, inside, params, stored):
    w_reduce, w_mid, w_small, w_pool, gain_vec, bias_vec = params
    block_in, mid_pad, small_pad, first_stored, second_stored = stored
    clip_count, slot_len, tile_rows, tile_cols, channels = block_in.shape
    extent = (slot_len, tile_rows, tile_cols)
    flat_inside = inside.reshape(-1, 1)
    flat_in = block_in.reshape(-1, channels)
    reduce_width = w_reduce.shape[1]
    first_width = reduce_width - w_mid.shape[1] - w_small.shape[1]
    mid_out = w_mid.shape[2]
    small_out = w_small.shape[2]
    flat_slope = slope_out.reshape(-1, slope_out.shape[-1])
    second_pre, second_gain, second_bias = norm_backward(
        flat_slope[:, first_width:], flat_inside, second_stored, gain_vec[reduce_width:]
    )
    second_low = second_pre.astype(jnp.bfloat16)
    mid_slope = second_low[:, :mid_out]
    small_slope = second_low[:, mid_out : mid_out + small_out]
    mid_kernel = conv_kernel_grad(mid_pad, mid_slope, extent)
    small_kernel = conv_kernel_grad(small_pad, small_slope, extent)
    joined = second_low.reshape(clip_count, slot_len, tile_rows, tile_cols, -1)
    extended = pad_frames(padded_2(joined, (("ha", 2), ("wa", 3)), 1))
    mid_back = conv_input_grad(extended[..., :mid_out], w_mid, extent)
    small_back = conv_input_grad(extended[..., mid_out : mid_out + small_out], w_small, extent)
    projected_slope = (box_sum(extended[..., mid_out + small_out :], extent) / 27.0).astype(
        jnp.bfloat16
    )
    pool_kernel = jnp.einsum(
        "vi,vo->io", flat_in, projected_slope, preferred_element_type=jnp.float32
    )
    first_slope = jnp.concatenate([flat_slope[:, :first_width], mid_back, small_back], axis=1)
    first_pre, first_gain, first_bias = norm_backward(
        first_slope, flat_inside, first_stored, gain_vec[:reduce_width]
    )
    first_low = first_pre.astype(jnp.bfloat16)
    reduce_kernel = jnp.einsum("vi,vo->io", flat_in, first_low, preferred_element_type=jnp.float32)
    input_slope = (
        jnp.einsum("vo,io->vi", first_low, w_reduce, preferred_element_type=jnp.float32)
        + jnp.einsum("vo,io->vi", projected_slope, w_pool, preferred_element_type=jnp.float32)
    ) * flat_inside
    kernels = (reduce_kernel, mid_kernel, small_kernel, pool_kernel)
    norm_grads = (
        jnp.concatenate([first_gain, second_gain]),
        jnp.concatenate([first_bias, second_bias]),
    )
    return (
        input_slope.reshape(clip_count, slot_len, tile_rows, tile_cols, channels),
        kernels,
        norm_grads,
    )


def on_device(
    clip_features, frame_counts, w_reduce, w_mid, w_small, w_pool, norm_gain, norm_bias, out_grad
):
    frames_dev, tile_rows, tile_cols, channels = clip_features.shape
    clip_count = frame_counts.shape[0]
    slot_len = frames_dev // clip_count
    first_inside = validity(frame_counts, slot_len, tile_rows, tile_cols, HEIGHT)
    second_inside = validity(
        frame_counts // 2, slot_len // 2, tile_rows // 2, tile_cols // 2, HEIGHT // 2
    )
    first_params = (w_reduce[0], w_mid[0], w_small[0], w_pool[0], norm_gain[0], norm_bias[0])
    second_params = (w_reduce[1], w_mid[1], w_small[1], w_pool[1], norm_gain[1], norm_bias[1])
    features = clip_features.reshape(clip_count, slot_len, tile_rows, tile_cols, channels)
    first_out, first_stored = layer_forward(features, first_inside, first_params)
    halved = first_out.reshape(
        clip_count, slot_len // 2, 2, tile_rows // 2, 2, tile_cols // 2, 2, channels
    )
    halved = jnp.mean(halved, axis=(2, 4, 6)).astype(jnp.bfloat16)
    second_out, second_stored = layer_forward(halved, second_inside, second_params)
    block_output = second_out.astype(jnp.bfloat16).reshape(
        frames_dev // 2, tile_rows // 2, tile_cols // 2, channels
    )
    incoming = out_grad.astype(jnp.float32).reshape(
        clip_count, slot_len // 2, tile_rows // 2, tile_cols // 2, channels
    )
    second_slope, second_kernels, second_norms = layer_backward(
        incoming, second_inside, second_params, second_stored
    )
    spread = jnp.broadcast_to(
        second_slope[:, :, None, :, None, :, None, :] / 8.0,
        (clip_count, slot_len // 2, 2, tile_rows // 2, 2, tile_cols // 2, 2, channels),
    )
    spread = spread.reshape(clip_count, slot_len, tile_rows, tile_cols, channels)
    first_slope, first_kernels, first_norms = layer_backward(
        spread, first_inside, first_params, first_stored
    )
    summed = lax.psum(
        (
            first_kernels[0],
            first_kernels[1],
            first_kernels[2],
            first_kernels[3],
            second_kernels[0],
            second_kernels[1],
            second_kernels[2],
            second_kernels[3],
        ),
        ("batch", "ha", "wa"),
    )
    first_kernels = summed[:4]
    second_kernels = summed[4:]
    input_grad = first_slope.astype(jnp.bfloat16).reshape(
        frames_dev, tile_rows, tile_cols, channels
    )
    reduce_grad = jnp.stack([first_kernels[0], second_kernels[0]])
    mid_grad = jnp.stack([first_kernels[1], second_kernels[1]])
    small_grad = jnp.stack([first_kernels[2], second_kernels[2]])
    pool_grad = jnp.stack([first_kernels[3], second_kernels[3]])
    gain_grad = jnp.stack([first_norms[0], second_norms[0]])
    bias_grad = jnp.stack([first_norms[1], second_norms[1]])
    return (
        block_output,
        input_grad,
        reduce_grad,
        mid_grad,
        small_grad,
        pool_grad,
        gain_grad,
        bias_grad,
    )


def solution(mesh):
    in_specs = (
        P("batch", "ha", "wa", None),
        P("batch"),
        P(),
        P(),
        P(),
        P(),
        P(),
        P(),
        P("batch", "ha", "wa", None),
    )
    out_specs = (
        P("batch", "ha", "wa", None),
        P("batch", "ha", "wa", None),
        P(),
        P(),
        P(),
        P(),
        P(),
        P(),
    )
    return jax.shard_map(
        on_device, mesh=mesh, in_specs=in_specs, out_specs=out_specs, check_vma=False
    )
```

profile of v0, /device:TPU:0, one launch (start us, length us, event | category | flops | bytes accessed | tf_op | source)
XLA Modules:
  0.0 1666.8 jit_solution(10062565480506845226)
XLA Ops:
  13.2 3.5 multiply_convert_fusion
  16.7 3.0 convert_element_type.759
  20.5 3.6 multiply_reduce_fusion.5
  24.1 42.2 %all-reduce.11 = (f32[448]{0:T(512)S(1)}, f32[]{:T(128)}, f32[448]{0:T(512)S(1)}) all-reduce(f32[448]{0:T(512)S(1)} %get-tuple-element.21, f32[]{:T(128)} %fusion.507, f32[448]{0:T(512)S(1)} %get-tuple-element.20), channel_id=1, replica_groups=mesh['batch'=4,'ha'=2,'wa'=4] {'batch','ha','wa'}, use_global_device_ids=true, to_apply=%region_5.6 | all-reduce | flops 897 | bytes 7176 | tf_op jit(solution)/shard_map/psum | solution.py:98
  67.4 3.1 fusion.14
  74.6 4.5 collective-permute-start
  89.1 5.2 copy.291
  96.1 2.3 fusion.346
  107.4 4.2 collective-permute-start.2
  113.2 2.4 fusion.355
  115.6 2.4 fusion.338
  121.0 12.6 collective-permute-done.3
  135.4 3.5 fusion.900
  138.8 4.5 fusion.899
  143.3 7.0 fusion.898
  156.5 4.6 fusion.225
  168.8 18.5 %add_add_fusion = f32[2,16,8,4,128]{4,3,2,1,0:T(4,128)} fusion(bf16[2,16,10,1,320]{4,3,2,1,0:T(2,128)(2,1)S(1)} %copy-done.10, bf16[2,16,10,4,320]{4,3,2,1,0:T(4,128)(2,1)S(1)} %get-tuple-element.349, bf16[2,16,10,1,320]{4,3,2,1,0:T(2,128)(2,1)S(1)} %copy-done.8, bf16[2,16,8,4,320]{4,3,2,1,0:T(4,128)(2,1)} %copy-done.11, ...), kind=kLoop, calls=%fused_computation.618 | loop fusion | flops 5373952 | bytes 4636672 | tf_op jit(solution)/shard_map/add | solution.py:93
  189.3 5.5 fusion.206
  205.7 2.4 fusion.341
  208.1 2.3 fusion.335
  257.8 2.3 reshape.1526
  290.4 2.6 reshape.1502
  334.1 39.6 %all-reduce.10 = (f32[576]{0:T(1024)S(1)}, f32[576]{0:T(1024)S(1)}) all-reduce(f32[576]{0:T(1024)S(1)} %get-tuple-element.17, f32[576]{0:T(1024)S(1)} %get-tuple-element.16), channel_id=1, replica_groups=mesh['batch'=4,'ha'=2,'wa'=4] {'batch','ha','wa'}, use_global_device_ids=true, to_apply=%region_7.8 | all-reduce | flops 1152 | bytes 9216 | tf_op jit(solution)/shard_map/psum | solution.py:98
  375.5 2.6 fusion.10
  380.3 4.9 copy.134
  385.2 5.4 reshape_reshape.12
  390.6 4.3 reduce_sum.184
  400.1 39.4 %all-reduce.9 = (f32[448]{0:T(512)S(1)}, f32[]{:T(128)}, f32[448]{0:T(512)S(1)}) all-reduce(f32[448]{0:T(512)S(1)} %get-tuple-element.29, f32[]{:T(128)} %fusion.779, f32[448]{0:T(512)S(1)} %get-tuple-element.28), channel_id=1, replica_groups=mesh['batch'=4,'ha'=2,'wa'=4] {'batch','ha','wa'}, use_global_device_ids=true, to_apply=%region_16.17 | all-reduce | flops 897 | bytes 7176 | tf_op jit(solution)/shard_map/psum | solution.py:98
  451.6 4.2 collective-permute-start.6
  623.8 40.1 %all-reduce.8 = (f32[576]{0:T(1024)S(1)}, f32[576]{0:T(1024)S(1)}) all-reduce(f32[576]{0:T(1024)S(1)} %get-tuple-element.25, f32[576]{0:T(1024)S(1)} %get-tuple-element.24), channel_id=1, replica_groups=mesh['batch'=4,'ha'=2,'wa'=4] {'batch','ha','wa'}, use_global_device_ids=true, to_apply=%region_18.19 | all-reduce | flops 1152 | bytes 9216 | tf_op jit(solution)/shard_map/psum | solution.py:98
  666.9 40.3 %all-reduce.7 = (f32[576]{0:T(1024)S(1)}, f32[576]{0:T(1024)S(1)}) all-reduce(f32[576]{0:T(1024)S(1)} %get-tuple-element.27, f32[576]{0:T(1024)S(1)} %get-tuple-element.26), channel_id=1, replica_groups=mesh['batch'=4,'ha'=2,'wa'=4] {'batch','ha','wa'}, use_global_device_ids=true, to_apply=%region_24.25 | all-reduce | flops 1152 | bytes 9216 | tf_op jit(solution)/shard_map/psum | solution.py:102
  713.1 3.2 collective-permute-start.8
  779.6 4.2 collective-permute-start.10
  924.7 41.2 %all-reduce.6 = (f32[448]{0:T(512)S(1)}, f32[448]{0:T(512)S(1)}) all-reduce(f32[448]{0:T(512)S(1)} %get-tuple-element.31, f32[448]{0:T(512)S(1)} %get-tuple-element.30), channel_id=1, replica_groups=mesh['batch'=4,'ha'=2,'wa'=4] {'batch','ha','wa'}, use_global_device_ids=true, to_apply=%region_28.29 | all-reduce | flops 896 | bytes 7168 | tf_op jit(solution)/shard_map/psum | solution.py:102
  966.0 2.6 fusion.183
  970.3 3.1 broadcast_in_dim.2
  973.4 5.5 reshape_reshape.15
  978.9 3.4 slice.3243
  982.3 3.2 copy.298
  985.5 4.0 fusion.888
  989.5 40.5 %all-reduce.5 = (f32[576]{0:T(1024)S(1)}, f32[576]{0:T(1024)}) all-reduce(f32[576]{0:T(1024)S(1)} %get-tuple-element.19, f32[576]{0:T(1024)S(1)} %get-tuple-element.18), channel_id=1, replica_groups=mesh['batch'=4,'ha'=2,'wa'=4] {'batch','ha','wa'}, use_global_device_ids=true, to_apply=%region_32.33 | all-reduce | flops 1152 | bytes 9216 | tf_op jit(solution)/shard_map/psum | solution.py:102
  1030.0 4.3 multiply_convert_fusion.3
  1036.6 2.6 reshape.1664
  1071.7 4.5 collective-permute-start.12
  1114.0 4.9 collective-permute-start.14
  1120.3 2.3 convolution_bitcast_fusion
  1132.3 4.7 collective-permute-done.15
  1138.7 5.0 fusion.216
  1143.7 2.9 fusion.6
  1146.6 6.4 fusion.192
  1153.0 9.5 multiply_convert_fusion.8
  1162.5 5.4 fusion.897
  1168.0 8.4 fusion.896
  1183.2 2.4 fusion.351
  1205.6 2.3 reshape.1687
  1223.8 2.5 reshape.1670
  1295.0 39.4 %all-reduce.4 = (f32[448]{0:T(512)S(1)}, f32[448]{0:T(512)S(1)}) all-reduce(f32[448]{0:T(512)S(1)} %get-tuple-element.23, f32[448]{0:T(512)S(1)} %get-tuple-element.22), channel_id=1, replica_groups=mesh['batch'=4,'ha'=2,'wa'=4] {'batch','ha','wa'}, use_global_device_ids=true, to_apply=%region_36.37 | all-reduce | flops 896 | bytes 7168 | tf_op jit(solution)/shard_map/psum | solution.py:102
  1334.4 4.1 multiply_convert_fusion.4
  1338.5 2.4 fusion.18
  1344.3 2.3 multiply_convert_fusion.2
  1346.6 3.2 copy.290
  1352.7 290.3 %all-reduce.15.cloned.1.call-done = (f32[1,832,448]{1,2,0:T(8,128)}, f32[1,832,448]{1,2,0:T(8,128)}, f32[1,27,160,320]{3,2,1,0:T(8,128)}, f32[1,27,160,320]{3,2,...) async-done(((f32[1,832,448]{1,2,0:T(8,128)}, f32[1,832,448]{1,2,0:T(8,128)}, ...) | async-done | bytes 15777808 | tf_op jit(solution)/shard_map/psum | solution.py:264
  1643.0 3.9 pad_maximum_fusion.2
  1648.8 10.7 pad_maximum_fusion
  (1553 shorter events, 788.1 us)
Async XLA Ops:
  7.2 1635.8 %all-reduce.15.cloned.1.call-start = ((), (), s32[]{:S(2)}) async-start(), calls=%async_computation | async-start | bytes 36438016 | tf_op jit(solution)/shard_map/psum | solution.py:264
  11.5 55.8 %copy-start.373 = (f32[1,448]{1,0:T(1,128)}, f32[1,448]{1,0:T(1,128)S(1)}, u32[]{:S(2)}) copy-start(f32[1,448]{1,0:T(1,128)S(1)} %get-tuple-element.357) | copy-start | bytes 5380
  12.9 54.5 %copy-start.383 = (f32[1,448]{1,0:T(1,128)}, f32[1,448]{1,0:T(1,128)S(1)}, u32[]{:S(2)}) copy-start(f32[1,448]{1,0:T(1,128)S(1)} %get-tuple-element.359) | copy-start | bytes 5380
  73.3 27.6 %collective-permute-start.1 = (bf16[2,16,1,4,320]{4,3,2,1,0:T(4,128)(2,1)}, bf16[2,16,1,4,320]{4,3,2,1,0:T(4,128)(2,1)}, u32[]{:S(2)}, u32[]{:S(2)}) collective-permute-start(bf16[2,16,1,4,320]{4,3,2,1,0:T(4,128)(2,1)} %get-tuple-element.241), channel_id=1, source_target_pairs={{4,0},{5,1},{6,2},{7,3},{12,8},{13,9},{14,10},{15,11},{20,16},{21,... | collective-permute-start | bytes 245768 | tf_op jit(solution)/shard_map/ppermute | solution.py:20
  74.6 24.6 %collective-permute-start = (bf16[2,16,1,4,320]{4,3,2,1,0:T(4,128)(2,1)}, bf16[2,16,1,4,320]{4,3,2,1,0:T(4,128)(2,1)}, u32[]{:S(2)}, u32[]{:S(2)}) collective-permute-start(bf16[2,16,1,4,320]{4,3,2,1,0:T(4,128)(2,1)} %get-tuple-element.242), channel_id=1, source_target_pairs={{0,4},{1,5},{2,6},{3,7},{8,12},{9,13},{10,14},{11,15},{16,20},{17,... | collective-permute-start | bytes 245768 | tf_op jit(solution)/shard_map/ppermute | solution.py:17
  107.4 13.6 collective-permute-start.2
  111.6 22.0 %collective-permute-start.3 = (bf16[2,16,10,1,320]{4,3,2,1,0:T(2,128)(2,1)S(1)}, bf16[2,16,10,1,320]{4,3,2,1,0:T(2,128)(2,1)S(1)}, u32[]{:S(2)}, u32[]{:S(2)}) collective-permute-start(bf16[2,16,10,1,320]{4,3,2,1,0:T(2,128)(2,1)S(1)} %get-tuple-element.237), channel_id=1, source_target_pairs={{1,0},{2,1},{3,2},{5,4},{6,5},{7,6},{9,8},{10,9},{11,10},{13,12},{... | collective-permute-start | bytes 614408 | tf_op jit(solution)/shard_map/ppermute | solution.py:20
  143.3 82.4 %copy-start.48 = (bf16[2,16,8,4,32]{4,3,2,1,0:T(4,128)(2,1)}, bf16[2,16,8,4,32]{4,3,2,1,0:T(4,128)(2,1)S(1)}, u32[]{:S(2)}) copy-start(bf16[2,16,8,4,32]{4,3,2,1,0:T(4,128)(2,1)S(1)} %get-tuple-element.141) | copy-start | bytes 196612
  257.8 63.7 %copy-start.114 = (bf16[1024,160]{1,0:T(8,128)(2,1)}, bf16[1024,160]{1,0:T(8,128)(2,1)S(1)}, u32[]{:S(2)}) copy-start(bf16[1024,160]{1,0:T(8,128)(2,1)S(1)} %reshape.1500) | copy-start | bytes 983044
  333.6 41.9 %copy-start.367 = (f32[576]{0:T(1024)S(1)}, f32[576]{0:T(1024)}, u32[]{:S(2)}) copy-start(f32[576]{0:T(1024)} %get-tuple-element.34) | copy-start | bytes 6916
  395.0 44.6 %copy-start.375 = (f32[1,448]{1,0:T(1,128)S(1)}, f32[1,448]{1,0:T(1,128)}, u32[]{:S(2)}) copy-start(f32[1,448]{1,0:T(1,128)} %get-tuple-element.356) | copy-start | bytes 5380
  395.0 45.8 %copy-start.385 = (f32[1,448]{1,0:T(1,128)S(1)}, f32[1,448]{1,0:T(1,128)}, u32[]{:S(2)}) copy-start(f32[1,448]{1,0:T(1,128)} %get-tuple-element.358) | copy-start | bytes 5380
  396.2 49.2 %copy-start.188 = (f32[2,8,4,2,832]{4,3,2,1,0:T(2,128)S(1)}, f32[2,8,4,2,832]{4,3,2,1,0:T(2,128)}, u32[]{:S(2)}) copy-start(f32[2,8,4,2,832]{4,3,2,1,0:T(2,128)} %get-tuple-element.288) | copy-start | bytes 1277956
  400.1 58.1 %copy-start.185 = (f32[128,448]{0,1:T(8,128)}, f32[128,448]{0,1:T(8,128)S(1)}, u32[]{:S(2)}) copy-start(f32[128,448]{0,1:T(8,128)S(1)} %get-tuple-element.363) | copy-start | bytes 688132
  442.6 7.1 collective-permute-start.4
  448.5 3.1 collective-permute-start.5
  451.6 8.9 collective-permute-start.6
  455.8 6.2 collective-permute-start.7
  459.7 122.7 %copy-start.324 = (bf16[2,8,4,2,32]{4,3,2,1,0:T(2,128)(2,1)}, bf16[2,8,4,2,32]{4,3,2,1,0:T(2,128)(2,1)S(1)}, u32[]{:S(2)}) copy-start(bf16[2,8,4,2,32]{4,3,2,1,0:T(2,128)(2,1)S(1)} %copy.176) | copy-start | bytes 24580
  468.6 115.4 %copy-start.329 = (bf16[2,8,4,2,32]{4,3,2,1,0:T(2,128)(2,1)}, bf16[2,8,4,2,32]{4,3,2,1,0:T(2,128)(2,1)S(1)}, u32[]{:S(2)}) copy-start(bf16[2,8,4,2,32]{4,3,2,1,0:T(2,128)(2,1)S(1)} %copy.181) | copy-start | bytes 24580
  469.3 114.1 %copy-start.331 = (bf16[2,8,4,2,32]{4,3,2,1,0:T(2,128)(2,1)}, bf16[2,8,4,2,32]{4,3,2,1,0:T(2,128)(2,1)S(1)}, u32[]{:S(2)}) copy-start(bf16[2,8,4,2,32]{4,3,2,1,0:T(2,128)(2,1)S(1)} %copy.179) | copy-start | bytes 24580
  470.6 113.0 %copy-start.332 = (bf16[2,8,4,2,32]{4,3,2,1,0:T(2,128)(2,1)}, bf16[2,8,4,2,32]{4,3,2,1,0:T(2,128)(2,1)S(1)}, u32[]{:S(2)}) copy-start(bf16[2,8,4,2,32]{4,3,2,1,0:T(2,128)(2,1)S(1)} %copy.180) | copy-start | bytes 24580
  489.7 37.7 %copy-start.190 = (bf16[2,27,32,128]{3,2,1,0:T(8,128)(2,1)S(1)}, bf16[2,27,32,128]{3,2,1,0:T(8,128)(2,1)}, u32[]{:S(2)}) copy-start(bf16[2,27,32,128]{3,2,1,0:T(8,128)(2,1)} %param.13) | copy-start | bytes 1327108
  495.3 54.2 %copy-start.352 = (bf16[2,8,4,2,160]{4,1,3,2,0:T(8,128)(2,1)S(1)}, bf16[2,8,4,2,160]{4,1,3,2,0:T(8,128)(2,1)}, u32[]{:S(2)}) copy-start(bf16[2,8,4,2,160]{4,1,3,2,0:T(8,128)(2,1)} %get-tuple-element.250) | copy-start | bytes 122884
  498.5 56.2 %copy-start.351 = (bf16[2,8,4,2,160]{4,1,3,2,0:T(8,128)(2,1)S(1)}, bf16[2,8,4,2,160]{4,1,3,2,0:T(8,128)(2,1)}, u32[]{:S(2)}) copy-start(bf16[2,8,4,2,160]{4,1,3,2,0:T(8,128)(2,1)} %get-tuple-element.252) | copy-start | bytes 122884
  504.9 86.5 %copy-start.325 = (bf16[2,8,4,2,32]{4,3,2,1,0:T(2,128)(2,1)}, bf16[2,8,4,2,32]{4,3,2,1,0:T(2,128)(2,1)S(1)}, u32[]{:S(2)}) copy-start(bf16[2,8,4,2,32]{4,3,2,1,0:T(2,128)(2,1)S(1)} %copy.190) | copy-start | bytes 24580
  505.7 85.5 %copy-start.327 = (bf16[2,8,4,2,32]{4,3,2,1,0:T(2,128)(2,1)}, bf16[2,8,4,2,32]{4,3,2,1,0:T(2,128)(2,1)S(1)}, u32[]{:S(2)}) copy-start(bf16[2,8,4,2,32]{4,3,2,1,0:T(2,128)(2,1)S(1)} %copy.189) | copy-start | bytes 24580
  508.5 60.5 %copy-start.350 = (bf16[2,8,4,2,160]{4,1,3,2,0:T(8,128)(2,1)S(1)}, bf16[2,8,4,2,160]{4,1,3,2,0:T(8,128)(2,1)}, u32[]{:S(2)}) copy-start(bf16[2,8,4,2,160]{4,1,3,2,0:T(8,128)(2,1)} %get-tuple-element.257) | copy-start | bytes 122884
  514.1 57.2 %copy-start.349 = (bf16[2,8,4,2,160]{4,1,3,2,0:T(8,128)(2,1)S(1)}, bf16[2,8,4,2,160]{4,1,3,2,0:T(8,128)(2,1)}, u32[]{:S(2)}) copy-start(bf16[2,8,4,2,160]{4,1,3,2,0:T(8,128)(2,1)} %get-tuple-element.258) | copy-start | bytes 122884
  519.7 52.4 %copy-start.348 = (bf16[2,8,4,2,160]{4,1,3,2,0:T(8,128)(2,1)S(1)}, bf16[2,8,4,2,160]{4,1,3,2,0:T(8,128)(2,1)}, u32[]{:S(2)}) copy-start(bf16[2,8,4,2,160]{4,1,3,2,0:T(8,128)(2,1)} %get-tuple-element.259) | copy-start | bytes 122884
  527.4 44.8 %copy-start.321 = (bf16[2,8,4,2,32]{4,3,2,1,0:T(2,128)(2,1)}, bf16[2,8,4,2,32]{4,3,2,1,0:T(2,128)(2,1)S(1)}, u32[]{:S(2)}) copy-start(bf16[2,8,4,2,32]{4,3,2,1,0:T(2,128)(2,1)S(1)} %copy.166) | copy-start | bytes 24580
  614.8 49.2 %copy-start.366 = (f32[576]{0:T(1024)S(1)}, f32[576]{0:T(1024)}, u32[]{:S(2)}) copy-start(f32[576]{0:T(1024)} %get-tuple-element.364) | copy-start | bytes 6916
  614.8 51.0 %copy-start.197 = (f32[128,576]{0,1:T(8,128)S(1)}, f32[128,576]{0,1:T(8,128)}, u32[]{:S(2)}) copy-start(f32[128,576]{0,1:T(8,128)} %copy.296) | copy-start | bytes 884740
  614.8 51.0 %copy-start.392 = (f32[576]{0:T(1024)S(1)}, f32[576]{0:T(1024)}, u32[]{:S(2)}) copy-start(f32[576]{0:T(1024)} %get-tuple-element.35) | copy-start | bytes 6916
  666.9 73.9 %copy-start.330 = (bf16[2,8,4,2,32]{4,3,2,1,0:T(2,128)(2,1)S(1)}, bf16[2,8,4,2,32]{4,3,2,1,0:T(2,128)(2,1)}, u32[]{:S(2)}) copy-start(bf16[2,8,4,2,32]{4,3,2,1,0:T(2,128)(2,1)} %copy-done.329) | copy-start | bytes 24580
  707.2 45.1 %copy-start.389 = (f32[576]{0:T(1024)}, f32[576]{0:T(1024)S(1)}, u32[]{:S(2)}) copy-start(f32[576]{0:T(1024)S(1)} %get-tuple-element.42) | copy-start | bytes 6916
  707.2 46.8 %copy-start.387 = (f32[576]{0:T(1024)}, f32[576]{0:T(1024)S(1)}, u32[]{:S(2)}) copy-start(f32[576]{0:T(1024)S(1)} %get-tuple-element.43) | copy-start | bytes 6916
  709.0 45.1 %copy-start.273 = (bf16[128,160]{1,0:T(8,128)(2,1)S(1)}, bf16[128,160]{1,0:T(8,128)(2,1)}, u32[]{:S(2)}) copy-start(bf16[128,160]{1,0:T(8,128)(2,1)} %reshape.1557) | copy-start | bytes 122884
  709.0 47.8 %copy-start.270 = (bf16[128,160]{1,0:T(8,128)(2,1)S(1)}, bf16[128,160]{1,0:T(8,128)(2,1)}, u32[]{:S(2)}) copy-start(bf16[128,160]{1,0:T(8,128)(2,1)} %reshape.1559) | copy-start | bytes 122884
  711.6 46.1 %copy-start.268 = (bf16[128,160]{1,0:T(8,128)(2,1)S(1)}, bf16[128,160]{1,0:T(8,128)(2,1)}, u32[]{:S(2)}) copy-start(bf16[128,160]{1,0:T(8,128)(2,1)} %reshape.1560) | copy-start | bytes 122884
  711.6 47.0 %copy-start.266 = (bf16[128,160]{1,0:T(8,128)(2,1)S(1)}, bf16[128,160]{1,0:T(8,128)(2,1)}, u32[]{:S(2)}) copy-start(bf16[128,160]{1,0:T(8,128)(2,1)} %reshape.1561) | copy-start | bytes 122884
  711.7 47.8 %copy-start.264 = (bf16[128,160]{1,0:T(8,128)(2,1)S(1)}, bf16[128,160]{1,0:T(8,128)(2,1)}, u32[]{:S(2)}) copy-start(bf16[128,160]{1,0:T(8,128)(2,1)} %reshape.1562) | copy-start | bytes 122884
  711.7 66.9 %collective-permute-start.9 = (bf16[2,8,1,2,576]{4,1,3,2,0:T(8,128)(2,1)S(1)}, bf16[2,8,1,2,576]{4,1,3,2,0:T(8,128)(2,1)S(1)}, u32[]{:S(2)}, u32[]{:S(2)}) collective-permute-start(bf16[2,8,1,2,576]{4,1,3,2,0:T(8,128)(2,1)S(1)} %get-tuple-element.330), channel_id=1, source_target_pairs={{4,0},{5,1},{6,2},{7,3},{12,8},{13,9},{14,10},{15,11},{20,16},{21,... | collective-permute-start | bytes 110600 | tf_op jit(solution)/shard_map/ppermute | solution.py:20
  713.0 47.4 %copy-start.262 = (bf16[128,160]{1,0:T(8,128)(2,1)S(1)}, bf16[128,160]{1,0:T(8,128)(2,1)}, u32[]{:S(2)}) copy-start(bf16[128,160]{1,0:T(8,128)(2,1)} %reshape.1563) | copy-start | bytes 122884
  713.1 65.5 %collective-permute-start.8 = (bf16[2,8,1,2,576]{4,1,3,2,0:T(8,128)(2,1)S(1)}, bf16[2,8,1,2,576]{4,1,3,2,0:T(8,128)(2,1)S(1)}, u32[]{:S(2)}, u32[]{:S(2)}) collective-permute-start(bf16[2,8,1,2,576]{4,1,3,2,0:T(8,128)(2,1)S(1)} %get-tuple-element.331), channel_id=1, source_target_pairs={{0,4},{1,5},{2,6},{3,7},{8,12},{9,13},{10,14},{11,15},{16,20},{17,... | collective-permute-start | bytes 110600 | tf_op jit(solution)/shard_map/ppermute | solution.py:17
  723.9 37.5 %copy-start.242 = (bf16[128,160]{1,0:T(8,128)(2,1)S(1)}, bf16[128,160]{1,0:T(8,128)(2,1)}, u32[]{:S(2)}) copy-start(bf16[128,160]{1,0:T(8,128)(2,1)} %reshape.1564) | copy-start | bytes 122884
  779.6 12.8 collective-permute-start.10
  783.8 8.6 collective-permute-start.11
  822.6 33.2 %copy-start.296 = (bf16[2,8,4,2,320]{4,1,3,2,0:T(8,128)(2,1)S(1)}, bf16[2,8,4,2,320]{4,1,3,2,0:T(8,128)(2,1)}, u32[]{:S(2)}) copy-start(bf16[2,8,4,2,320]{4,1,3,2,0:T(8,128)(2,1)} %get-tuple-element.196) | copy-start | bytes 245764
  822.6 38.8 %copy-start.295 = (bf16[2,8,4,2,320]{4,1,3,2,0:T(8,128)(2,1)S(1)}, bf16[2,8,4,2,320]{4,1,3,2,0:T(8,128)(2,1)}, u32[]{:S(2)}) copy-start(bf16[2,8,4,2,320]{4,1,3,2,0:T(8,128)(2,1)} %get-tuple-element.198) | copy-start | bytes 245764
  822.6 41.1 %copy-start.294 = (bf16[2,8,4,2,320]{4,1,3,2,0:T(8,128)(2,1)S(1)}, bf16[2,8,4,2,320]{4,1,3,2,0:T(8,128)(2,1)}, u32[]{:S(2)}) copy-start(bf16[2,8,4,2,320]{4,1,3,2,0:T(8,128)(2,1)} %get-tuple-element.199) | copy-start | bytes 245764
  822.6 41.9 %copy-start.293 = (bf16[2,8,4,2,320]{4,1,3,2,0:T(8,128)(2,1)S(1)}, bf16[2,8,4,2,320]{4,1,3,2,0:T(8,128)(2,1)}, u32[]{:S(2)}) copy-start(bf16[2,8,4,2,320]{4,1,3,2,0:T(8,128)(2,1)} %get-tuple-element.200) | copy-start | bytes 245764
  826.0 39.3 %copy-start.292 = (bf16[2,8,4,2,320]{4,1,3,2,0:T(8,128)(2,1)S(1)}, bf16[2,8,4,2,320]{4,1,3,2,0:T(8,128)(2,1)}, u32[]{:S(2)}) copy-start(bf16[2,8,4,2,320]{4,1,3,2,0:T(8,128)(2,1)} %get-tuple-element.201) | copy-start | bytes 245764
  834.4 31.1 %copy-start.291 = (bf16[2,8,4,2,320]{4,1,3,2,0:T(8,128)(2,1)S(1)}, bf16[2,8,4,2,320]{4,1,3,2,0:T(8,128)(2,1)}, u32[]{:S(2)}) copy-start(bf16[2,8,4,2,320]{4,1,3,2,0:T(8,128)(2,1)} %get-tuple-element.202) | copy-start | bytes 245764
  869.4 31.9 %copy-start.317 = (bf16[128,320]{1,0:T(8,128)(2,1)S(1)}, bf16[128,320]{1,0:T(8,128)(2,1)}, u32[]{:S(2)}) copy-start(bf16[128,320]{1,0:T(8,128)(2,1)} %reshape.1617) | copy-start | bytes 245764
  913.0 53.0 %copy-start.396 = (f32[448]{0:T(512)S(1)}, f32[448]{0:T(512)}, u32[]{:S(2)}) copy-start(f32[448]{0:T(512)} %get-tuple-element.68) | copy-start | bytes 5380
  919.7 48.9 %copy-start.359 = (bf16[2,8,4,2,128]{4,3,2,1,0:T(2,128)(2,1)S(1)}, bf16[2,8,4,2,128]{4,3,2,1,0:T(2,128)(2,1)}, u32[]{:S(2)}) copy-start(bf16[2,8,4,2,128]{4,3,2,1,0:T(2,128)(2,1)} %copy.279) | copy-start | bytes 98308
  919.7 48.9 %copy-start.364 = (f32[128]{0:T(128)S(1)}, f32[128]{0:T(128)}, u32[]{:S(2)}) copy-start(f32[128]{0:T(128)} %reshape.1743) | copy-start | bytes 1540
  924.7 43.9 %copy-start.222 = (f32[128,448]{0,1:T(8,128)}, f32[128,448]{0,1:T(8,128)S(1)}, u32[]{:S(2)}) copy-start(f32[128,448]{0,1:T(8,128)S(1)} %get-tuple-element.70) | copy-start | bytes 688132
  1070.3 39.9 %collective-permute-start.13 = (bf16[2,16,1,4,576]{4,3,2,1,0:T(4,128)(2,1)}, bf16[2,16,1,4,576]{4,3,2,1,0:T(4,128)(2,1)}, u32[]{:S(2)}, u32[]{:S(2)}) collective-permute-start(bf16[2,16,1,4,576]{4,3,2,1,0:T(4,128)(2,1)} %get-tuple-element.190), channel_id=1, source_target_pairs={{4,0},{5,1},{6,2},{7,3},{12,8},{13,9},{14,10},{15,11},{20,16},{21,... | collective-permute-start | bytes 442376 | tf_op jit(solution)/shard_map/ppermute | solution.py:20
  1071.7 36.1 %collective-permute-start.12 = (bf16[2,16,1,4,576]{4,3,2,1,0:T(4,128)(2,1)}, bf16[2,16,1,4,576]{4,3,2,1,0:T(4,128)(2,1)}, u32[]{:S(2)}, u32[]{:S(2)}) collective-permute-start(bf16[2,16,1,4,576]{4,3,2,1,0:T(4,128)(2,1)} %get-tuple-element.191), channel_id=1, source_target_pairs={{0,4},{1,5},{2,6},{3,7},{8,12},{9,13},{10,14},{11,15},{16,20},{17,... | collective-permute-start | bytes 442376 | tf_op jit(solution)/shard_map/ppermute | solution.py:17
  1114.0 16.7 %collective-permute-start.14 = (bf16[2,16,10,1,576]{4,1,3,2,0:T(8,128)(2,1)}, bf16[2,16,10,1,576]{4,1,3,2,0:T(8,128)(2,1)}, u32[]{:S(2)}, u32[]{:S(2)}) collective-permute-start(bf16[2,16,10,1,576]{4,1,3,2,0:T(8,128)(2,1)} %copy.284), channel_id=1, source_target_pairs={{0,1},{1,2},{2,3},{4,5},{5,6},{6,7},{8,9},{9,10},{10,11},{12,13},{... | collective-permute-start | bytes 1105928 | tf_op jit(solution)/shard_map/ppermute | solution.py:17
  1118.9 18.2 %collective-permute-start.15 = (bf16[2,16,10,1,576]{4,1,3,2,0:T(8,128)(2,1)S(1)}, bf16[2,16,10,1,576]{4,1,3,2,0:T(8,128)(2,1)}, u32[]{:S(2)}, u32[]{:S(2)}) collective-permute-start(bf16[2,16,10,1,576]{4,1,3,2,0:T(8,128)(2,1)S(1)} %copy.285), channel_id=1, source_target_pairs={{1,0},{2,1},{3,2},{5,4},{6,5},{7,6},{9,8},{10,9},{11,10},{13,12},{... | collective-permute-start | bytes 1105928 | tf_op jit(solution)/shard_map/ppermute | solution.py:20
  1293.0 41.4 %copy-start.395 = (f32[448]{0:T(512)S(1)}, f32[448]{0:T(512)}, u32[]{:S(2)}) copy-start(f32[448]{0:T(512)} %get-tuple-element.62) | copy-start | bytes 5380
  (363 other events, 2921.7 us)
Sparse Core Ops, SparseCore 0:
  1341.1 301.7 all-reduce.14
where the time goes:
time: 1690 us; the launch traced here: 1670 us
  local copies, waits for them, and re-layouts  432 us (26%)
  matrix products  407 us (24%)
  blocking collectives  323 us (19%)
  waiting for transfers between devices  311 us (18%)
  other arithmetic  131 us (8%)
  starting transfers between devices  42.7 us (3%)
  between operations  20.3 us (1%)
    psum x1, waiting for transfers between devices, on_device(): lax.psum((first_kernels[0], first_kernels[1], first_kernels[2], first_ker...  290 us
    psum x4, blocking collectives, slope_totals(): return lax.psum((partial_value[0], partial_value[1]), ('batch', 'ha', 'wa'))  161 us
    psum x4, blocking collectives, norm_sums(): lax.psum((partial_value[0], partial_value[1], partial_value[2]), ('batch'...  161 us
    reshape x108, local copies, waits for them, and re-layouts, window_slice(): return window.reshape(-1, padded.shape[-1])  159 us
    slice x138, local copies, waits for them, and re-layouts, window_slice(): padded[:, off_time:off_time + slot_len, off_row:off_row + tile_rows, off_...  142 us
    dot_general x104, matrix products, conv_forward(): jnp.dot(window_slice(padded, offset, extent), kernel[offset], preferred_e...  136 us
    dot_general x108, matrix products, conv_kernel_grad(): jnp.einsum('vi,vo->io', window_slice(padded, offset, extent), grad_low, p...  124 us
    dot_general x104, matrix products, conv_input_grad(): jnp.einsum('vo,io->vi', window_slice(padded, 26 - offset, extent), kernel...  116 us
  transfers between devices with their start and end apart: 17, of which 6 were waited for; matrix products, arithmetic and copies ran while one was open for 10% of the time, Pallas kernels for 0%

commit v1 on v0

v1 whole, which is shorter than its diff:
```python
import functools
from types import SimpleNamespace

import jax
import jax.numpy as jnp
from jax import lax
from jax.experimental import pallas as pl
from jax.experimental.pallas import tpu as pltpu
from jax.sharding import PartitionSpec as P

HEIGHT = 14
EPSILON = 1e-05
MESH = pl.DeviceIdType.MESH
F32 = jnp.float32
BF16 = jnp.bfloat16

B0, B1R, B2R, B1, B2, BP = 256, 160, 32, 320, 128, 128
NARROW = B1R + B2R
REDUCE = B0 + NARROW
SECOND = (B1, B2, BP)
SECOND_AT = (0, 384, 512)
SECOND_WIDTH = 640
SUM_WIDTH = 1280
AXES = ("batch", "ha", "wa")

TAP_BLOCKS = 88
LOW_AT = 800
LOW_OUT = 1024
GRAD_BLOCKS = 1056
BUNDLES = ((0, 352), (352, 448), (800, 256))
OWNERS = 4

SCHEDULE = {
    (1, 1): ((1, 0), (1, 1)),
    (1, 5): ((1, 0), (1, 1)),
    (1, 6): (),
    (0, 7): ((1, 0), (1, 1), (1, 2)),
    (0, 0): ((1, 0), (1, 1), (1, 2)),
    (0, 1): ((0, 0), (0, 1), (1, 0), (1, 1), (1, 2)),
    (0, 2): ((1, 0), (1, 1), (1, 2)),
    (0, 3): ((0, 0), (0, 1), (1, 0), (1, 1), (1, 2)),
    (0, 4): ((1, 0), (1, 1), (1, 2)),
    (0, 5): ((0, 0), (0, 1), (1, 0), (1, 1), (1, 2)),
    (0, 6): ((0, 0), (0, 1)),
}
LAST_STEPS = ((0, 2), (0, 0), (0, 1)) * 9

NN = (((1,), (0,)), ((), ()))
NT = (((1,), (1,)), ((), ()))


def dot(a, b, dims=NN):
    return lax.dot_general(a, b, dims, preferred_element_type=F32)


def softplus(x):
    return jnp.maximum(x, 0.0) + jnp.log1p(jnp.exp(-jnp.abs(x)))


def sigmoid(x):
    return 1.0 / (1.0 + jnp.exp(-x))


class Layer:
    def __init__(self, index, rows, cols, clips, slot):
        self.index, self.rows, self.cols = index, rows, cols
        self.clips, self.slot = clips, slot
        self.frames = clips * slot
        self.cells = rows * cols * self.frames
        self.row_cells = cols * self.frames

    def scratch(self, channels):
        r, c, t, n = self.rows, self.cols, self.frames, self.cells
        pad = (r + 2, c + 2, t)
        return dict(
            mask=pltpu.VMEM(pad + (1,), F32),
            block_in=pltpu.VMEM((r, c, t, channels), BF16),
            first=pltpu.VMEM((r, c, t, B0), F32),
            narrow=pltpu.VMEM(pad + (NARROW,), F32),
            border=pltpu.VMEM(pad + (BP + NARROW,), BF16),
            mid_in=pltpu.VMEM(pad + (3 * B1R,), BF16),
            small_in=pltpu.VMEM(pad + (3 * B2R,), BF16),
            box=pltpu.VMEM((r + 2, c, t, BP), F32),
            mid=pltpu.VMEM((n, 3 * B1R), F32),
            small=pltpu.VMEM((n, B2), F32),
            pool=pltpu.VMEM((n, BP), F32),
            normed=pltpu.VMEM(pad + (SECOND_WIDTH,), BF16),
            projected_slope=pltpu.VMEM((n, BP), BF16),
            low=pltpu.VMEM((n, REDUCE), BF16),
        )


def batch_norm_scale(total, square, count, gain):
    average = total / count
    variance = square / count - average * average
    inv_std = lax.rsqrt(variance + EPSILON)
    return average, inv_std, inv_std * gain


def kernel_body(names, sizes, refs):
    k = SimpleNamespace(**dict(zip(names, refs)))
    n_batch, n_wa, layers = sizes
    b, h, w = (lax.axis_index(a) for a in AXES)
    chips = n_batch * n_wa
    my_chip = b * n_wa + w
    one, two = layers

    def chip_at(p):
        return lax.div(p, n_wa), h, lax.rem(p, n_wa)

    def rotated(i):
        return lax.rem(my_chip + i, chips)

    loads = []
    for at, (source, target) in enumerate(
        (
            (k.features, one.s.block_in),
            (k.w_reduce, k.v_w_reduce),
            (k.w_pool, k.v_w_pool),
            (k.w_mid, k.v_w_mid),
            (k.w_small, k.v_w_small),
            (k.out_grad, k.v_out_grad),
        )
    ):
        copy = pltpu.make_async_copy(source, target, k.load_sem.at[at])
        copy.start()
        loads.append(copy)

    for lay in layers:
        s = lay.s
        for ref in (s.border, s.normed):
            for row in (0, lay.rows + 1):
                ref[row] = jnp.zeros(ref.shape[1:], ref.dtype)
            for col in (0, lay.cols + 1):
                ref[:, col] = jnp.zeros((ref.shape[0],) + ref.shape[2:], ref.dtype)
    ref = k.grad_border
    ref[...] = jnp.zeros(ref.shape, ref.dtype)
    for layer in range(2):
        for begin, end in ((9 * TAP_BLOCKS, LOW_AT), (LOW_AT + 252, GRAD_BLOCKS)):
            k.grads[layer, begin:end] = jnp.zeros((end - begin, 16, 128), BF16)
    k.sums[...] = jnp.zeros(k.sums.shape, F32)

    barrier = pltpu.get_barrier_semaphore()
    pl.semaphore_signal(barrier, inc=1, device_id=(b, 1 - h, w), device_id_type=MESH)

    @pl.when(w > 0)
    def _():
        pl.semaphore_signal(barrier, inc=1, device_id=(b, 1 - h, w - 1), device_id_type=MESH)

    @pl.when(w < n_wa - 1)
    def _():
        pl.semaphore_signal(barrier, inc=1, device_id=(b, 1 - h, w + 1), device_id_type=MESH)

    def greet(i, carry):
        pl.semaphore_signal(barrier, inc=1, device_id=chip_at(rotated(i)), device_id_type=MESH)
        return carry

    lax.fori_loop(1, chips, greet, 0)

    for lay in layers:
        frame_at = lax.broadcasted_iota(jnp.int32, (lay.frames, 1), 0)
        inside = jnp.zeros((lay.frames, 1), F32)
        for clip in range(lay.clips):
            valid = k.frame_counts[clip]
            valid = valid if lay.index == 0 else lax.div(valid, 2)
            begin = clip * lay.slot
            inside = jnp.where((frame_at >= begin) & (frame_at < begin + valid), 1.0, inside)
        height = HEIGHT if lay.index == 0 else HEIGHT // 2
        for row in range(lay.rows + 2):
            at_row = h * lay.rows + row - 1
            for col in range(lay.cols + 2):
                at_col = w * lay.cols + col - 1
                good = (at_row >= 0) & (at_row < height) & (at_col >= 0) & (at_col < height)
                lay.s.mask[row, col] = inside * good.astype(F32)

    def start_sum(at):
        pair = pltpu.make_async_remote_copy(
            src_ref=k.sums.at[at],
            dst_ref=k.pair_sums.at[at],
            send_sem=k.pair_sem.at[0, at],
            recv_sem=k.pair_sem.at[1, at],
            device_id=(b, 1 - h, w),
            device_id_type=MESH,
        )
        pair.start()
        pair.wait()
        k.chip_sums[at % 2, my_chip] = k.sums[at] + k.pair_sums[at]

        def send(i, carry):
            pltpu.make_async_remote_copy(
                src_ref=k.chip_sums.at[at % 2, my_chip],
                dst_ref=k.chip_sums.at[at % 2, my_chip],
                send_sem=k.chip_sem.at[0, at],
                recv_sem=k.chip_sem.at[1, at],
                device_id=chip_at(rotated(i)),
                device_id_type=MESH,
            ).start()
            return carry

        if chips <= 16:
            for i in range(1, chips):
                send(i, 0)
        else:
            lax.fori_loop(1, chips, send, 0)

    def end_sum(at):
        for way in (1, 0):
            others = k.chip_sums.at[at % 2, pl.ds(0, chips - 1)]
            pltpu.make_async_copy(others, others, k.chip_sem.at[way, at]).wait()
        total = k.chip_sums[at % 2, 0]
        for p in range(1, chips):
            total = total + k.chip_sums[at % 2, p]
        return total

    def halo_copies(lay, ref, at):
        src_row = jnp.where(h == 0, lay.rows, 1)
        dst_row = jnp.where(h == 0, 0, lay.rows + 1)
        rows, cols = lay.rows, lay.cols

        def remote(src, dst, way, device):
            return pltpu.make_async_remote_copy(
                src_ref=ref.at[src],
                dst_ref=ref.at[dst],
                send_sem=k.halo_sem.at[0, at, way],
                recv_sem=k.halo_sem.at[1, at, way],
                device_id=device,
                device_id_type=MESH,
            )

        all_rows, all_cols = pl.ds(1, rows), pl.ds(1, cols)
        row = remote((src_row, all_cols), (dst_row, all_cols), 0, (b, 1 - h, w))
        to_left = [
            remote((all_rows, 1), (all_rows, cols + 1), 1, (b, h, w - 1)),
            remote((src_row, 1), (dst_row, cols + 1), 2, (b, 1 - h, w - 1)),
        ]
        to_right = [
            remote((all_rows, cols), (all_rows, 0), 3, (b, h, w + 1)),
            remote((src_row, cols), (dst_row, 0), 4, (b, 1 - h, w + 1)),
        ]
        return row, to_left, to_right

    def start_halo(lay, ref, at):
        row, to_left, to_right = halo_copies(lay, ref, at)
        row.start()

        @pl.when(w > 0)
        def _():
            for copy in to_left:
                copy.start()

        @pl.when(w < n_wa - 1)
        def _():
            for copy in to_right:
                copy.start()

    def end_halo(lay, ref, at):
        row, to_left, to_right = halo_copies(lay, ref, at)
        row.wait()

        @pl.when(w > 0)
        def _():
            for copy in to_left:
                copy.wait_send()
            for copy in to_right:
                copy.wait_recv()

        @pl.when(w < n_wa - 1)
        def _():
            for copy in to_right:
                copy.wait_send()
            for copy in to_left:
                copy.wait_recv()

    def exchange(layer, number):
        begin, count = BUNDLES[number]
        half, quarter, eighth = count // 2, count // 4, count // 8
        piece, chunk = count // 16, count // 32
        stride = n_batch // OWNERS
        g = k.grads.at[layer]
        x, y = lax.rem(w, 2), lax.div(w, 2)
        pair, beside, below = (b, 1 - h, w), (b, h, w + 1 - 2 * x), (b, h, w + 2 - 4 * y)

        def copy(source, at, target, to, size, slot, device):
            return pltpu.make_async_remote_copy(
                src_ref=source.at[pl.ds(at, size)],
                dst_ref=target.at[pl.ds(to, size)],
                send_sem=k.grad_sem.at[0, layer, number, slot],
                recv_sem=k.grad_sem.at[1, layer, number, slot],
                device_id=device,
                device_id_type=MESH,
            )

        def go(copies):
            for c in copies:
                c.start()

        def end(copies):
            for c in copies:
                c.wait()

        def add(at, other, to, size):
            step = 16 if size % 16 == 0 else size

            def body(i, carry):
                mine = pl.ds(at + i * step, step)
                g[mine] = g[mine] + other[pl.ds(to + i * step, step)]
                return carry

            lax.fori_loop(0, size // step, body, 0)

        def free(slot, device):
            sem = k.free_sem.at[layer, number, slot]
            pl.semaphore_signal(sem, inc=1, device_id=device, device_id_type=MESH)

        def wait_free(slot):
            pl.semaphore_wait(k.free_sem.at[layer, number, slot], 1)

        r1, r2, r3, r4 = (r.at[layer] for r in (k.got_half, k.got_eighth, k.got_piece, k.got_chunk))
        mine = begin + h * half
        copies = [copy(g, begin + (1 - h) * half, r1, begin // 2, half, 0, pair)]
        go(copies)
        yield
        end(copies)
        free(0, pair)
        add(mine, r1, begin // 2, half)
        at_a, at_b = mine, mine + quarter
        to = begin // 4
        copies = [
            copy(g, at_a + (1 - x) * eighth, r2, to, eighth, 1, beside),
            copy(g, at_b + (1 - y) * eighth, r2, to + eighth, eighth, 2, below),
        ]
        go(copies)
        yield
        end(copies)
        at_a, at_b = at_a + x * eighth, at_b + y * eighth
        add(at_a, r2, to, eighth)
        add(at_b, r2, to + eighth, eighth)
        to = begin // 8
        copies = [
            copy(g, at_a + (1 - y) * piece, r3, to, piece, 3, below),
            copy(g, at_b + (1 - x) * piece, r3, to + piece, piece, 4, beside),
        ]
        go(copies)
        yield
        end(copies)
        free(1, below)
        free(2, beside)
        at_a, at_b = at_a + y * piece, at_b + x * piece
        add(at_a, r3, to, piece)
        add(at_b, r3, to + piece, piece)

        def chunk_at(owner):
            return (at_a, at_b)[owner // 2] + owner % 2 * chunk

        to = begin // 32
        r5 = k.got_total.at[layer]
        for owner in range(OWNERS):

            @pl.when(b != owner * stride)
            def _(owner=owner):
                pltpu.make_async_remote_copy(
                    src_ref=g.at[pl.ds(chunk_at(owner), chunk)],
                    dst_ref=r4.at[b, pl.ds(to, chunk)],
                    send_sem=k.grad_sem.at[0, layer, number, 5 + owner],
                    recv_sem=k.grad_sem.at[1, layer, number, 5],
                    device_id=(owner * stride, h, w),
                    device_id_type=MESH,
                ).start()

        yield

        def for_owner(do):
            if stride == 1:
                do()
            else:
                pl.when(lax.rem(b, stride) == 0)(do)

        rank = lax.div(b, stride)
        my_chunk = jnp.where(rank < 2, at_a, at_b) + lax.rem(rank, 2) * chunk

        def collect():
            others = r4.at[pl.ds(0, n_batch - 1), pl.ds(to, chunk)]
            pltpu.make_async_copy(others, others, k.grad_sem.at[1, layer, number, 5]).wait()
            r4[b, pl.ds(to, chunk)] = g[pl.ds(my_chunk, chunk)]
            total = r4[0, pl.ds(to, chunk)].astype(F32)
            for slot in range(1, n_batch):
                total = total + r4[slot, pl.ds(to, chunk)].astype(F32)
            g[pl.ds(my_chunk, chunk)] = total.astype(BF16)

        for_owner(collect)
        for owner in range(OWNERS):

            @pl.when(b != owner * stride)
            def _(owner=owner):
                part = g.at[pl.ds(chunk_at(owner), chunk)]
                pltpu.make_async_copy(part, part, k.grad_sem.at[0, layer, number, 5 + owner]).wait()

        def share_copy(i):
            return pltpu.make_async_remote_copy(
                src_ref=g.at[pl.ds(my_chunk, chunk)],
                dst_ref=r5.at[rank, pl.ds(to, chunk)],
                send_sem=k.grad_sem.at[0, layer, number, 9],
                recv_sem=k.grad_sem.at[1, layer, number, 9 + rank],
                device_id=(lax.rem(b + i, n_batch), h, w),
                device_id_type=MESH,
            )

        def share():
            def body(i, carry):
                share_copy(i).start()
                return carry

            lax.fori_loop(1, n_batch, body, 0)

        for_owner(share)
        yield

        def shared():
            def body(i, carry):
                share_copy(i).wait_send()
                return carry

            lax.fori_loop(1, n_batch, body, 0)

        for_owner(shared)
        for owner in range(OWNERS):

            @pl.when(b != owner * stride)
            def _(owner=owner):
                part = r5.at[owner, pl.ds(to, chunk)]
                pltpu.make_async_copy(part, part, k.grad_sem.at[1, layer, number, 9 + owner]).wait()
                g[pl.ds(chunk_at(owner), chunk)] = r5[owner, pl.ds(to, chunk)]

        copies = [
            copy(g, at_a, g, at_a, piece, 13, below),
            copy(g, at_b, g, at_b, piece, 14, beside),
        ]
        wait_free(1)
        wait_free(2)
        go(copies)
        yield
        end(copies)
        at_a, at_b = mine + x * eighth, mine + quarter + y * eighth
        copies = [
            copy(g, at_a, g, at_a, eighth, 15, beside),
            copy(g, at_b, g, at_b, eighth, 16, below),
        ]
        go(copies)
        yield
        end(copies)
        copies = [copy(g, mine, g, mine, half, 17, pair)]
        wait_free(0)
        go(copies)
        yield
        end(copies)
        target = k.weight_grads.at[layer, pl.ds(LOW_OUT if begin == LOW_AT else begin, count)]
        out = pltpu.make_async_copy(g.at[pl.ds(begin, count)], target, k.out_sem.at[layer, number])
        out.start()
        yield
        out.wait()

    exchanges = {}

    def start_exchange(layer, number):
        exchanges[layer, number] = exchange(layer, number)
        next(exchanges[layer, number])

    def progress(layer, at):
        for key in SCHEDULE.get((layer, at), ()):
            next(exchanges[key], None)

    def flat_block(lay):
        block = lay.s.block_in[...]
        return block.reshape(lay.cells, block.shape[-1])

    def store_blocks(layer, at, value):
        rows, lanes = value.shape
        for lane in range(0, lanes, 128):
            size = min(128, lanes - lane)
            blocks = pl.ds(at + lane // 128 * (rows // 16), rows // 16)
            tile = value[:, lane : lane + size].reshape(rows // 16, 16, size)
            k.grads[layer, blocks, :, 0:size] = tile

    def column_sum(value):
        return jnp.sum(value, axis=0, keepdims=True)

    def center_mask(lay, row, count=1):
        mask = lay.s.mask[pl.ds(row + 1, count), 1 : lay.cols + 1]
        return mask.reshape(count * lay.row_cells, 1)

    def shifted(lay, value):
        count = value.shape[0]
        frame_at = lax.rem(lax.broadcasted_iota(jnp.int32, (count, 1), 0), lay.slot)
        before = jnp.where(frame_at == 0, 0.0, pltpu.roll(value, 1, 0))
        after = jnp.where(frame_at == lay.slot - 1, 0.0, pltpu.roll(value, count - 1, 0))
        return before, after

    def reduce_conv(lay):
        s, at = lay.s, lay.index
        step = 2
        count = step * lay.row_cells

        def body(i, sums):
            mask = center_mask(lay, i * step, step)
            block = s.block_in[pl.ds(i * step, step)]
            block = block.reshape(count, block.shape[-1])
            if lay.index == 0:
                block = (block.astype(F32) * mask).astype(BF16)
                shape = (step, lay.cols, lay.frames, block.shape[-1])
                s.block_in[pl.ds(i * step, step)] = block.reshape(shape)
            reduced = dot(block, k.v_w_reduce[at], NT)
            projected = dot(block, k.v_w_pool[at])
            rows = pl.ds(i * step, step)
            inner = pl.ds(i * step + 1, step)
            shape = (step, lay.cols, lay.frames)
            s.first[rows] = reduced[:, :B0].reshape(shape + (B0,))
            thin = reduced[:, B0:].reshape(shape + (NARROW,))
            s.narrow[inner, 1 : lay.cols + 1] = thin
            s.border[inner, 1 : lay.cols + 1, :, 0:BP] = projected.reshape(shape + (BP,)).astype(BF16)
            s.border[inner, 1 : lay.cols + 1, :, BP:] = thin.astype(BF16)
            total, square, valid = sums
            return (
                total + column_sum(reduced),
                square + column_sum(reduced * reduced),
                valid + column_sum(mask),
            )

        zero = jnp.zeros((1, REDUCE), F32)
        return lax.fori_loop(0, lay.rows // step, body, (zero, zero, jnp.zeros((1, 1), F32)))

    def narrow_windows(lay, norm):
        s = lay.s
        average, scale, bias = norm
        rows, cols, t = lay.rows, lay.cols, lay.frames
        for row in (0, rows + 1):
            s.narrow[row] = s.border[row, :, :, BP:].astype(F32)
        for col in (0, cols + 1):
            s.narrow[1 : rows + 1, col] = s.border[1 : rows + 1, col, :, BP:].astype(F32)

        def body(row, carry):
            count = (cols + 2) * t
            z = s.narrow[row].reshape(count, NARROW)
            mask = s.mask[row].reshape(count, 1)
            value = jnp.where(mask > 0.0, softplus((z - average) * scale + bias), 0.0)
            before, after = shifted(lay, value)
            parts = (before, value, after)
            mid = jnp.concatenate([p[:, :B1R] for p in parts], axis=1)
            small = jnp.concatenate([p[:, B1R:] for p in parts], axis=1)
            s.mid_in[row] = mid.astype(BF16).reshape(cols + 2, t, 3 * B1R)
            s.small_in[row] = small.astype(BF16).reshape(cols + 2, t, 3 * B2R)
            s.box[row] = box_row(lay, s.border[row, :, :, 0:BP].astype(F32))
            return carry

        lax.fori_loop(0, rows + 2, body, 0)

    def box_row(lay, value):
        cols, t = lay.cols, lay.frames
        flat = value.reshape((cols + 2) * t, BP)
        before, after = shifted(lay, flat)
        flat = (flat + before + after).reshape(cols + 2, t, BP)
        return flat[0:cols] + flat[1 : cols + 1] + flat[2 : cols + 2]

    def box_rows(lay, row):
        box = lay.s.box
        total = box[row] + box[row + 1] + box[row + 2]
        return total.reshape(lay.row_cells, BP) * (1.0 / 27.0)

    def window(lay, ref, row, col, width):
        value = ref[pl.ds(row, lay.rows), pl.ds(col, lay.cols)]
        return value.reshape(lay.cells, width)

    def cube_conv(lay):
        s, at = lay.s, lay.index
        s.mid[:, 0:B1] = jnp.zeros((lay.cells, B1), F32)
        s.small[...] = jnp.zeros(s.small.shape, F32)

        def body(tap, carry):
            row, col = lax.div(tap, 3), lax.rem(tap, 3)
            s.mid[:, 0:B1] += dot(window(lay, s.mid_in, row, col, 3 * B1R), mid_kernel(at, tap))
            s.small[...] += dot(window(lay, s.small_in, row, col, 3 * B2R), small_kernel(at, tap))
            return carry

        lax.fori_loop(0, 9, body, 0)

    def mid_kernel(at, tap):
        return jnp.concatenate([k.v_w_mid[at, 9 * t + tap] for t in range(3)], axis=0)

    def small_kernel(at, tap):
        return jnp.concatenate([k.v_w_small[at, 9 * t + tap] for t in range(3)], axis=0)

    def second_rows(lay, row, count=1):
        cells = pl.ds(pl.multiple_of(row * lay.row_cells, lay.row_cells), count * lay.row_cells)
        return [
            ref[cells, 0:n] for ref, n in zip((lay.s.mid, lay.s.small, lay.s.pool), SECOND)
        ]

    def second_sums(lay):
        def body(row, sums):
            cells = pl.ds(pl.multiple_of(row * lay.row_cells, lay.row_cells), lay.row_cells)
            lay.s.pool[cells, :] = box_rows(lay, row)
            mask = center_mask(lay, row)
            out = []
            for (total, square), value in zip(sums, second_rows(lay, row)):
                inside = value * mask
                out.append((total + column_sum(inside), square + column_sum(inside * value)))
            return tuple(out)

        zero = tuple((jnp.zeros((1, n), F32),) * 2 for n in SECOND)
        return lax.fori_loop(0, lay.rows, body, zero)

    def put_second(at, sums):
        for which in range(2):
            for begin, part, width in zip(SECOND_AT, sums, SECOND):
                begin += which * SECOND_WIDTH
                k.sums[at, :, begin : begin + width] = part[which]

    def get_second(total, which):
        return [total[:, which * SECOND_WIDTH + a : which * SECOND_WIDTH + a + n] for a, n in zip(SECOND_AT, SECOND)]

    def put_first(at, sums):
        for which in range(2):
            k.sums[at, :, which * 512 : which * 512 + REDUCE] = sums[which]

    def get_first(total, which):
        return total[:, which * 512 : which * 512 + REDUCE]

    def second_params(k_of, at):
        row = k_of[at]
        out, begin = [], REDUCE
        for width in SECOND:
            out.append(row[:, begin : begin + width])
            begin += width
        return out

    def first_params(k_of, at):
        return k_of[at][:, :REDUCE]

    def forward(lay, at, count):
        s = lay.s
        total, square, valid = reduce_conv(lay)
        start_halo(lay, s.border, 2 * lay.index)
        put_first(at, (total, square))
        if count is None:
            k.sums[at, :, 1024:1152] = jnp.broadcast_to(valid, (1, 128))
        start_sum(at)
        end_halo(lay, s.border, 2 * lay.index)
        summed = end_sum(at)
        if count is None:
            count = summed[:, 1024:1025]
        average, inv_std, scale = batch_norm_scale(
            get_first(summed, 0), get_first(summed, 1), count, first_params(k.gain, lay.index)
        )
        first = (average, inv_std, scale, first_params(k.bias, lay.index))
        narrow_windows(lay, (average[:, B0:], scale[:, B0:], first[3][:, B0:]))
        cube_conv(lay)
        put_second(at + 1, second_sums(lay))
        start_sum(at + 1)
        summed = end_sum(at + 1)
        second = []
        for total, square, gain, bias in zip(
            get_second(summed, 0),
            get_second(summed, 1),
            second_params(k.gain, lay.index),
            second_params(k.bias, lay.index),
        ):
            second.append(batch_norm_scale(total, square, count, gain) + (bias,))
        return first, second, count

    def normalised(value, norm):
        average, inv_std, scale, bias = norm
        return (value - average) * inv_std

    def affine(value, norm):
        average, inv_std, scale, bias = norm
        return (value - average) * scale + bias

    def left_half(norm):
        return tuple(p[:, :B0] for p in norm)

    def outputs(lay, row, first, second):
        mask = center_mask(lay, row)
        z = lay.s.first[row].reshape(lay.row_cells, B0)
        parts = [softplus(affine(z, left_half(first))) * mask]
        values = second_rows(lay, row)
        parts += [softplus(affine(v, n)) * mask for v, n in zip(values, second)]
        for begin, width, v, n in zip(SECOND_AT, SECOND, values, second):
            normed = normalised(v, n).astype(BF16).reshape(lay.cols, lay.frames, width)
            lay.s.normed[row + 1, 1 : lay.cols + 1, :, begin : begin + width] = normed
        return parts

    for copy in loads[:3]:
        copy.wait()
    beside = (w > 0).astype(jnp.int32) + (w < n_wa - 1).astype(jnp.int32)
    pl.semaphore_wait(barrier, chips + beside)

    for copy in loads[3:]:
        copy.wait()
    first_one, second_one, count_one = forward(one, 0, None)

    def halve(row, carry):
        low = outputs(one, 2 * row, first_one, second_one)
        high = outputs(one, 2 * row + 1, first_one, second_one)
        begin = 0
        for p, q in zip(low, high):
            width = p.shape[-1]
            both = (p + q).reshape(two.cols, 2, one.frames, width)
            both = both[:, 0] + both[:, 1]
            for lane in range(0, width, 128):
                size = min(128, width - lane)
                k.pairs[:, begin + lane // 128, :, 0:size] = both[:, :, lane : lane + size]
            begin += -(-width // 128)
        for col in range(two.cols):
            tiles = []
            for lane in range(begin):
                even = k.pairs[col, lane, pl.ds(0, two.frames, stride=2), :]
                odd = k.pairs[col, lane, pl.ds(1, two.frames, stride=2), :]
                tiles.append((even + odd) * 0.125)
            half = (B0 + B1) // 128
            tiles[half] = tiles[half][:, : (B0 + B1) % 128]
            mean = jnp.concatenate(tiles, axis=1)
            two.s.block_in[row, col] = mean.astype(BF16)
        return carry

    lax.fori_loop(0, two.rows, halve, 0)
    start_halo(one, one.s.normed, 1)

    first_two, second_two, count_two = forward(two, 2, count_one * 0.125)

    def finish(row, carry):
        parts = outputs(two, row, first_two, second_two)
        value = jnp.concatenate(parts, axis=1).astype(BF16)
        k.block_output[row] = value.reshape(two.cols, two.frames, value.shape[-1])
        return carry

    lax.fori_loop(0, two.rows, finish, 0)
    start_halo(two, two.s.normed, 3)

    def backward(lay, out_slope, border_slope, at, first, second, count, before_end):
        s, index = lay.s, lay.index

        def second_slope(row):
            mask = center_mask(lay, row)
            slopes = out_slope(row)[1:]
            values = second_rows(lay, row)
            normed = [normalised(v, n) for v, n in zip(values, second)]
            slopes = [
                g * mask * sigmoid(m * (n[2] / n[1]) + n[3])
                for g, m, n in zip(slopes, normed, second)
            ]
            return mask, normed, slopes

        def sum_body(row, sums):
            mask, normed, slopes = second_slope(row)
            return tuple(
                (t + column_sum(g), q + column_sum(g * m))
                for (t, q), g, m in zip(sums, slopes, normed)
            )

        zero = tuple((jnp.zeros((1, n), F32),) * 2 for n in SECOND)
        put_second(at, lax.fori_loop(0, lay.rows, sum_body, zero))
        start_sum(at)
        before_end()
        progress(index, 7)
        summed = end_sum(at)
        totals = list(zip(get_second(summed, 0), get_second(summed, 1)))
        begin = REDUCE
        for (bias_grad, gain_grad), width in zip(totals, SECOND):
            k.bias_grad[index, :, begin : begin + width] = bias_grad
            k.gain_grad[index, :, begin : begin + width] = gain_grad
            begin += width

        def pre_slope(g, m, norm, total):
            return norm[2] * (g - (total[0] + m * total[1]) / count)

        def center_body(row, carry):
            mask, normed, slopes = second_slope(row)
            for a, width, g, m, n, total in zip(SECOND_AT, SECOND, slopes, normed, second, totals):
                value = (pre_slope(g, m, n, total) * mask).astype(BF16)
                s.normed[row + 1, 1 : lay.cols + 1, :, a : a + width] = value.reshape(
                    lay.cols, lay.frames, width
                )
            return carry

        lax.fori_loop(0, lay.rows, center_body, 0)

        def border_cells(row, col):
            mask = s.mask[row, col]
            normed = s.normed[row, col].astype(F32)
            slopes = border_slope(row, col)
            for a, width, g, n, total in zip(SECOND_AT, SECOND, slopes, second, totals):
                m = normed[:, a : a + width]
                g = g * sigmoid(m * (n[2] / n[1]) + n[3])
                value = jnp.where(mask > 0.0, pre_slope(g, m, n, total), 0.0)
                s.normed[row, col, :, a : a + width] = value.astype(BF16)

        def across(col, carry):
            border_cells(0, col)
            border_cells(lay.rows + 1, col)
            return carry

        lax.fori_loop(0, lay.cols + 2, across, 0)

        def along(row, carry):
            border_cells(row, 0)
            border_cells(row, lay.cols + 1)
            return carry

        lax.fori_loop(1, lay.rows + 1, along, 0)

        center = s.normed[1 : lay.rows + 1, 1 : lay.cols + 1].reshape(lay.cells, SECOND_WIDTH)
        turned_mid = center[:, 0:B1].T
        turned_small = center[:, 384:512].T

        def tap_body(tap, carry):
            row, col = lax.div(tap, 3), lax.rem(tap, 3)
            mid = dot(turned_mid, window(lay, s.mid_in, row, col, 3 * B1R)).astype(BF16)
            small = dot(turned_small, window(lay, s.small_in, row, col, 3 * B2R)).astype(BF16)
            store_blocks(index, tap * TAP_BLOCKS, mid)
            store_blocks(index, tap * TAP_BLOCKS + 80, small)
            return carry

        lax.fori_loop(0, 4, tap_body, 0)
        start_exchange(index, 0)
        lax.fori_loop(4, 9, tap_body, 0)
        start_exchange(index, 1)
        progress(index, 0)

        s.mid[...] = jnp.zeros(s.mid.shape, F32)
        s.small[:, 0 : 3 * B2R] = jnp.zeros((lay.cells, 3 * B2R), F32)

        def back_body(tap, carry):
            row, col = 2 - lax.div(tap, 3), 2 - lax.rem(tap, 3)
            slope = window(lay, s.normed, row, col, SECOND_WIDTH)
            s.mid[...] += dot(slope[:, 0:B1], mid_kernel(index, tap), NT)
            s.small[:, 0 : 3 * B2R] += dot(slope[:, 384:512], small_kernel(index, tap), NT)
            return carry

        for part in range(3):
            lax.fori_loop(3 * part, 3 * part + 3, back_body, 0)
            progress(index, 1 + part)

        def box_body(row, carry):
            s.box[row] = box_row(lay, s.normed[row, :, :, 512:640].astype(F32))
            return carry

        lax.fori_loop(0, lay.rows + 2, box_body, 0)

        def first_body(row, sums):
            cells = pl.ds(pl.multiple_of(row * lay.row_cells, lay.row_cells), lay.row_cells)
            s.projected_slope[cells, :] = box_rows(lay, row).astype(BF16)
            mid = s.mid[cells, :]
            small = s.small[cells, 0 : 3 * B2R]
            thirds = [
                jnp.concatenate(
                    [mid[:, B1R * t : B1R * (t + 1)], small[:, B2R * t : B2R * (t + 1)]], axis=1
                )
                for t in range(3)
            ]
            thin = thirds[1] + shifted(lay, thirds[2])[0] + shifted(lay, thirds[0])[1]
            mask = center_mask(lay, row)
            z = s.first[row].reshape(lay.row_cells, B0)
            z_thin = s.narrow[row + 1, 1 : lay.cols + 1].reshape(lay.row_cells, NARROW)
            normed = normalised(jnp.concatenate([z, z_thin], axis=1), first)
            g = jnp.concatenate([out_slope(row)[0], thin], axis=1)
            g = g * mask * sigmoid(normed * (first[2] / first[1]) + first[3])
            s.mid[cells, 0:REDUCE] = g
            return sums[0] + column_sum(g), sums[1] + column_sum(g * normed)

        zero = (jnp.zeros((1, REDUCE), F32),) * 2
        put_first(at + 1, lax.fori_loop(0, lay.rows, first_body, zero))
        start_sum(at + 1)

        progress(index, 4)
        store_blocks(index, LOW_AT + 196, dot(s.projected_slope[...].T, flat_block(lay)).astype(BF16))
        progress(index, 5)
        summed = end_sum(at + 1)
        total = (get_first(summed, 0), get_first(summed, 1))
        k.bias_grad[index, :, 0:REDUCE] = total[0]
        k.gain_grad[index, :, 0:REDUCE] = total[1]

        def low_body(row, carry):
            cells = pl.ds(pl.multiple_of(row * lay.row_cells, lay.row_cells), lay.row_cells)
            mask = center_mask(lay, row)
            z = s.first[row].reshape(lay.row_cells, B0)
            z_thin = s.narrow[row + 1, 1 : lay.cols + 1].reshape(lay.row_cells, NARROW)
            normed = normalised(jnp.concatenate([z, z_thin], axis=1), first)
            value = (pre_slope(s.mid[cells, 0:REDUCE], normed, first, total) * mask).astype(BF16)
            s.low[cells, :] = value
            slope = dot(value, k.v_w_reduce[index])
            slope = slope + dot(s.projected_slope[cells, :], k.v_w_pool[index], NT)
            lay.put_slope(row, slope * mask)
            return carry

        lax.fori_loop(0, lay.rows, low_body, 0)
        store_blocks(index, LOW_AT, dot(s.low[...].T, flat_block(lay)).astype(BF16))
        start_exchange(index, 2)
        progress(index, 6)

    def split(value):
        a, b_, c, d = B0, B0 + B1, B0 + B1 + B2, B0 + B1 + B2 + BP
        return [value[:, :a], value[:, a:b_], value[:, b_:c], value[:, c:d]]

    def spread_two(row, carry):
        value = k.v_out_grad[row].astype(F32).reshape(two.row_cells, k.v_out_grad.shape[-1])
        for a, part, width in zip(SECOND_AT, split(value)[1:], SECOND):
            part = part.reshape(two.cols, two.frames, width)
            k.grad_border[0, row + 1, 1 : two.cols + 1, :, a : a + width] = part.astype(BF16)
        return carry

    lax.fori_loop(0, two.rows, spread_two, 0)
    start_halo(two, k.grad_border.at[0], 4)

    def slope_two(row):
        value = k.v_out_grad[row].astype(F32).reshape(two.row_cells, k.v_out_grad.shape[-1])
        return split(value)

    def border_two(row, col):
        value = k.grad_border[0, row, col].astype(F32)
        return [value[:, a : a + n] for a, n in zip(SECOND_AT, SECOND)]

    def widen(ref, begin, value):
        width = value.shape[-1]
        for lane in range(0, width, 128):
            size = min(128, width - lane)
            for odd in range(2):
                ref[(begin + lane) // 128, pl.ds(odd, two.frames, stride=2), 0:size] = value[
                    :, lane : lane + size
                ]

    def wide(value, a, width):
        tiles = [value[..., lane // 128, :, :] for lane in range(a, a + width, 128)]
        return jnp.concatenate(tiles, axis=-1)[..., :width]

    def put_two(row, slope):
        slope = slope * 0.125
        for a, part in zip((0,) + tuple(B0 + a for a in SECOND_AT), split(slope)):
            width = part.shape[-1]
            part = part.reshape(two.cols, two.frames, width)
            for col in range(two.cols):
                widen(k.spread.at[row, col], a, part[col])
            if a >= B0:
                k.grad_border[1, row + 1, 1 : two.cols + 1, :, a - B0 : a - B0 + width] = part.astype(BF16)

    two.put_slope = put_two

    def end_two():
        end_halo(two, two.s.normed, 3)
        end_halo(two, k.grad_border.at[0], 4)

    backward(two, slope_two, border_two, 4, first_two, second_two, count_two, end_two)
    start_halo(two, k.grad_border.at[1], 5)

    def slope_one(row):
        value = k.spread[lax.div(row, 2)]
        out = []
        for a, width in zip((0,) + tuple(B0 + a for a in SECOND_AT), (B0,) + SECOND):
            part = wide(value, a, width)
            pieces = [part[col // 2] for col in range(one.cols)]
            out.append(jnp.concatenate(pieces, axis=0))
        return out

    def border_one(row, col):
        value = k.border_spread[lax.div(row + 1, 2), lax.div(col + 1, 2)]
        return [wide(value, a, n) for a, n in zip(SECOND_AT, SECOND)]

    def end_one():
        end_halo(one, one.s.normed, 1)
        end_halo(two, k.grad_border.at[1], 5)

        def widen_border(row, col):
            value = k.grad_border[1, row, col].astype(F32)
            widen(k.border_spread.at[row, col], 0, value)

        def across(col, carry):
            widen_border(0, col)
            widen_border(two.rows + 1, col)
            return carry

        lax.fori_loop(0, two.cols + 2, across, 0)

        def along(row, carry):
            widen_border(row, 0)
            widen_border(row, two.cols + 1)
            return carry

        lax.fori_loop(1, two.rows + 1, along, 0)

    def put_one(row, slope):
        k.input_grad[row] = slope.astype(BF16).reshape(one.cols, one.frames, slope.shape[-1])

    one.put_slope = put_one
    backward(one, slope_one, border_one, 6, first_one, second_one, count_one, end_one)
    for key in LAST_STEPS:
        next(exchanges[key], None)
    for steps in exchanges.values():
        for _ in steps:
            pass


def unpack_body(taps, low, mid_out, small_out, reduce_out, pool_out, unit):
    def lanes(blocks, tiles, rows, width):
        parts = []
        for tile in range(tiles):
            size = min(128, width - 128 * tile)
            part = blocks[tile * (rows // 16) : (tile + 1) * (rows // 16), :, 0:size]
            parts.append(part.reshape(rows, size))
        return parts

    @pl.when((pl.program_id(0) == 0) & (pl.program_id(1) == 0))
    def _():
        shape = unit.shape
        same = lax.broadcasted_iota(jnp.int32, shape, 0) == lax.broadcasted_iota(jnp.int32, shape, 1)
        unit[...] = same.astype(F32).astype(BF16)

    mid = jnp.concatenate(lanes(taps.at[0], 4, B1, 3 * B1R), axis=1)
    mid = dot(unit[...], mid, NT)
    small = lanes(taps.at[0, 80:88], 1, B2, 3 * B2R)[0]
    small = dot(unit[0 : 3 * B2R, 0 : 3 * B2R], small, NT)
    for t in range(3):
        mid_out[0, t, 0] = mid[B1R * t : B1R * (t + 1)]
        small_out[0, t, 0] = small[B2R * t : B2R * (t + 1)]

    @pl.when(pl.program_id(1) == 0)
    def _():
        channels = reduce_out.shape[-1]
        tiles = -(-channels // 128)
        for at, part in enumerate(lanes(low.at[0, 0:196], tiles, REDUCE, channels)):
            reduce_out[0, :, 128 * at : 128 * at + part.shape[1]] = part.astype(F32)
        for at, part in enumerate(lanes(low.at[0, 196:252], tiles, BP, channels)):
            size = part.shape[1]
            pool_out[0, 128 * at : 128 * at + size, :] = dot(unit[0:size, 0:size], part, NT)


def unpack(grads, channels):
    grid = (2, 9)
    shapes = ((2, 3, 9, B1R, B1), (2, 3, 9, B2R, B2), (2, REDUCE, channels), (2, channels, BP))
    mid_grad, small_grad, reduce_grad, pool_grad = pl.pallas_call(
        unpack_body,
        grid=grid,
        out_shape=[jax.ShapeDtypeStruct(shape, F32) for shape in shapes],
        in_specs=[
            pl.BlockSpec((1, TAP_BLOCKS, 16, 128), lambda i, j: (i, j, 0, 0)),
            pl.BlockSpec((1, 256, 16, 128), lambda i, j: (i, LOW_OUT // 256, 0, 0)),
        ],
        out_specs=[
            pl.BlockSpec((1, 3, 1, B1R, B1), lambda i, j: (i, 0, j, 0, 0)),
            pl.BlockSpec((1, 3, 1, B2R, B2), lambda i, j: (i, 0, j, 0, 0)),
            pl.BlockSpec((1, REDUCE, channels), lambda i, j: (i, 0, 0)),
            pl.BlockSpec((1, channels, BP), lambda i, j: (i, 0, 0)),
        ],
        scratch_shapes=[pltpu.VMEM((3 * B1R, 3 * B1R), BF16)],
        compiler_params=pltpu.CompilerParams(vmem_limit_bytes=40 * 1024 * 1024),
        name="unpack",
    )(grads, grads)
    return (
        jnp.swapaxes(reduce_grad, 1, 2),
        mid_grad.reshape(2, 27, B1R, B1),
        small_grad.reshape(2, 27, B2R, B2),
        pool_grad,
    )


def on_device(
    n_batch, n_wa, clip_features, frame_counts, w_reduce, w_mid, w_small, w_pool, norm_gain, norm_bias, out_grad
):
    frames, rows, cols, channels = clip_features.shape
    clips = frame_counts.shape[0]
    slot = frames // clips
    layers = (
        Layer(0, rows, cols, clips, slot),
        Layer(1, rows // 2, cols // 2, clips, slot // 2),
    )
    one, two = layers
    chips = n_batch * n_wa

    def cells_first(array):
        return array.transpose(1, 2, 0, 3)

    operands = dict(
        features=cells_first(clip_features),
        frame_counts=frame_counts,
        w_reduce=jnp.swapaxes(w_reduce, 1, 2),
        w_mid=w_mid,
        w_small=w_small,
        w_pool=w_pool,
        gain=norm_gain.reshape(2, 1, -1),
        bias=norm_bias.reshape(2, 1, -1),
        out_grad=cells_first(out_grad),
    )
    in_space = dict(frame_counts=pltpu.SMEM, gain=pltpu.VMEM, bias=pltpu.VMEM)
    out_space = dict(weight_grads=pl.ANY)
    results = dict(
        block_output=jax.ShapeDtypeStruct((two.rows, two.cols, two.frames, channels), BF16),
        input_grad=jax.ShapeDtypeStruct((rows, cols, frames, channels), BF16),
        weight_grads=jax.ShapeDtypeStruct((2, LOW_OUT + 256, 16, 128), BF16),
        gain_grad=jax.ShapeDtypeStruct(norm_gain[:, None].shape, F32),
        bias_grad=jax.ShapeDtypeStruct(norm_bias[:, None].shape, F32),
    )
    scratch = {}
    for name in ("w_reduce", "w_mid", "w_small", "w_pool", "out_grad"):
        scratch["v_" + name] = pltpu.VMEM(operands[name].shape, BF16)
    small_pad = (two.rows + 2, two.cols + 2)
    scratch.update(
        pairs=pltpu.VMEM((two.cols, (B0 + SECOND_WIDTH) // 128, one.frames, 128), F32),
        spread=pltpu.VMEM(
            (two.rows, two.cols, (B0 + SECOND_WIDTH) // 128, one.frames, 128), F32
        ),
        border_spread=pltpu.VMEM(small_pad + (SECOND_WIDTH // 128, one.frames, 128), F32),
        grad_border=pltpu.VMEM((2,) + small_pad + (two.frames, SECOND_WIDTH), BF16),
        sums=pltpu.VMEM((8, 1, SUM_WIDTH), F32),
        pair_sums=pltpu.VMEM((8, 1, SUM_WIDTH), F32),
        chip_sums=pltpu.VMEM((2, chips, 1, SUM_WIDTH), F32),
        load_sem=pltpu.SemaphoreType.DMA((6,)),
        pair_sem=pltpu.SemaphoreType.DMA((2, 8)),
        chip_sem=pltpu.SemaphoreType.DMA((2, 8)),
        halo_sem=pltpu.SemaphoreType.DMA((2, 6, 5)),
        grads=pltpu.VMEM((2, GRAD_BLOCKS, 16, 128), BF16),
        got_half=pltpu.VMEM((2, GRAD_BLOCKS // 2, 16, 128), BF16),
        got_eighth=pltpu.VMEM((2, GRAD_BLOCKS // 4, 16, 128), BF16),
        got_piece=pltpu.VMEM((2, GRAD_BLOCKS // 8, 16, 128), BF16),
        got_chunk=pltpu.VMEM((2, n_batch, GRAD_BLOCKS // 32, 16, 128), BF16),
        got_total=pltpu.VMEM((2, OWNERS, GRAD_BLOCKS // 32, 16, 128), BF16),
        free_sem=pltpu.SemaphoreType.REGULAR((2, 3, 3)),
        grad_sem=pltpu.SemaphoreType.DMA((2, 2, 3, 18)),
        out_sem=pltpu.SemaphoreType.DMA((2, 3)),
    )
    names = list(operands) + list(results) + list(scratch)
    layer_scratch = [lay.scratch(channels) for lay in layers]

    def body(*refs):
        rest = refs[len(names) :]
        for lay, parts in zip(layers, layer_scratch):
            lay.s = SimpleNamespace(**dict(zip(parts, rest[: len(parts)])))
            rest = rest[len(parts) :]
        kernel_body(names, (n_batch, n_wa, layers), refs[: len(names)])

    out = pl.pallas_call(
        body,
        out_shape=list(results.values()),
        in_specs=[pl.BlockSpec(memory_space=in_space.get(name, pl.ANY)) for name in operands],
        out_specs=[pl.BlockSpec(memory_space=out_space.get(name, pltpu.VMEM)) for name in results],
        scratch_shapes=list(scratch.values()) + [r for parts in layer_scratch for r in parts.values()],
        compiler_params=pltpu.CompilerParams(
            collective_id=0, has_side_effects=True, vmem_limit_bytes=63 * 1024 * 1024
        ),
        name="layers",
    )(*operands.values())
    out = dict(zip(results, out))

    reduce_grad, mid_grad, small_grad, pool_grad = unpack(out["weight_grads"], channels)

    return (
        out["block_output"].transpose(2, 0, 1, 3),
        out["input_grad"].transpose(2, 0, 1, 3),
        reduce_grad,
        mid_grad,
        small_grad,
        pool_grad,
        out["gain_grad"].reshape(norm_gain.shape),
        out["bias_grad"].reshape(norm_bias.shape),
    )


def solution(mesh):
    in_specs = (
        P("batch", "ha", "wa", None),
        P("batch"),
        P(),
        P(),
        P(),
        P(),
        P(),
        P(),
        P("batch", "ha", "wa", None),
    )
    out_specs = (
        P("batch", "ha", "wa", None),
        P("batch", "ha", "wa", None),
        P(),
        P(),
        P(),
        P(),
        P(),
        P(),
    )
    return jax.shard_map(
        functools.partial(on_device, mesh.shape["batch"], mesh.shape["wa"]),
        mesh=mesh,
        in_specs=in_specs,
        out_specs=out_specs,
        check_vma=False,
    )
```

time: 1690 us -> 242 us (0.14); the launches traced: 1670 us -> 242 us
  local copies, waits for them, and re-layouts: 432 us -> 17.6 us
  matrix products: 407 us -> 0 us
  blocking collectives: 323 us -> 0 us
  waiting for transfers between devices: 311 us -> 0 us
  Pallas kernels: 0 us -> 224 us
  other arithmetic: 131 us -> 0 us
  starting transfers between devices: 42.7 us -> 0 us
  between operations: 20.3 us -> 0.65 us
    dot_general x336 -> x0, matrix products: 407 us -> none  [the longest x104 136 us: conv_forward(): jnp.dot(window_slice(padded, offset, extent), kernel[offset], preferred_e...]
    psum x8 -> x0, blocking collectives: 323 us -> none  [the longest x4 161 us: slope_totals(): return lax.psum((partial_value[0], partial_value[1]), ('batch', 'ha', 'wa'))]
    psum x1 -> x0, waiting for transfers between devices: 290 us -> none  [on_device(): lax.psum((first_kernels[0], first_kernels[1], first_kernels[2], first_ker...]
    pallas_call x0 -> x2, Pallas kernels: none -> 224 us  [the longest x1 210 us: on_device(): pl.pallas_call(body, out_shape=list(results.values()), in_specs=[pl.Block...]
    reshape x114 -> x2, local copies, waits for them, and re-layouts: 162 us -> 2.6 us  [the longest x1 1.3 us: on_device(): norm_gain.reshape(2, 1, -1)]
    slice x163 -> x0, local copies, waits for them, and re-layouts: 156 us -> none  [the longest x138 142 us: window_slice(): padded[:, off_time:off_time + slot_len, off_row:off_row + tile_rows, off_...]
    convert_element_type x50 -> x0, local copies, waits for them, and re-layouts: 60.7 us -> none  [the longest x35 36.7 us: box_sum(): summed = summed + window_slice(padded, offset, extent).astype(jnp.float32)]
    ppermute x16 -> x0, starting transfers between devices: 42.7 us -> none  [the longest x8 31.5 us: padded_2(): lax.ppermute(lax.slice_in_dim(block, block.shape[dim] - width, None, axis...]
  transfers between devices with their start and end apart: 17 -> 0, of which waited for: 6 -> 0; matrix products, arithmetic and copies ran while one was open for 10% -> 0% of each run, Pallas kernels for 0% -> 0%
where the time goes in v1:
time: 242 us
  Pallas kernels  224 us (93%)
  local copies, waits for them, and re-layouts  17.6 us (7%)
    pallas_call x1, Pallas kernels, on_device(): pl.pallas_call(body, out_shape=list(results.values()), in_specs=[pl.Block...  210 us
    unnamed x11, local copies, waits for them, and re-layouts  15 us
    pallas_call x1, Pallas kernels, unpack(): pl.pallas_call(unpack_body, grid=grid, out_shape=[jax.ShapeDtypeStruct(sh...  13.8 us

profile of v1, /device:TPU:0, one launch (start us, length us, event | category | flops | bytes accessed | tf_op | source)
XLA Modules:
  0.0 241.9 jit_solution(17158624246094661614)
XLA Ops:
  0.6 1.3 reshape.34.refs_6_
  1.9 1.3 reshape.35.refs_7_
  3.2 1.7 copy.28
  4.9 3.3 %copy.27 = bf16[32,8,4,832]{3,0,2,1:T(8,128)(2,1)} copy(bf16[32,8,4,832]{3,2,1,0:T(4,128)(2,1)} %param.9) | data formatting | bytes 3407872 | tf_op args[0]
  8.2 209.8 %layers.1 = (bf16[4,2,16,832]{3,2,1,0:T(8,128)(2,1)}, bf16[8,4,32,832]{3,2,1,0:T(8,128)(2,1)}, bf16[2,1280,16,128]{3,2,1,0:T(8,128)(2,1)}, f32[2,1,1024]{2,1,0:T(1,128)}, f32[2,1,1024]{2,1,0:T(1,128)}) custom-call(bf16[8,4,32,832]{3,2,1,0:T(8,128)(2,1)} %bitcast.16, s32[2]{0:T(128)} %refs_1_.1, bf16[2,448,832]{2,1,0:T(8,128)(2,1)} %bitcast.18, ...), custom_call_target="tpu_custom_call" | custom-call | tf_op jit(solution)/shard_map/layers/pallas_call | solution.py:1137
  218.0 1.8 copy.19
  219.8 0.0 copy-start.1
  219.8 0.0 copy-start.2
  219.8 3.7 %copy.20 = bf16[32,8,4,832]{3,2,1,0:T(4,128)(2,1)} copy(bf16[32,8,4,832]{3,0,2,1:T(8,128)(2,1)} %bitcast.17) | data formatting | bytes 3407872
  223.5 0.0 copy-done.1
  223.5 0.0 copy-done.2
  223.5 0.6 copy_bitcast_fusion.2
  224.1 0.0 copy-start
  224.1 4.0 %copy-done = bf16[2,1280,16,128]{3,2,1,0:T(8,128)(2,1)S(1)} copy-done((bf16[2,1280,16,128]{3,2,1,0:T(8,128)(2,1)S(1)}, bf16[2,1280,16,128]{3,2,1,0:T(8,128)(2,1)}, u32[]{:S(2)}) %copy-start) | copy-done | bytes 10485784
  228.1 13.8 %unpack.1 = (f32[2,3,9,160,320]{4,3,2,1,0:T(8,128)}, f32[2,3,9,32,128]{4,3,2,1,0:T(8,128)}, f32[2,448,832]{2,1,0:T(8,128)}, f32[2,832,128]{2,1,0:T(8,128)}) custom-call(bf16[2,1280,16,128]{3,2,1,0:T(8,128)(2,1)S(1)} %copy-done, bf16[2,1280,16,128]{3,2,1,0:T(8,128)(2,1)S(1)} %copy-done), custom_call_target="tpu_custom_call" | custom-call | tf_op jit(solution)/shard_map/unpack/pallas_call | solution.py:1037
Async XLA Ops:
  219.8 3.7 %copy-start.1 = (f32[2,1,1024]{2,1,0:T(1,128)S(1)}, f32[2,1,1024]{2,1,0:T(1,128)}, u32[]{:S(2)}) copy-start(f32[2,1,1024]{2,1,0:T(1,128)} %get-tuple-element.24) | copy-start | bytes 24580
  219.8 3.7 %copy-start.2 = (f32[2,1,1024]{2,1,0:T(1,128)S(1)}, f32[2,1,1024]{2,1,0:T(1,128)}, u32[]{:S(2)}) copy-start(f32[2,1,1024]{2,1,0:T(1,128)} %get-tuple-element.25) | copy-start | bytes 24580
  224.1 4.0 %copy-start = (bf16[2,1280,16,128]{3,2,1,0:T(8,128)(2,1)S(1)}, bf16[2,1280,16,128]{3,2,1,0:T(8,128)(2,1)}, u32[]{:S(2)}) copy-start(bf16[2,1280,16,128]{3,2,1,0:T(8,128)(2,1)} %get-tuple-element.19.taps.low) | copy-start | bytes 31457284

commit v2 on v1

--- a/solution.py
+++ b/solution.py
@@ -31,19 +31,66 @@
 OWNERS = 4
 
 SCHEDULE = {
-    (1, 1): ((1, 0), (1, 1)),
-    (1, 5): ((1, 0), (1, 1)),
-    (1, 6): (),
-    (0, 7): ((1, 0), (1, 1), (1, 2)),
-    (0, 0): ((1, 0), (1, 1), (1, 2)),
-    (0, 1): ((0, 0), (0, 1), (1, 0), (1, 1), (1, 2)),
-    (0, 2): ((1, 0), (1, 1), (1, 2)),
-    (0, 3): ((0, 0), (0, 1), (1, 0), (1, 1), (1, 2)),
-    (0, 4): ((1, 0), (1, 1), (1, 2)),
-    (0, 5): ((0, 0), (0, 1), (1, 0), (1, 1), (1, 2)),
-    (0, 6): ((0, 0), (0, 1)),
+    (1, (5, 3)): ((1, 0),),
+    (1, (5, 8)): ((1, 1),),
+    (1, 7): ((1, 0),),
+    (1, 8): ((1, 2), (1, 1)),
+    (0, 0): ((1, 2),),
+    (0, 1): ((1, 0),),
+    (0, (2, 0)): ((1, 1),),
+    (0, (2, 3)): ((1, 2),),
+    (0, (2, 5)): ((1, 0),),
+    (0, (2, 8)): ((1, 1),),
+    (0, 3): ((1, 2),),
+    (0, (5, 1)): ((1, 0),),
+    (0, (5, 3)): ((0, 0),),
+    (0, (5, 7)): ((0, 0), (1, 1)),
+    (0, (5, 8)): ((0, 1),),
+    (0, 7): ((1, 2),),
+    (0, 8): ((0, 2), (0, 1)),
 }
-LAST_STEPS = ((0, 2), (0, 0), (0, 1)) * 9
+LAST_STEPS = (
+    (1, 0),
+    (0, 0),
+    (0, 2),
+    (1, 1),
+    (0, 1),
+    (1, 2),
+    (1, 0),
+    (0, 0),
+    (0, 2),
+    (1, 1),
+    (0, 0),
+    (0, 1),
+    (1, 2),
+    (1, 0),
+    (0, 2),
+    (0, 0),
+    (1, 0),
+    (1, 0),
+    (1, 1),
+    (0, 1),
+    (1, 2),
+    (1, 1),
+    (0, 2),
+    (0, 0),
+    (1, 2),
+    (1, 1),
+    (1, 2),
+    (0, 1),
+    (0, 0),
+    (0, 2),
+    (0, 0),
+    (0, 1),
+    (0, 0),
+    (0, 2),
+    (0, 1),
+    (0, 2),
+    (0, 1),
+    (0, 2),
+    (0, 1),
+    (0, 2),
+)
 
 NN = (((1,), (0,)), ((), ()))
 NT = (((1,), (1,)), ((), ()))
@@ -59,6 +106,10 @@
 
 def sigmoid(x):
     return 1.0 / (1.0 + jnp.exp(-x))
+
+
+def loop(count, body, init):
+    return body(0, init) if count == 1 else lax.fori_loop(0, count, body, init)
 
 
 class Layer:
@@ -68,6 +119,8 @@
         self.frames = clips * slot
         self.cells = rows * cols * self.frames
         self.row_cells = cols * self.frames
+        self.step = rows if index else 2
+        self.pad_step = rows + 2 if index else 2
 
     def scratch(self, channels):
         r, c, t, n = self.rows, self.cols, self.frames, self.cells
@@ -111,20 +164,36 @@
     def rotated(i):
         return lax.rem(my_chip + i, chips)
 
-    loads = []
-    for at, (source, target) in enumerate(
-        (
-            (k.features, one.s.block_in),
-            (k.w_reduce, k.v_w_reduce),
-            (k.w_pool, k.v_w_pool),
-            (k.w_mid, k.v_w_mid),
-            (k.w_small, k.v_w_small),
-            (k.out_grad, k.v_out_grad),
-        )
-    ):
-        copy = pltpu.make_async_copy(source, target, k.load_sem.at[at])
+    def load(at, source, target):
+        return pltpu.make_async_copy(source, target, k.load_sem.at[at])
+
+    def load_features(i):
+        rows = pl.ds(i * one.step, one.step)
+        return pltpu.make_async_copy(k.features.at[rows], one.s.block_in.at[rows], k.feature_sem.at[i])
+
+    def load_cubes(at, layer):
+        copies = []
+        for t in range(3):
+            mid, small = pl.ds(B1R * t, B1R), pl.ds(B2R * t, B2R)
+            copies.append(load(at + 2 * t, k.w_mid.at[layer, t], k.v_w_mid.at[layer, :, mid]))
+            copies.append(load(at + 2 * t + 1, k.w_small.at[layer, t], k.v_w_small.at[layer, :, small]))
+        return copies
+
+    def load_flat(at, layer):
+        return [
+            load(at, k.w_reduce.at[layer], k.v_w_reduce.at[layer]),
+            load(at + 1, k.w_pool.at[layer], k.v_w_pool.at[layer]),
+        ]
+
+    flat_one, flat_two = load_flat(0, 0), load_flat(2, 1)
+    cubes_one, cubes_two = load_cubes(4, 0), load_cubes(10, 1)
+    slope_load = load(16, k.out_grad, k.v_out_grad)
+    for copy in flat_one:
         copy.start()
-        loads.append(copy)
+    for i in range(one.rows // one.step):
+        load_features(i).start()
+    for copy in cubes_one + [slope_load] + flat_two + cubes_two:
+        copy.start()
 
     for lay in layers:
         s = lay.s
@@ -277,8 +346,26 @@
         piece, chunk = count // 16, count // 32
         stride = n_batch // OWNERS
         g = k.grads.at[layer]
-        x, y = lax.rem(w, 2), lax.div(w, 2)
-        pair, beside, below = (b, 1 - h, w), (b, h, w + 1 - 2 * x), (b, h, w + 2 - 4 * y)
+        r1, r2, r3, r4, r5 = (
+            r.at[layer] for r in (k.got_half, k.got_eighth, k.got_piece, k.got_chunk, k.got_total)
+        )
+        to_half, to_eighth, to_piece, to_chunk = begin // 2, begin // 4, begin // 8, begin // 32
+
+        def places():
+            b, h, w = (lax.axis_index(a) for a in AXES)
+            x, y = lax.rem(w, 2), lax.div(w, 2)
+            at = SimpleNamespace(b=b, h=h, w=w)
+            at.pair, at.beside, at.below = (b, 1 - h, w), (b, h, w + 1 - 2 * x), (b, h, w + 2 - 4 * y)
+            at.mine, at.other = begin + h * half, begin + (1 - h) * half
+            half_a, half_b = at.mine, at.mine + quarter
+            at.eighth_a, at.eighth_b = half_a + x * eighth, half_b + y * eighth
+            at.a, at.b_ = at.eighth_a + y * piece, at.eighth_b + x * piece
+            at.sent_a, at.sent_b = half_a + (1 - x) * eighth, half_b + (1 - y) * eighth
+            at.last_a, at.last_b = at.eighth_a + (1 - y) * piece, at.eighth_b + (1 - x) * piece
+            at.rank = lax.div(b, stride)
+            at.chunk = jnp.where(at.rank < 2, at.a, at.b_) + lax.rem(at.rank, 2) * chunk
+            at.chunks = [(at.a, at.b_)[owner // 2] + owner % 2 * chunk for owner in range(OWNERS)]
+            return at
 
         def copy(source, at, target, to, size, slot, device):
             return pltpu.make_async_remote_copy(
@@ -290,6 +377,36 @@
                 device_id_type=MESH,
             )
 
+        def pair_copies(at):
+            return [copy(g, at.other, r1, to_half, half, 0, at.pair)]
+
+        def eighth_copies(at):
+            return [
+                copy(g, at.sent_a, r2, to_eighth, eighth, 1, at.beside),
+                copy(g, at.sent_b, r2, to_eighth + eighth, eighth, 2, at.below),
+            ]
+
+        def piece_copies(at):
+            return [
+                copy(g, at.last_a, r3, to_piece, piece, 3, at.below),
+                copy(g, at.last_b, r3, to_piece + piece, piece, 4, at.beside),
+            ]
+
+        def piece_returns(at):
+            return [
+                copy(g, at.a, g, at.a, piece, 13, at.below),
+                copy(g, at.b_, g, at.b_, piece, 14, at.beside),
+            ]
+
+        def eighth_returns(at):
+            return [
+                copy(g, at.eighth_a, g, at.eighth_a, eighth, 15, at.beside),
+                copy(g, at.eighth_b, g, at.eighth_b, eighth, 16, at.below),
+            ]
+
+        def pair_returns(at):
+            return [copy(g, at.mine, g, at.mine, half, 17, at.pair)]
+
         def go(copies):
             for c in copies:
                 c.start()
@@ -315,159 +432,154 @@
         def wait_free(slot):
             pl.semaphore_wait(k.free_sem.at[layer, number, slot], 1)
 
-        r1, r2, r3, r4 = (r.at[layer] for r in (k.got_half, k.got_eighth, k.got_piece, k.got_chunk))
-        mine = begin + h * half
-        copies = [copy(g, begin + (1 - h) * half, r1, begin // 2, half, 0, pair)]
-        go(copies)
-        yield
-        end(copies)
-        free(0, pair)
-        add(mine, r1, begin // 2, half)
-        at_a, at_b = mine, mine + quarter
-        to = begin // 4
-        copies = [
-            copy(g, at_a + (1 - x) * eighth, r2, to, eighth, 1, beside),
-            copy(g, at_b + (1 - y) * eighth, r2, to + eighth, eighth, 2, below),
-        ]
-        go(copies)
-        yield
-        end(copies)
-        at_a, at_b = at_a + x * eighth, at_b + y * eighth
-        add(at_a, r2, to, eighth)
-        add(at_b, r2, to + eighth, eighth)
-        to = begin // 8
-        copies = [
-            copy(g, at_a + (1 - y) * piece, r3, to, piece, 3, below),
-            copy(g, at_b + (1 - x) * piece, r3, to + piece, piece, 4, beside),
-        ]
-        go(copies)
-        yield
-        end(copies)
-        free(1, below)
-        free(2, beside)
-        at_a, at_b = at_a + y * piece, at_b + x * piece
-        add(at_a, r3, to, piece)
-        add(at_b, r3, to + piece, piece)
-
-        def chunk_at(owner):
-            return (at_a, at_b)[owner // 2] + owner % 2 * chunk
-
-        to = begin // 32
-        r5 = k.got_total.at[layer]
-        for owner in range(OWNERS):
-
-            @pl.when(b != owner * stride)
-            def _(owner=owner):
-                pltpu.make_async_remote_copy(
-                    src_ref=g.at[pl.ds(chunk_at(owner), chunk)],
-                    dst_ref=r4.at[b, pl.ds(to, chunk)],
-                    send_sem=k.grad_sem.at[0, layer, number, 5 + owner],
-                    recv_sem=k.grad_sem.at[1, layer, number, 5],
-                    device_id=(owner * stride, h, w),
-                    device_id_type=MESH,
-                ).start()
-
-        yield
-
-        def for_owner(do):
+        def for_owner(at, do):
             if stride == 1:
                 do()
             else:
-                pl.when(lax.rem(b, stride) == 0)(do)
-
-        rank = lax.div(b, stride)
-        my_chunk = jnp.where(rank < 2, at_a, at_b) + lax.rem(rank, 2) * chunk
-
-        def collect():
-            others = r4.at[pl.ds(0, n_batch - 1), pl.ds(to, chunk)]
-            pltpu.make_async_copy(others, others, k.grad_sem.at[1, layer, number, 5]).wait()
-            r4[b, pl.ds(to, chunk)] = g[pl.ds(my_chunk, chunk)]
-            total = r4[0, pl.ds(to, chunk)].astype(F32)
-            for slot in range(1, n_batch):
-                total = total + r4[slot, pl.ds(to, chunk)].astype(F32)
-            g[pl.ds(my_chunk, chunk)] = total.astype(BF16)
-
-        for_owner(collect)
-        for owner in range(OWNERS):
-
-            @pl.when(b != owner * stride)
-            def _(owner=owner):
-                part = g.at[pl.ds(chunk_at(owner), chunk)]
+                pl.when(lax.rem(at.b, stride) == 0)(do)
+
+        def for_others(at, do):
+            for owner in range(OWNERS):
+                pl.when(at.b != owner * stride)(functools.partial(do, owner))
+
+        def share_copies(at):
+            return [
+                pltpu.make_async_remote_copy(
+                    src_ref=g.at[pl.ds(at.chunk, chunk)],
+                    dst_ref=r5.at[at.rank, pl.ds(to_chunk, chunk)],
+                    send_sem=k.grad_sem.at[0, layer, number, 9],
+                    recv_sem=k.grad_sem.at[1, layer, number, 9 + at.rank],
+                    device_id=(lax.rem(at.b + i, n_batch), at.h, at.w),
+                    device_id_type=MESH,
+                )
+                for i in range(1, n_batch)
+            ]
+
+        def start_pair():
+            go(pair_copies(places()))
+
+        def start_eighths():
+            at = places()
+            end(pair_copies(at))
+            free(0, at.pair)
+            add(at.mine, r1, to_half, half)
+            go(eighth_copies(at))
+
+        def start_pieces():
+            at = places()
+            end(eighth_copies(at))
+            add(at.eighth_a, r2, to_eighth, eighth)
+            add(at.eighth_b, r2, to_eighth + eighth, eighth)
+            go(piece_copies(at))
+
+        def start_chunks():
+            at = places()
+            end(piece_copies(at))
+            free(1, at.below)
+            free(2, at.beside)
+            add(at.a, r3, to_piece, piece)
+            add(at.b_, r3, to_piece + piece, piece)
+
+            def send_chunk(owner):
+                pltpu.make_async_remote_copy(
+                    src_ref=g.at[pl.ds(at.chunks[owner], chunk)],
+                    dst_ref=r4.at[at.b, pl.ds(to_chunk, chunk)],
+                    send_sem=k.grad_sem.at[0, layer, number, 5 + owner],
+                    recv_sem=k.grad_sem.at[1, layer, number, 5],
+                    device_id=(owner * stride, at.h, at.w),
+                    device_id_type=MESH,
+                ).start()
+
+            for_others(at, send_chunk)
+
+        def share_chunk():
+            at = places()
+
+            def collect():
+                others = r4.at[pl.ds(0, n_batch - 1), pl.ds(to_chunk, chunk)]
+                pltpu.make_async_copy(others, others, k.grad_sem.at[1, layer, number, 5]).wait()
+                r4[at.b, pl.ds(to_chunk, chunk)] = g[pl.ds(at.chunk, chunk)]
+                total = r4[0, pl.ds(to_chunk, chunk)].astype(F32)
+                for slot in range(1, n_batch):
+                    total = total + r4[slot, pl.ds(to_chunk, chunk)].astype(F32)
+                g[pl.ds(at.chunk, chunk)] = total.astype(BF16)
+                go(share_copies(at))
+
+            for_owner(at, collect)
+
+            def sent_chunk(owner):
+                part = g.at[pl.ds(at.chunks[owner], chunk)]
                 pltpu.make_async_copy(part, part, k.grad_sem.at[0, layer, number, 5 + owner]).wait()
 
-        def share_copy(i):
-            return pltpu.make_async_remote_copy(
-                src_ref=g.at[pl.ds(my_chunk, chunk)],
-                dst_ref=r5.at[rank, pl.ds(to, chunk)],
-                send_sem=k.grad_sem.at[0, layer, number, 9],
-                recv_sem=k.grad_sem.at[1, layer, number, 9 + rank],
-                device_id=(lax.rem(b + i, n_batch), h, w),
-                device_id_type=MESH,
-            )
-
-        def share():
-            def body(i, carry):
-                share_copy(i).start()
-                return carry
-
-            lax.fori_loop(1, n_batch, body, 0)
-
-        for_owner(share)
-        yield
-
-        def shared():
-            def body(i, carry):
-                share_copy(i).wait_send()
-                return carry
-
-            lax.fori_loop(1, n_batch, body, 0)
-
-        for_owner(shared)
-        for owner in range(OWNERS):
-
-            @pl.when(b != owner * stride)
-            def _(owner=owner):
-                part = r5.at[owner, pl.ds(to, chunk)]
+            for_others(at, sent_chunk)
+
+        def return_pieces():
+            at = places()
+
+            def shared():
+                for c in share_copies(at):
+                    c.wait_send()
+
+            for_owner(at, shared)
+
+            def take_chunk(owner):
+                part = r5.at[owner, pl.ds(to_chunk, chunk)]
                 pltpu.make_async_copy(part, part, k.grad_sem.at[1, layer, number, 9 + owner]).wait()
-                g[pl.ds(chunk_at(owner), chunk)] = r5[owner, pl.ds(to, chunk)]
-
-        copies = [
-            copy(g, at_a, g, at_a, piece, 13, below),
-            copy(g, at_b, g, at_b, piece, 14, beside),
-        ]
-        wait_free(1)
-        wait_free(2)
-        go(copies)
-        yield
-        end(copies)
-        at_a, at_b = mine + x * eighth, mine + quarter + y * eighth
-        copies = [
-            copy(g, at_a, g, at_a, eighth, 15, beside),
-            copy(g, at_b, g, at_b, eighth, 16, below),
-        ]
-        go(copies)
-        yield
-        end(copies)
-        copies = [copy(g, mine, g, mine, half, 17, pair)]
-        wait_free(0)
-        go(copies)
-        yield
-        end(copies)
-        target = k.weight_grads.at[layer, pl.ds(LOW_OUT if begin == LOW_AT else begin, count)]
-        out = pltpu.make_async_copy(g.at[pl.ds(begin, count)], target, k.out_sem.at[layer, number])
-        out.start()
-        yield
-        out.wait()
-
-    exchanges = {}
-
-    def start_exchange(layer, number):
-        exchanges[layer, number] = exchange(layer, number)
-        next(exchanges[layer, number])
-
-    def progress(layer, at):
-        for key in SCHEDULE.get((layer, at), ()):
-            next(exchanges[key], None)
+                g[pl.ds(at.chunks[owner], chunk)] = r5[owner, pl.ds(to_chunk, chunk)]
+
+            for_others(at, take_chunk)
+            wait_free(1)
+            wait_free(2)
+            go(piece_returns(at))
+
+        def return_eighths():
+            at = places()
+            end(piece_returns(at))
+            go(eighth_returns(at))
+
+        def return_halves():
+            at = places()
+            end(eighth_returns(at))
+            wait_free(0)
+            go(pair_returns(at))
+
+        def result():
+            target = k.weight_grads.at[layer, pl.ds(LOW_OUT if begin == LOW_AT else begin, count)]
+            sem = k.out_sem.at[layer, number]
+            return pltpu.make_async_copy(g.at[pl.ds(begin, count)], target, sem)
+
+        def start_result():
+            end(pair_returns(places()))
+
+            result().start()
+
+        def end_result():
+            result().wait()
+
+        return (
+            start_pair,
+            start_eighths,
+            start_pieces,
+            start_chunks,
+            share_chunk,
+            return_pieces,
+            return_eighths,
+            return_halves,
+            start_result,
+            end_result,
+        )
+
+    exchanges = {(layer, number): exchange(layer, number) for layer in range(2) for number in range(3)}
+    plan, taken = {}, dict.fromkeys(exchanges, 0)
+    for point, keys in list(SCHEDULE.items()) + [(None, LAST_STEPS)]:
+        for key in keys:
+            plan.setdefault(point, []).append(exchanges[key][taken[key]])
+            taken[key] += 1
+    assert all(taken[key] == len(exchanges[key]) for key in exchanges)
+
+    def progress(*point):
+        for step in plan.get(point, ()):
+            step()
 
     def flat_block(lay):
         block = lay.s.block_in[...]
@@ -495,13 +607,18 @@
         after = jnp.where(frame_at == lay.slot - 1, 0.0, pltpu.roll(value, count - 1, 0))
         return before, after
 
+    def cells_of(lay, i):
+        size = lay.step * lay.row_cells
+        return pl.ds(i * size if isinstance(i, int) else pl.multiple_of(i * size, size), size)
+
     def reduce_conv(lay):
-        s, at = lay.s, lay.index
-        step = 2
+        s, at, step = lay.s, lay.index, lay.step
         count = step * lay.row_cells
 
         def body(i, sums):
             mask = center_mask(lay, i * step, step)
+            if lay.index == 0:
+                load_features(i).wait()
             block = s.block_in[pl.ds(i * step, step)]
             block = block.reshape(count, block.shape[-1])
             if lay.index == 0:
@@ -526,48 +643,72 @@
             )
 
         zero = jnp.zeros((1, REDUCE), F32)
-        return lax.fori_loop(0, lay.rows // step, body, (zero, zero, jnp.zeros((1, 1), F32)))
+        return loop(lay.rows // step, body, (zero, zero, jnp.zeros((1, 1), F32)))
 
     def narrow_windows(lay, norm):
         s = lay.s
         average, scale, bias = norm
-        rows, cols, t = lay.rows, lay.cols, lay.frames
+        rows, cols, t, step = lay.rows, lay.cols, lay.frames, lay.pad_step
         for row in (0, rows + 1):
             s.narrow[row] = s.border[row, :, :, BP:].astype(F32)
         for col in (0, cols + 1):
             s.narrow[1 : rows + 1, col] = s.border[1 : rows + 1, col, :, BP:].astype(F32)
 
-        def body(row, carry):
-            count = (cols + 2) * t
-            z = s.narrow[row].reshape(count, NARROW)
-            mask = s.mask[row].reshape(count, 1)
+        def body(i, carry):
+            at = pl.ds(i * step, step)
+            count = step * (cols + 2) * t
+            z = s.narrow[at].reshape(count, NARROW)
+            mask = s.mask[at].reshape(count, 1)
             value = jnp.where(mask > 0.0, softplus((z - average) * scale + bias), 0.0)
             before, after = shifted(lay, value)
             parts = (before, value, after)
             mid = jnp.concatenate([p[:, :B1R] for p in parts], axis=1)
             small = jnp.concatenate([p[:, B1R:] for p in parts], axis=1)
-            s.mid_in[row] = mid.astype(BF16).reshape(cols + 2, t, 3 * B1R)
-            s.small_in[row] = small.astype(BF16).reshape(cols + 2, t, 3 * B2R)
-            s.box[row] = box_row(lay, s.border[row, :, :, 0:BP].astype(F32))
+            s.mid_in[at] = mid.astype(BF16).reshape(step, cols + 2, t, 3 * B1R)
+            s.small_in[at] = small.astype(BF16).reshape(step, cols + 2, t, 3 * B2R)
+            s.box[at] = box_row(lay, s.border[at, :, :, 0:BP].astype(F32))
             return carry
 
-        lax.fori_loop(0, rows + 2, body, 0)
+        loop((rows + 2) // step, body, 0)
 
     def box_row(lay, value):
-        cols, t = lay.cols, lay.frames
-        flat = value.reshape((cols + 2) * t, BP)
+        cols, t, step = lay.cols, lay.frames, lay.pad_step
+        flat = value.reshape(step * (cols + 2) * t, BP)
         before, after = shifted(lay, flat)
-        flat = (flat + before + after).reshape(cols + 2, t, BP)
-        return flat[0:cols] + flat[1 : cols + 1] + flat[2 : cols + 2]
+        flat = (flat + before + after).reshape(step, cols + 2, t, BP)
+        return flat[:, 0:cols] + flat[:, 1 : cols + 1] + flat[:, 2 : cols + 2]
 
     def box_rows(lay, row):
-        box = lay.s.box
-        total = box[row] + box[row + 1] + box[row + 2]
-        return total.reshape(lay.row_cells, BP) * (1.0 / 27.0)
+        box, step = lay.s.box, lay.step
+        total = box[pl.ds(row, step)] + box[pl.ds(row + 1, step)] + box[pl.ds(row + 2, step)]
+        return total.reshape(step * lay.row_cells, BP) * (1.0 / 27.0)
 
     def window(lay, ref, row, col, width):
         value = ref[pl.ds(row, lay.rows), pl.ds(col, lay.cols)]
         return value.reshape(lay.cells, width)
+
+    def taps(lay, body, at=None):
+        if lay.index:
+            for tap in range(9):
+                body(tap, 0)
+                progress(1, (at, tap))
+            return
+
+        def with_progress(tap, carry):
+            body(tap, carry)
+            for some in range(9):
+                if (0, (at, some)) in SCHEDULE:
+
+                    @pl.when(tap == some)
+                    def _(some=some):
+                        progress(0, (at, some))
+
+            return carry
+
+        lax.fori_loop(0, 9, with_progress, 0)
+
+    def tap_at(tap):
+        return (tap // 3, tap % 3) if isinstance(tap, int) else (lax.div(tap, 3), lax.rem(tap, 3))
 
     def cube_conv(lay):
         s, at = lay.s, lay.index
@@ -575,38 +716,31 @@
         s.small[...] = jnp.zeros(s.small.shape, F32)
 
         def body(tap, carry):
-            row, col = lax.div(tap, 3), lax.rem(tap, 3)
-            s.mid[:, 0:B1] += dot(window(lay, s.mid_in, row, col, 3 * B1R), mid_kernel(at, tap))
-            s.small[...] += dot(window(lay, s.small_in, row, col, 3 * B2R), small_kernel(at, tap))
+            row, col = tap_at(tap)
+            s.mid[:, 0:B1] += dot(window(lay, s.mid_in, row, col, 3 * B1R), k.v_w_mid[at, tap])
+            s.small[...] += dot(window(lay, s.small_in, row, col, 3 * B2R), k.v_w_small[at, tap])
             return carry
 
-        lax.fori_loop(0, 9, body, 0)
-
-    def mid_kernel(at, tap):
-        return jnp.concatenate([k.v_w_mid[at, 9 * t + tap] for t in range(3)], axis=0)
-
-    def small_kernel(at, tap):
-        return jnp.concatenate([k.v_w_small[at, 9 * t + tap] for t in range(3)], axis=0)
-
-    def second_rows(lay, row, count=1):
-        cells = pl.ds(pl.multiple_of(row * lay.row_cells, lay.row_cells), count * lay.row_cells)
+        taps(lay, body)
+
+    def second_rows(lay, i):
+        cells = cells_of(lay, i)
         return [
             ref[cells, 0:n] for ref, n in zip((lay.s.mid, lay.s.small, lay.s.pool), SECOND)
         ]
 
     def second_sums(lay):
-        def body(row, sums):
-            cells = pl.ds(pl.multiple_of(row * lay.row_cells, lay.row_cells), lay.row_cells)
-            lay.s.pool[cells, :] = box_rows(lay, row)
-            mask = center_mask(lay, row)
+        def body(i, sums):
+            lay.s.pool[cells_of(lay, i), :] = box_rows(lay, i * lay.step)
+            mask = center_mask(lay, i * lay.step, lay.step)
             out = []
-            for (total, square), value in zip(sums, second_rows(lay, row)):
+            for (total, square), value in zip(sums, second_rows(lay, i)):
                 inside = value * mask
                 out.append((total + column_sum(inside), square + column_sum(inside * value)))
             return tuple(out)
 
         zero = tuple((jnp.zeros((1, n), F32),) * 2 for n in SECOND)
-        return lax.fori_loop(0, lay.rows, body, zero)
+        return loop(lay.rows // lay.step, body, zero)
 
     def put_second(at, sums):
         for which in range(2):
@@ -635,23 +769,26 @@
     def first_params(k_of, at):
         return k_of[at][:, :REDUCE]
 
-    def forward(lay, at, count):
+    def forward(lay, at, count, cubes, before, meanwhile):
         s = lay.s
         total, square, valid = reduce_conv(lay)
+        before()
         start_halo(lay, s.border, 2 * lay.index)
         put_first(at, (total, square))
         if count is None:
             k.sums[at, :, 1024:1152] = jnp.broadcast_to(valid, (1, 128))
         start_sum(at)
+        meanwhile()
         end_halo(lay, s.border, 2 * lay.index)
+        for copy in cubes:
+            copy.wait()
         summed = end_sum(at)
         if count is None:
             count = summed[:, 1024:1025]
-        average, inv_std, scale = batch_norm_scale(
-            get_first(summed, 0), get_first(summed, 1), count, first_params(k.gain, lay.index)
-        )
-        first = (average, inv_std, scale, first_params(k.bias, lay.index))
-        narrow_windows(lay, (average[:, B0:], scale[:, B0:], first[3][:, B0:]))
+        gain = first_params(k.gain, lay.index)
+        first = batch_norm_scale(get_first(summed, 0), get_first(summed, 1), count, gain)
+        first += (first_params(k.bias, lay.index), gain)
+        narrow_windows(lay, (first[0][:, B0:], first[2][:, B0:], first[3][:, B0:]))
         cube_conv(lay)
         put_second(at + 1, second_sums(lay))
         start_sum(at + 1)
@@ -663,48 +800,68 @@
             second_params(k.gain, lay.index),
             second_params(k.bias, lay.index),
         ):
-            second.append(batch_norm_scale(total, square, count, gain) + (bias,))
+            second.append(batch_norm_scale(total, square, count, gain) + (bias, gain))
         return first, second, count
 
     def normalised(value, norm):
-        average, inv_std, scale, bias = norm
+        average, inv_std, scale, bias, gain = norm
         return (value - average) * inv_std
 
     def affine(value, norm):
-        average, inv_std, scale, bias = norm
+        average, inv_std, scale, bias, gain = norm
         return (value - average) * scale + bias
 
     def left_half(norm):
         return tuple(p[:, :B0] for p in norm)
 
-    def outputs(lay, row, first, second):
-        mask = center_mask(lay, row)
-        z = lay.s.first[row].reshape(lay.row_cells, B0)
+    def outputs(lay, i, first, second):
+        mask = center_mask(lay, i * lay.step, lay.step)
+        z = lay.s.first[pl.ds(i * lay.step, lay.step)].reshape(lay.step * lay.row_cells, B0)
         parts = [softplus(affine(z, left_half(first))) * mask]
-        values = second_rows(lay, row)
-        parts += [softplus(affine(v, n)) * mask for v, n in zip(values, second)]
-        for begin, width, v, n in zip(SECOND_AT, SECOND, values, second):
-            normed = normalised(v, n).astype(BF16).reshape(lay.cols, lay.frames, width)
-            lay.s.normed[row + 1, 1 : lay.cols + 1, :, begin : begin + width] = normed
+        parts += [softplus(affine(v, n)) * mask for v, n in zip(second_rows(lay, i), second)]
         return parts
 
-    for copy in loads[:3]:
+    def put_normed(lay, second):
+        def body(i, carry):
+            inner = pl.ds(i * lay.step + 1, lay.step)
+            for begin, width, v, n in zip(SECOND_AT, SECOND, second_rows(lay, i), second):
+                normed = normalised(v, n).astype(BF16)
+                normed = normed.reshape(lay.step, lay.cols, lay.frames, width)
+                lay.s.normed[inner, 1 : lay.cols + 1, :, begin : begin + width] = normed
+            return carry
+
+        loop(lay.rows // lay.step, body, 0)
+
+    for copy in flat_one:
         copy.wait()
-    beside = (w > 0).astype(jnp.int32) + (w < n_wa - 1).astype(jnp.int32)
-    pl.semaphore_wait(barrier, chips + beside)
-
-    for copy in loads[3:]:
-        copy.wait()
-    first_one, second_one, count_one = forward(one, 0, None)
+
+    def wait_barrier():
+        beside = (w > 0).astype(jnp.int32) + (w < n_wa - 1).astype(jnp.int32)
+        pl.semaphore_wait(barrier, chips + beside)
+
+    def spread_two():
+        slope_load.wait()
+        for a, part, width in zip(SECOND_AT, slope_two(0)[1:], SECOND):
+            part = part.reshape(two.rows, two.cols, two.frames, width).astype(BF16)
+            k.grad_border[0, 1 : two.rows + 1, 1 : two.cols + 1, :, a : a + width] = part
+        start_halo(two, k.grad_border.at[0], 4)
+
+    def split(value):
+        a, b_, c, d = B0, B0 + B1, B0 + B1 + B2, B0 + B1 + B2 + BP
+        return [value[:, :a], value[:, a:b_], value[:, b_:c], value[:, c:d]]
+
+    def slope_two(i):
+        value = k.v_out_grad[...].astype(F32)
+        return split(value.reshape(two.cells, value.shape[-1]))
+
+    first_one, second_one, count_one = forward(one, 0, None, cubes_one, wait_barrier, spread_two)
 
     def halve(row, carry):
-        low = outputs(one, 2 * row, first_one, second_one)
-        high = outputs(one, 2 * row + 1, first_one, second_one)
         begin = 0
-        for p, q in zip(low, high):
+        for p in outputs(one, row, first_one, second_one):
             width = p.shape[-1]
-            both = (p + q).reshape(two.cols, 2, one.frames, width)
-            both = both[:, 0] + both[:, 1]
+            both = p.reshape(2, two.cols, 2, one.frames, width)
+            both = both[0, :, 0] + both[0, :, 1] + both[1, :, 0] + both[1, :, 1]
             for lane in range(0, width, 128):
                 size = min(128, width - lane)
                 k.pairs[:, begin + lane // 128, :, 0:size] = both[:, :, lane : lane + size]
@@ -722,45 +879,45 @@
         return carry
 
     lax.fori_loop(0, two.rows, halve, 0)
-    start_halo(one, one.s.normed, 1)
-
-    first_two, second_two, count_two = forward(two, 2, count_one * 0.125)
-
-    def finish(row, carry):
-        parts = outputs(two, row, first_two, second_two)
-        value = jnp.concatenate(parts, axis=1).astype(BF16)
-        k.block_output[row] = value.reshape(two.cols, two.frames, value.shape[-1])
-        return carry
-
-    lax.fori_loop(0, two.rows, finish, 0)
-    start_halo(two, two.s.normed, 3)
+
+    for copy in flat_two:
+        copy.wait()
+
+    def share_normed():
+        put_normed(one, second_one)
+        start_halo(one, one.s.normed, 1)
+
+    first_two, second_two, count_two = forward(
+        two, 2, count_one * 0.125, cubes_two, lambda: None, share_normed
+    )
 
     def backward(lay, out_slope, border_slope, at, first, second, count, before_end):
-        s, index = lay.s, lay.index
-
-        def second_slope(row):
-            mask = center_mask(lay, row)
-            slopes = out_slope(row)[1:]
-            values = second_rows(lay, row)
+        s, index, step = lay.s, lay.index, lay.step
+        chunks = lay.rows // step
+        per_cell = 1.0 / count
+
+        def second_slope(i):
+            mask = center_mask(lay, i * step, step)
+            values = second_rows(lay, i)
             normed = [normalised(v, n) for v, n in zip(values, second)]
             slopes = [
-                g * mask * sigmoid(m * (n[2] / n[1]) + n[3])
-                for g, m, n in zip(slopes, normed, second)
+                g * mask * sigmoid(m * n[4] + n[3])
+                for g, m, n in zip(out_slope(i)[1:], normed, second)
             ]
             return mask, normed, slopes
 
-        def sum_body(row, sums):
-            mask, normed, slopes = second_slope(row)
+        def sum_body(i, sums):
+            mask, normed, slopes = second_slope(i)
             return tuple(
                 (t + column_sum(g), q + column_sum(g * m))
                 for (t, q), g, m in zip(sums, slopes, normed)
             )
 
         zero = tuple((jnp.zeros((1, n), F32),) * 2 for n in SECOND)
-        put_second(at, lax.fori_loop(0, lay.rows, sum_body, zero))
+        put_second(at, loop(chunks, sum_body, zero))
         start_sum(at)
         before_end()
-        progress(index, 7)
+        progress(index, 0)
         summed = end_sum(at)
         totals = list(zip(get_second(summed, 0), get_second(summed, 1)))
         begin = REDUCE
@@ -768,86 +925,70 @@
             k.bias_grad[index, :, begin : begin + width] = bias_grad
             k.gain_grad[index, :, begin : begin + width] = gain_grad
             begin += width
+        totals = [(t * per_cell, q * per_cell) for t, q in totals]
 
         def pre_slope(g, m, norm, total):
-            return norm[2] * (g - (total[0] + m * total[1]) / count)
-
-        def center_body(row, carry):
-            mask, normed, slopes = second_slope(row)
+            return norm[2] * (g - (total[0] + m * total[1]))
+
+        def center_body(i, carry):
+            mask, normed, slopes = second_slope(i)
+            inner = pl.ds(i * step + 1, step)
             for a, width, g, m, n, total in zip(SECOND_AT, SECOND, slopes, normed, second, totals):
                 value = (pre_slope(g, m, n, total) * mask).astype(BF16)
-                s.normed[row + 1, 1 : lay.cols + 1, :, a : a + width] = value.reshape(
-                    lay.cols, lay.frames, width
+                s.normed[inner, 1 : lay.cols + 1, :, a : a + width] = value.reshape(
+                    step, lay.cols, lay.frames, width
                 )
             return carry
 
-        lax.fori_loop(0, lay.rows, center_body, 0)
-
-        def border_cells(row, col):
-            mask = s.mask[row, col]
-            normed = s.normed[row, col].astype(F32)
-            slopes = border_slope(row, col)
+        loop(chunks, center_body, 0)
+
+        def border_cells(where, slopes):
+            mask = s.mask[where]
+            cells = mask.shape[0]
+            mask = mask.reshape(cells * lay.frames, 1)
+            normed = s.normed[where].astype(F32).reshape(cells * lay.frames, SECOND_WIDTH)
             for a, width, g, n, total in zip(SECOND_AT, SECOND, slopes, second, totals):
                 m = normed[:, a : a + width]
-                g = g * sigmoid(m * (n[2] / n[1]) + n[3])
-                value = jnp.where(mask > 0.0, pre_slope(g, m, n, total), 0.0)
-                s.normed[row, col, :, a : a + width] = value.astype(BF16)
-
-        def across(col, carry):
-            border_cells(0, col)
-            border_cells(lay.rows + 1, col)
-            return carry
-
-        lax.fori_loop(0, lay.cols + 2, across, 0)
-
-        def along(row, carry):
-            border_cells(row, 0)
-            border_cells(row, lay.cols + 1)
-            return carry
-
-        lax.fori_loop(1, lay.rows + 1, along, 0)
-
-        center = s.normed[1 : lay.rows + 1, 1 : lay.cols + 1].reshape(lay.cells, SECOND_WIDTH)
-        turned_mid = center[:, 0:B1].T
-        turned_small = center[:, 384:512].T
-
-        def tap_body(tap, carry):
-            row, col = lax.div(tap, 3), lax.rem(tap, 3)
-            mid = dot(turned_mid, window(lay, s.mid_in, row, col, 3 * B1R)).astype(BF16)
-            small = dot(turned_small, window(lay, s.small_in, row, col, 3 * B2R)).astype(BF16)
-            store_blocks(index, tap * TAP_BLOCKS, mid)
-            store_blocks(index, tap * TAP_BLOCKS + 80, small)
-            return carry
-
-        lax.fori_loop(0, 4, tap_body, 0)
-        start_exchange(index, 0)
-        lax.fori_loop(4, 9, tap_body, 0)
-        start_exchange(index, 1)
-        progress(index, 0)
-
+                g = g * sigmoid(m * n[4] + n[3])
+                value = jnp.where(mask > 0.0, pre_slope(g, m, n, total), 0.0).astype(BF16)
+                s.normed[where + (slice(None), slice(a, a + width))] = value.reshape(
+                    cells, lay.frames, width
+                )
+
+        border_cells((jnp.where(h == 0, lay.rows + 1, 0), slice(None)), border_slope(True, None))
+        for col in (0, lay.cols + 1):
+            border_cells((slice(1, lay.rows + 1), col), border_slope(False, col > 0))
+
+        progress(index, 1)
         s.mid[...] = jnp.zeros(s.mid.shape, F32)
         s.small[:, 0 : 3 * B2R] = jnp.zeros((lay.cells, 3 * B2R), F32)
 
         def back_body(tap, carry):
-            row, col = 2 - lax.div(tap, 3), 2 - lax.rem(tap, 3)
-            slope = window(lay, s.normed, row, col, SECOND_WIDTH)
-            s.mid[...] += dot(slope[:, 0:B1], mid_kernel(index, tap), NT)
-            s.small[:, 0 : 3 * B2R] += dot(slope[:, 384:512], small_kernel(index, tap), NT)
+            row, col = tap_at(tap)
+            slope = window(lay, s.normed, 2 - row, 2 - col, SECOND_WIDTH)
+            s.mid[...] += dot(slope[:, 0:B1], k.v_w_mid[index, tap], NT)
+            s.small[:, 0 : 3 * B2R] += dot(slope[:, 384:512], k.v_w_small[index, tap], NT)
             return carry
 
-        for part in range(3):
-            lax.fori_loop(3 * part, 3 * part + 3, back_body, 0)
-            progress(index, 1 + part)
-
-        def box_body(row, carry):
-            s.box[row] = box_row(lay, s.normed[row, :, :, 512:640].astype(F32))
+        taps(lay, back_body, 2)
+
+        def box_body(i, carry):
+            at = pl.ds(i * lay.pad_step, lay.pad_step)
+            s.box[at] = box_row(lay, s.normed[at, :, :, 512:640].astype(F32))
             return carry
 
-        lax.fori_loop(0, lay.rows + 2, box_body, 0)
-
-        def first_body(row, sums):
-            cells = pl.ds(pl.multiple_of(row * lay.row_cells, lay.row_cells), lay.row_cells)
-            s.projected_slope[cells, :] = box_rows(lay, row).astype(BF16)
+        loop((lay.rows + 2) // lay.pad_step, box_body, 0)
+        progress(index, 3)
+
+        def first_normed(i):
+            size = step * lay.row_cells
+            z = s.first[pl.ds(i * step, step)].reshape(size, B0)
+            z_thin = s.narrow[pl.ds(i * step + 1, step), 1 : lay.cols + 1].reshape(size, NARROW)
+            return normalised(jnp.concatenate([z, z_thin], axis=1), first)
+
+        def first_body(i, sums):
+            cells = cells_of(lay, i)
+            s.projected_slope[cells, :] = box_rows(lay, i * step).astype(BF16)
             mid = s.mid[cells, :]
             small = s.small[cells, 0 : 3 * B2R]
             thirds = [
@@ -857,66 +998,56 @@
                 for t in range(3)
             ]
             thin = thirds[1] + shifted(lay, thirds[2])[0] + shifted(lay, thirds[0])[1]
-            mask = center_mask(lay, row)
-            z = s.first[row].reshape(lay.row_cells, B0)
-            z_thin = s.narrow[row + 1, 1 : lay.cols + 1].reshape(lay.row_cells, NARROW)
-            normed = normalised(jnp.concatenate([z, z_thin], axis=1), first)
-            g = jnp.concatenate([out_slope(row)[0], thin], axis=1)
-            g = g * mask * sigmoid(normed * (first[2] / first[1]) + first[3])
+            mask = center_mask(lay, i * step, step)
+            normed = first_normed(i)
+            g = jnp.concatenate([out_slope(i)[0], thin], axis=1)
+            g = g * mask * sigmoid(normed * first[4] + first[3])
             s.mid[cells, 0:REDUCE] = g
             return sums[0] + column_sum(g), sums[1] + column_sum(g * normed)
 
         zero = (jnp.zeros((1, REDUCE), F32),) * 2
-        put_first(at + 1, lax.fori_loop(0, lay.rows, first_body, zero))
+        put_first(at + 1, loop(chunks, first_body, zero))
         start_sum(at + 1)
 
         progress(index, 4)
+
+        center = s.normed[1 : lay.rows + 1, 1 : lay.cols + 1].reshape(lay.cells, SECOND_WIDTH)
+        turned_mid = center[:, 0:B1].T
+        turned_small = center[:, 384:512].T
+
+        def tap_body(tap, carry):
+            row, col = tap_at(tap)
+            mid = dot(turned_mid, window(lay, s.mid_in, row, col, 3 * B1R)).astype(BF16)
+            small = dot(turned_small, window(lay, s.small_in, row, col, 3 * B2R)).astype(BF16)
+            store_blocks(index, tap * TAP_BLOCKS, mid)
+            store_blocks(index, tap * TAP_BLOCKS + 80, small)
+            return carry
+
+        taps(lay, tap_body, 5)
         store_blocks(index, LOW_AT + 196, dot(s.projected_slope[...].T, flat_block(lay)).astype(BF16))
-        progress(index, 5)
+        progress(index, 6)
         summed = end_sum(at + 1)
         total = (get_first(summed, 0), get_first(summed, 1))
         k.bias_grad[index, :, 0:REDUCE] = total[0]
         k.gain_grad[index, :, 0:REDUCE] = total[1]
 
-        def low_body(row, carry):
-            cells = pl.ds(pl.multiple_of(row * lay.row_cells, lay.row_cells), lay.row_cells)
-            mask = center_mask(lay, row)
-            z = s.first[row].reshape(lay.row_cells, B0)
-            z_thin = s.narrow[row + 1, 1 : lay.cols + 1].reshape(lay.row_cells, NARROW)
-            normed = normalised(jnp.concatenate([z, z_thin], axis=1), first)
+        total = (total[0] * per_cell, total[1] * per_cell)
+
+        def low_body(i, carry):
+            cells = cells_of(lay, i)
+            mask = center_mask(lay, i * step, step)
+            normed = first_normed(i)
             value = (pre_slope(s.mid[cells, 0:REDUCE], normed, first, total) * mask).astype(BF16)
             s.low[cells, :] = value
             slope = dot(value, k.v_w_reduce[index])
             slope = slope + dot(s.projected_slope[cells, :], k.v_w_pool[index], NT)
-            lay.put_slope(row, slope * mask)
+            lay.put_slope(i, slope * mask)
             return carry
 
-        lax.fori_loop(0, lay.rows, low_body, 0)
+        loop(chunks, low_body, 0)
+        progress(index, 7)
         store_blocks(index, LOW_AT, dot(s.low[...].T, flat_block(lay)).astype(BF16))
-        start_exchange(index, 2)
-        progress(index, 6)
-
-    def split(value):
-        a, b_, c, d = B0, B0 + B1, B0 + B1 + B2, B0 + B1 + B2 + BP
-        return [value[:, :a], value[:, a:b_], value[:, b_:c], value[:, c:d]]
-
-    def spread_two(row, carry):
-        value = k.v_out_grad[row].astype(F32).reshape(two.row_cells, k.v_out_grad.shape[-1])
-        for a, part, width in zip(SECOND_AT, split(value)[1:], SECOND):
-            part = part.reshape(two.cols, two.frames, width)
-            k.grad_border[0, row + 1, 1 : two.cols + 1, :, a : a + width] = part.astype(BF16)
-        return carry
-
-    lax.fori_loop(0, two.rows, spread_two, 0)
-    start_halo(two, k.grad_border.at[0], 4)
-
-    def slope_two(row):
-        value = k.v_out_grad[row].astype(F32).reshape(two.row_cells, k.v_out_grad.shape[-1])
-        return split(value)
-
-    def border_two(row, col):
-        value = k.grad_border[0, row, col].astype(F32)
-        return [value[:, a : a + n] for a, n in zip(SECOND_AT, SECOND)]
+        progress(index, 8)
 
     def widen(ref, begin, value):
         width = value.shape[-1]
@@ -931,70 +1062,76 @@
         tiles = [value[..., lane // 128, :, :] for lane in range(a, a + width, 128)]
         return jnp.concatenate(tiles, axis=-1)[..., :width]
 
-    def put_two(row, slope):
+    def put_two(i, slope):
         slope = slope * 0.125
         for a, part in zip((0,) + tuple(B0 + a for a in SECOND_AT), split(slope)):
             width = part.shape[-1]
-            part = part.reshape(two.cols, two.frames, width)
-            for col in range(two.cols):
-                widen(k.spread.at[row, col], a, part[col])
+            part = part.reshape(two.rows, two.cols, two.frames, width)
+            for row in range(two.rows):
+                for col in range(two.cols):
+                    widen(k.spread.at[row, col], a, part[row, col])
             if a >= B0:
-                k.grad_border[1, row + 1, 1 : two.cols + 1, :, a - B0 : a - B0 + width] = part.astype(BF16)
+                inner = (slice(1, two.rows + 1), slice(1, two.cols + 1), slice(None))
+                k.grad_border[(1,) + inner + (slice(a - B0, a - B0 + width),)] = part.astype(BF16)
 
     two.put_slope = put_two
 
+    def side(lay, across, last):
+        if across:
+            return (jnp.where(h == 0, lay.rows + 1, 0), slice(None))
+        return (slice(1, lay.rows + 1), lay.cols + 1 if last else 0)
+
+    def border_two(across, last):
+        value = k.grad_border[(0,) + side(two, across, last)].astype(F32)
+        value = value.reshape(value.shape[0] * two.frames, SECOND_WIDTH)
+        return [value[:, a : a + n] for a, n in zip(SECOND_AT, SECOND)]
+
     def end_two():
+        put_normed(two, second_two)
+        start_halo(two, two.s.normed, 3)
+        value = jnp.concatenate(outputs(two, 0, first_two, second_two), axis=1).astype(BF16)
+        k.block_output[...] = value.reshape(k.block_output.shape)
         end_halo(two, two.s.normed, 3)
         end_halo(two, k.grad_border.at[0], 4)
 
     backward(two, slope_two, border_two, 4, first_two, second_two, count_two, end_two)
     start_halo(two, k.grad_border.at[1], 5)
 
-    def slope_one(row):
-        value = k.spread[lax.div(row, 2)]
+    def slope_one(i):
+        value = k.spread[i]
         out = []
         for a, width in zip((0,) + tuple(B0 + a for a in SECOND_AT), (B0,) + SECOND):
             part = wide(value, a, width)
             pieces = [part[col // 2] for col in range(one.cols)]
-            out.append(jnp.concatenate(pieces, axis=0))
+            out.append(jnp.concatenate(pieces * one.step, axis=0))
         return out
 
-    def border_one(row, col):
-        value = k.border_spread[lax.div(row + 1, 2), lax.div(col + 1, 2)]
-        return [wide(value, a, n) for a, n in zip(SECOND_AT, SECOND)]
+    def border_one(across, last):
+        where = side(two, across, last)
+        value = k.border_spread[where] if across else k.border_spread[:, where[1]]
+        cells = range(one.cols + 2) if across else range(1, one.rows + 1)
+        out = []
+        for a, n in zip(SECOND_AT, SECOND):
+            part = wide(value, a, n)
+            out.append(jnp.concatenate([part[(cell + 1) // 2] for cell in cells], axis=0))
+        return out
 
     def end_one():
         end_halo(one, one.s.normed, 1)
         end_halo(two, k.grad_border.at[1], 5)
-
-        def widen_border(row, col):
-            value = k.grad_border[1, row, col].astype(F32)
-            widen(k.border_spread.at[row, col], 0, value)
-
-        def across(col, carry):
-            widen_border(0, col)
-            widen_border(two.rows + 1, col)
-            return carry
-
-        lax.fori_loop(0, two.cols + 2, across, 0)
-
-        def along(row, carry):
-            widen_border(row, 0)
-            widen_border(row, two.cols + 1)
-            return carry
-
-        lax.fori_loop(1, two.rows + 1, along, 0)
-
-    def put_one(row, slope):
-        k.input_grad[row] = slope.astype(BF16).reshape(one.cols, one.frames, slope.shape[-1])
+        places = [(side(two, True, None)[0], col) for col in range(two.cols + 2)]
+        places += [(row, col) for row in range(1, two.rows + 1) for col in (0, two.cols + 1)]
+        for row, col in places:
+            widen(k.border_spread.at[row, col], 0, k.grad_border[1, row, col].astype(F32))
+
+    def put_one(i, slope):
+        shape = (one.step, one.cols, one.frames, slope.shape[-1])
+        k.input_grad[pl.ds(i * one.step, one.step)] = slope.astype(BF16).reshape(shape)
 
     one.put_slope = put_one
     backward(one, slope_one, border_one, 6, first_one, second_one, count_one, end_one)
-    for key in LAST_STEPS:
-        next(exchanges[key], None)
-    for steps in exchanges.values():
-        for _ in steps:
-            pass
+    for step in plan[None]:
+        step()
 
 
 def unpack_body(taps, low, mid_out, small_out, reduce_out, pool_out, unit):
@@ -1080,8 +1217,8 @@
         features=cells_first(clip_features),
         frame_counts=frame_counts,
         w_reduce=jnp.swapaxes(w_reduce, 1, 2),
-        w_mid=w_mid,
-        w_small=w_small,
+        w_mid=w_mid.reshape(2, 3, 9, B1R, B1),
+        w_small=w_small.reshape(2, 3, 9, B2R, B2),
         w_pool=w_pool,
         gain=norm_gain.reshape(2, 1, -1),
         bias=norm_bias.reshape(2, 1, -1),
@@ -1097,8 +1234,12 @@
         bias_grad=jax.ShapeDtypeStruct(norm_bias[:, None].shape, F32),
     )
     scratch = {}
-    for name in ("w_reduce", "w_mid", "w_small", "w_pool", "out_grad"):
+    for name in ("w_reduce", "w_pool", "out_grad"):
         scratch["v_" + name] = pltpu.VMEM(operands[name].shape, BF16)
+    scratch.update(
+        v_w_mid=pltpu.VMEM((2, 9, 3 * B1R, B1), BF16),
+        v_w_small=pltpu.VMEM((2, 9, 3 * B2R, B2), BF16),
+    )
     small_pad = (two.rows + 2, two.cols + 2)
     scratch.update(
         pairs=pltpu.VMEM((two.cols, (B0 + SECOND_WIDTH) // 128, one.frames, 128), F32),
@@ -1110,7 +1251,8 @@
         sums=pltpu.VMEM((8, 1, SUM_WIDTH), F32),
         pair_sums=pltpu.VMEM((8, 1, SUM_WIDTH), F32),
         chip_sums=pltpu.VMEM((2, chips, 1, SUM_WIDTH), F32),
-        load_sem=pltpu.SemaphoreType.DMA((6,)),
+        load_sem=pltpu.SemaphoreType.DMA((17,)),
+        feature_sem=pltpu.SemaphoreType.DMA((one.rows // one.step,)),
         pair_sem=pltpu.SemaphoreType.DMA((2, 8)),
         chip_sem=pltpu.SemaphoreType.DMA((2, 8)),
         halo_sem=pltpu.SemaphoreType.DMA((2, 6, 5)),

time: 242 us -> 220 us (0.909)
  Pallas kernels: 224 us -> 201 us
    pallas_call x1, Pallas kernels: 210 us -> 187 us  [on_device(): pl.pallas_call(body, out_shape=list(results.values()), in_specs=[pl.Block...]
where the time goes in v2:
time: 220 us; the launch traced here: 219 us
  Pallas kernels  201 us (91%)
  local copies, waits for them, and re-layouts  17.6 us (8%)
    pallas_call x1, Pallas kernels, on_device(): pl.pallas_call(body, out_shape=list(results.values()), in_specs=[pl.Block...  187 us
    unnamed x11, local copies, waits for them, and re-layouts  15 us
    pallas_call x1, Pallas kernels, unpack(): pl.pallas_call(unpack_body, grid=grid, out_shape=[jax.ShapeDtypeStruct(sh...  13.8 us

profile of v2, /device:TPU:0, one launch (start us, length us, event | category | flops | bytes accessed | tf_op | source)
XLA Modules:
  0.0 219.2 jit_solution(11719227299929197289)
XLA Ops:
  0.6 1.3 reshape.42.refs_6_
  1.9 1.3 reshape.43.refs_7_
  3.2 1.7 copy.28
  4.9 3.3 %copy.27 = bf16[32,8,4,832]{3,0,2,1:T(8,128)(2,1)} copy(bf16[32,8,4,832]{3,2,1,0:T(4,128)(2,1)} %param.9) | data formatting | bytes 3407872 | tf_op args[0]
  8.2 187.1 %layers.1 = (bf16[4,2,16,832]{3,2,1,0:T(8,128)(2,1)}, bf16[8,4,32,832]{3,2,1,0:T(8,128)(2,1)}, bf16[2,1280,16,128]{3,2,1,0:T(8,128)(2,1)}, f32[2,1,1024]{2,1,0:T(1,128)}, f32[2,1,1024]{2,1,0:T(1,128)}) custom-call(bf16[8,4,32,832]{3,2,1,0:T(8,128)(2,1)} %bitcast.18, s32[2]{0:T(128)} %refs_1_.1, bf16[2,448,832]{2,1,0:T(8,128)(2,1)} %bitcast.21, ...), custom_call_target="tpu_custom_call" | custom-call | tf_op jit(solution)/shard_map/layers/pallas_call | solution.py:1279
  195.3 1.8 copy.19
  197.1 0.0 copy-start.1
  197.1 0.0 copy-start.2
  197.1 3.7 %copy.20 = bf16[32,8,4,832]{3,2,1,0:T(4,128)(2,1)} copy(bf16[32,8,4,832]{3,0,2,1:T(8,128)(2,1)} %bitcast.20) | data formatting | bytes 3407872
  200.8 0.0 copy-done.1
  200.8 0.0 copy-done.2
  200.8 0.6 copy_bitcast_fusion.2
  201.4 0.0 copy-start
  201.4 4.0 %copy-done = bf16[2,1280,16,128]{3,2,1,0:T(8,128)(2,1)S(1)} copy-done((bf16[2,1280,16,128]{3,2,1,0:T(8,128)(2,1)S(1)}, bf16[2,1280,16,128]{3,2,1,0:T(8,128)(2,1)}, u32[]{:S(2)}) %copy-start) | copy-done | bytes 10485784
  205.4 13.8 %unpack.1 = (f32[2,3,9,160,320]{4,3,2,1,0:T(8,128)}, f32[2,3,9,32,128]{4,3,2,1,0:T(8,128)}, f32[2,448,832]{2,1,0:T(8,128)}, f32[2,832,128]{2,1,0:T(8,128)}) custom-call(bf16[2,1280,16,128]{3,2,1,0:T(8,128)(2,1)S(1)} %copy-done, bf16[2,1280,16,128]{3,2,1,0:T(8,128)(2,1)S(1)} %copy-done), custom_call_target="tpu_custom_call" | custom-call | tf_op jit(solution)/shard_map/unpack/pallas_call | solution.py:1174
Async XLA Ops:
  197.1 3.7 %copy-start.1 = (f32[2,1,1024]{2,1,0:T(1,128)S(1)}, f32[2,1,1024]{2,1,0:T(1,128)}, u32[]{:S(2)}) copy-start(f32[2,1,1024]{2,1,0:T(1,128)} %get-tuple-element.24) | copy-start | bytes 24580
  197.1 3.7 %copy-start.2 = (f32[2,1,1024]{2,1,0:T(1,128)S(1)}, f32[2,1,1024]{2,1,0:T(1,128)}, u32[]{:S(2)}) copy-start(f32[2,1,1024]{2,1,0:T(1,128)} %get-tuple-element.25) | copy-start | bytes 24580
  201.4 4.0 %copy-start = (bf16[2,1280,16,128]{3,2,1,0:T(8,128)(2,1)S(1)}, bf16[2,1280,16,128]{3,2,1,0:T(8,128)(2,1)}, u32[]{:S(2)}) copy-start(bf16[2,1280,16,128]{3,2,1,0:T(8,128)(2,1)} %get-tuple-element.19.taps.low) | copy-start | bytes 31457284

commit v3 on v2

--- a/solution.py
+++ b/solution.py
@@ -33,51 +33,49 @@
 SCHEDULE = {
     (1, (5, 3)): ((1, 0),),
     (1, (5, 8)): ((1, 1),),
-    (1, 7): ((1, 0),),
-    (1, 8): ((1, 2), (1, 1)),
-    (0, 0): ((1, 2),),
-    (0, 1): ((1, 0),),
-    (0, (2, 0)): ((1, 1),),
-    (0, (2, 3)): ((1, 2),),
-    (0, (2, 5)): ((1, 0),),
+    (1, 6): ((1, 0),),
+    (1, 8): ((1, 2),),
+    (0, 0): ((1, 1), (1, 2), (1, 0),),
+    (0, 1): ((1, 1),),
+    (0, (5, 2)): ((1, 2),),
+    (0, (5, 3)): ((0, 0),),
+    (0, (5, 4)): ((1, 0),),
+    (0, (5, 6)): ((0, 0), (1, 1),),
+    (0, (5, 8)): ((0, 1), (1, 2),),
+    (0, (2, 3)): ((0, 1), (1, 0),),
+    (0, (2, 4)): ((0, 0),),
     (0, (2, 8)): ((1, 1),),
-    (0, 3): ((1, 2),),
-    (0, (5, 1)): ((1, 0),),
-    (0, (5, 3)): ((0, 0),),
-    (0, (5, 7)): ((0, 0), (1, 1)),
-    (0, (5, 8)): ((0, 1),),
-    (0, 7): ((1, 2),),
-    (0, 8): ((0, 2), (0, 1)),
+    (0, 4): ((1, 2), (0, 1),),
+    (0, 6): ((0, 0), (1, 0),),
+    (0, 7): ((0, 1),),
+    (0, 8): ((0, 2),),
 }
+EARLY_TAPS = (9, 0)
 LAST_STEPS = (
     (1, 0),
+    (1, 1),
+    (0, 2),
+    (1, 2),
     (0, 0),
+    (1, 0),
+    (1, 1),
+    (1, 0),
+    (0, 1),
     (0, 2),
+    (1, 0),
+    (1, 2),
+    (0, 0),
     (1, 1),
+    (0, 2),
+    (0, 1),
+    (1, 1),
+    (1, 2),
+    (1, 1),
+    (0, 0),
+    (1, 2),
+    (0, 2),
     (0, 1),
     (1, 2),
-    (1, 0),
-    (0, 0),
-    (0, 2),
-    (1, 1),
-    (0, 0),
-    (0, 1),
-    (1, 2),
-    (1, 0),
-    (0, 2),
-    (0, 0),
-    (1, 0),
-    (1, 0),
-    (1, 1),
-    (0, 1),
-    (1, 2),
-    (1, 1),
-    (0, 2),
-    (0, 0),
-    (1, 2),
-    (1, 1),
-    (1, 2),
-    (0, 1),
     (0, 0),
     (0, 2),
     (0, 0),
@@ -85,12 +83,13 @@
     (0, 0),
     (0, 2),
     (0, 1),
-    (0, 2),
     (0, 1),
     (0, 2),
-    (0, 1),
+    (0, 2),
     (0, 2),
 )
+
+NORMED_AT = ((0,), (1,), (2,), (3,), ())
 
 NN = (((1,), (0,)), ((), ()))
 NT = (((1,), (1,)), ((), ()))
@@ -169,7 +168,9 @@
 
     def load_features(i):
         rows = pl.ds(i * one.step, one.step)
-        return pltpu.make_async_copy(k.features.at[rows], one.s.block_in.at[rows], k.feature_sem.at[i])
+        return pltpu.make_async_copy(
+            k.features.at[:, rows], k.input_grad.at[:, rows], k.feature_sem.at[i]
+        )
 
     def load_cubes(at, layer):
         copies = []
@@ -192,9 +193,6 @@
         copy.start()
     for i in range(one.rows // one.step):
         load_features(i).start()
-    for copy in cubes_one + [slope_load] + flat_two + cubes_two:
-        copy.start()
-
     for lay in layers:
         s = lay.s
         for ref in (s.border, s.normed):
@@ -287,7 +285,7 @@
         rows, cols = lay.rows, lay.cols
 
         def remote(src, dst, way, device):
-            return pltpu.make_async_remote_copy(
+            return lambda: pltpu.make_async_remote_copy(
                 src_ref=ref.at[src],
                 dst_ref=ref.at[dst],
                 send_sem=k.halo_sem.at[0, at, way],
@@ -308,37 +306,100 @@
         ]
         return row, to_left, to_right
 
-    def start_halo(lay, ref, at):
+    def normed_copies():
+        ref, rows, cols = one.s.normed, one.rows, one.cols
+        half = rows // 2
+        src_row = jnp.where(h == 0, rows, 1)
+        dst_row = jnp.where(h == 0, 0, rows + 1)
+
+        def remote(part, slot, src, dst, device):
+            return lambda: pltpu.make_async_remote_copy(
+                src_ref=ref.at[src],
+                dst_ref=ref.at[dst],
+                send_sem=k.normed_sem.at[0, part, slot],
+                recv_sem=k.normed_sem.at[1, part, slot],
+                device_id=device,
+                device_id_type=MESH,
+            )
+
+        parts = []
+        for part in range(4):
+            left, low = part < 2, part % 2 == 0
+            src, dst = (1, cols + 1) if left else (cols, 0)
+            way = w - 1 if left else w + 1
+            run = pl.ds(1 if low else 1 + half, half)
+            copies = [remote(part, 0, (run, src), (run, dst), (b, h, way))]
+            if low:
+                copies.append(remote(part, 1, (src_row, src), (dst_row, dst), (b, 1 - h, way)))
+            parts.append((w > 0 if left else w < n_wa - 1, w < n_wa - 1 if left else w > 0, copies))
+        inner = pl.ds(1, cols)
+        row = remote(0, 2, (src_row, inner), (dst_row, inner), (b, 1 - h, w))
+        return row, parts
+
+    def start_normed(*which):
+        row, parts = normed_copies()
+        if 0 in which:
+            row().start()
+        for part in which:
+            sends, _, copies = parts[part]
+
+            @pl.when(sends)
+            def _(copies=copies):
+                for copy in copies:
+                    copy().start()
+
+    def end_normed():
+        row, parts = normed_copies()
+        row().wait()
+        for sends, receives, copies in parts:
+
+            @pl.when(sends)
+            def _(copies=copies):
+                for copy in copies:
+                    copy().wait_send()
+
+            @pl.when(receives)
+            def _(copies=copies):
+                for copy in copies:
+                    copy().wait_recv()
+
+    def start_halo(lay, ref, at, first=True, last=True):
         row, to_left, to_right = halo_copies(lay, ref, at)
-        row.start()
+        if first:
+            row().start()
+
+            @pl.when(w > 0)
+            def _():
+                for copy in to_left:
+                    copy().start()
+
+        if last:
+
+            @pl.when(w < n_wa - 1)
+            def _():
+                for copy in to_right:
+                    copy().start()
+
+    def end_halo(lay, ref, at, rows=True, cols=True):
+        row, to_left, to_right = halo_copies(lay, ref, at)
+        if rows:
+            row().wait()
+        if not cols:
+            return
 
         @pl.when(w > 0)
         def _():
             for copy in to_left:
-                copy.start()
+                copy().wait_send()
+            for copy in to_right:
+                copy().wait_recv()
 
         @pl.when(w < n_wa - 1)
         def _():
             for copy in to_right:
-                copy.start()
-
-    def end_halo(lay, ref, at):
-        row, to_left, to_right = halo_copies(lay, ref, at)
-        row.wait()
-
-        @pl.when(w > 0)
-        def _():
+                copy().wait_send()
             for copy in to_left:
-                copy.wait_send()
-            for copy in to_right:
-                copy.wait_recv()
-
-        @pl.when(w < n_wa - 1)
-        def _():
-            for copy in to_right:
-                copy.wait_send()
-            for copy in to_left:
-                copy.wait_recv()
+                copy().wait_recv()
 
     def exchange(layer, number):
         begin, count = BUNDLES[number]
@@ -607,6 +668,17 @@
         after = jnp.where(frame_at == lay.slot - 1, 0.0, pltpu.roll(value, count - 1, 0))
         return before, after
 
+    def reorder(lay, value, cells_first):
+        size, cols, frames = lay.row_cells, lay.cols, lay.frames
+        to = lax.broadcasted_iota(jnp.int32, (size, size), 0)
+        source = lax.broadcasted_iota(jnp.int32, (size, size), 1)
+        if cells_first:
+            wanted = lax.rem(to, frames) * cols + lax.div(to, frames)
+        else:
+            wanted = lax.rem(to, cols) * frames + lax.div(to, cols)
+        swap = (source == wanted).astype(F32).astype(BF16)
+        return dot(swap, value.reshape(size, value.shape[-1]))
+
     def cells_of(lay, i):
         size = lay.step * lay.row_cells
         return pl.ds(i * size if isinstance(i, int) else pl.multiple_of(i * size, size), size)
@@ -619,12 +691,14 @@
             mask = center_mask(lay, i * step, step)
             if lay.index == 0:
                 load_features(i).wait()
-            block = s.block_in[pl.ds(i * step, step)]
-            block = block.reshape(count, block.shape[-1])
             if lay.index == 0:
-                block = (block.astype(F32) * mask).astype(BF16)
+                block = [reorder(lay, k.input_grad[:, i * step + row], True) for row in range(step)]
+                block = (jnp.concatenate(block, axis=0) * mask).astype(BF16)
                 shape = (step, lay.cols, lay.frames, block.shape[-1])
                 s.block_in[pl.ds(i * step, step)] = block.reshape(shape)
+            else:
+                block = s.block_in[pl.ds(i * step, step)]
+                block = block.reshape(count, block.shape[-1])
             reduced = dot(block, k.v_w_reduce[at], NT)
             projected = dot(block, k.v_w_pool[at])
             rows = pl.ds(i * step, step)
@@ -645,31 +719,45 @@
         zero = jnp.zeros((1, REDUCE), F32)
         return loop(lay.rows // step, body, (zero, zero, jnp.zeros((1, 1), F32)))
 
-    def narrow_windows(lay, norm):
+    def narrow_cells(lay, norm, where):
         s = lay.s
         average, scale, bias = norm
-        rows, cols, t, step = lay.rows, lay.cols, lay.frames, lay.pad_step
-        for row in (0, rows + 1):
-            s.narrow[row] = s.border[row, :, :, BP:].astype(F32)
-        for col in (0, cols + 1):
-            s.narrow[1 : rows + 1, col] = s.border[1 : rows + 1, col, :, BP:].astype(F32)
+        z = s.narrow[where]
+        shape = z.shape[:-1]
+        z = z.reshape(-1, NARROW)
+        mask = s.mask[where].reshape(-1, 1)
+        value = jnp.where(mask > 0.0, softplus((z - average) * scale + bias), 0.0)
+        before, after = shifted(lay, value)
+        parts = (before, value, after)
+        mid = jnp.concatenate([p[:, :B1R] for p in parts], axis=1)
+        small = jnp.concatenate([p[:, B1R:] for p in parts], axis=1)
+        s.mid_in[where] = mid.astype(BF16).reshape(shape + (3 * B1R,))
+        s.small_in[where] = small.astype(BF16).reshape(shape + (3 * B2R,))
+
+    def narrow_center(lay, norm):
+        s, step = lay.s, lay.pad_step
+        inner = slice(1, lay.cols + 1)
+        for row in (0, lay.rows + 1):
+            s.narrow[row, inner] = s.border[row, inner, :, BP:].astype(F32)
+
+        def body(i, carry):
+            narrow_cells(lay, norm, (pl.ds(i * step, step), inner))
+            return carry
+
+        loop((lay.rows + 2) // step, body, 0)
+
+    def narrow_sides(lay, norm):
+        s, step = lay.s, lay.pad_step
+        for col in (0, lay.cols + 1):
+            s.narrow[:, col] = s.border[:, col, :, BP:].astype(F32)
+            narrow_cells(lay, norm, (slice(None), col))
 
         def body(i, carry):
             at = pl.ds(i * step, step)
-            count = step * (cols + 2) * t
-            z = s.narrow[at].reshape(count, NARROW)
-            mask = s.mask[at].reshape(count, 1)
-            value = jnp.where(mask > 0.0, softplus((z - average) * scale + bias), 0.0)
-            before, after = shifted(lay, value)
-            parts = (before, value, after)
-            mid = jnp.concatenate([p[:, :B1R] for p in parts], axis=1)
-            small = jnp.concatenate([p[:, B1R:] for p in parts], axis=1)
-            s.mid_in[at] = mid.astype(BF16).reshape(step, cols + 2, t, 3 * B1R)
-            s.small_in[at] = small.astype(BF16).reshape(step, cols + 2, t, 3 * B2R)
             s.box[at] = box_row(lay, s.border[at, :, :, 0:BP].astype(F32))
             return carry
 
-        loop((rows + 2) // step, body, 0)
+        loop((lay.rows + 2) // step, body, 0)
 
     def box_row(lay, value):
         cols, t, step = lay.cols, lay.frames, lay.pad_step
@@ -687,16 +775,16 @@
         value = ref[pl.ds(row, lay.rows), pl.ds(col, lay.cols)]
         return value.reshape(lay.cells, width)
 
-    def taps(lay, body, at=None):
+    def taps(lay, body, at, begin=0, end=9):
         if lay.index:
-            for tap in range(9):
+            for tap in range(begin, end):
                 body(tap, 0)
                 progress(1, (at, tap))
             return
 
         def with_progress(tap, carry):
             body(tap, carry)
-            for some in range(9):
+            for some in range(begin, end):
                 if (0, (at, some)) in SCHEDULE:
 
                     @pl.when(tap == some)
@@ -705,12 +793,12 @@
 
             return carry
 
-        lax.fori_loop(0, 9, with_progress, 0)
+        lax.fori_loop(begin, end, with_progress, 0)
 
     def tap_at(tap):
         return (tap // 3, tap % 3) if isinstance(tap, int) else (lax.div(tap, 3), lax.rem(tap, 3))
 
-    def cube_conv(lay):
+    def cube_conv(lay, meanwhile):
         s, at = lay.s, lay.index
         s.mid[:, 0:B1] = jnp.zeros((lay.cells, B1), F32)
         s.small[...] = jnp.zeros(s.small.shape, F32)
@@ -721,7 +809,20 @@
             s.small[...] += dot(window(lay, s.small_in, row, col, 3 * B2R), k.v_w_small[at, tap])
             return carry
 
-        taps(lay, body)
+        def inner_tap(i):
+            return 3 * i + 1
+
+        def outer_tap(i):
+            return 3 * (i // 2) + 2 * (i % 2) if isinstance(i, int) else 3 * lax.div(i, 2) + 2 * lax.rem(i, 2)
+
+        for count, to_tap in ((3, inner_tap), (6, outer_tap)):
+            if lay.index:
+                for i in range(count):
+                    body(to_tap(i), 0)
+            else:
+                lax.fori_loop(0, count, lambda i, carry, to_tap=to_tap: body(to_tap(i), carry), 0)
+            if to_tap is inner_tap:
+                meanwhile()
 
     def second_rows(lay, i):
         cells = cells_of(lay, i)
@@ -759,7 +860,7 @@
         return total[:, which * 512 : which * 512 + REDUCE]
 
     def second_params(k_of, at):
-        row = k_of[at]
+        row = k_of[at : at + 1, :]
         out, begin = [], REDUCE
         for width in SECOND:
             out.append(row[:, begin : begin + width])
@@ -767,19 +868,19 @@
         return out
 
     def first_params(k_of, at):
-        return k_of[at][:, :REDUCE]
-
-    def forward(lay, at, count, cubes, before, meanwhile):
+        return k_of[at : at + 1, 0:REDUCE]
+
+    def forward(lay, at, count, cubes, before, first_idle, after_first, in_conv, second_idle):
         s = lay.s
         total, square, valid = reduce_conv(lay)
         before()
-        start_halo(lay, s.border, 2 * lay.index)
         put_first(at, (total, square))
         if count is None:
             k.sums[at, :, 1024:1152] = jnp.broadcast_to(valid, (1, 128))
         start_sum(at)
-        meanwhile()
-        end_halo(lay, s.border, 2 * lay.index)
+        start_halo(lay, s.border, 2 * lay.index)
+        first_idle()
+        end_halo(lay, s.border, 2 * lay.index, cols=False)
         for copy in cubes:
             copy.wait()
         summed = end_sum(at)
@@ -788,10 +889,19 @@
         gain = first_params(k.gain, lay.index)
         first = batch_norm_scale(get_first(summed, 0), get_first(summed, 1), count, gain)
         first += (first_params(k.bias, lay.index), gain)
-        narrow_windows(lay, (first[0][:, B0:], first[2][:, B0:], first[3][:, B0:]))
-        cube_conv(lay)
+        after_first()
+        thin = (first[0][:, B0:], first[2][:, B0:], first[3][:, B0:])
+        narrow_center(lay, thin)
+
+        def sides():
+            end_halo(lay, s.border, 2 * lay.index, rows=False)
+            narrow_sides(lay, thin)
+            in_conv()
+
+        cube_conv(lay, sides)
         put_second(at + 1, second_sums(lay))
         start_sum(at + 1)
+        second_idle()
         summed = end_sum(at + 1)
         second = []
         for total, square, gain, bias in zip(
@@ -836,25 +946,35 @@
         copy.wait()
 
     def wait_barrier():
+        for copy in cubes_one + [slope_load] + flat_two + cubes_two:
+            copy.start()
         beside = (w > 0).astype(jnp.int32) + (w < n_wa - 1).astype(jnp.int32)
         pl.semaphore_wait(barrier, chips + beside)
 
     def spread_two():
         slope_load.wait()
+        for row in range(two.rows):
+            k.slopes[pl.ds(row * two.row_cells, two.row_cells), :] = reorder(
+                two, k.v_out_grad[:, row], True
+            ).astype(BF16)
         for a, part, width in zip(SECOND_AT, slope_two(0)[1:], SECOND):
             part = part.reshape(two.rows, two.cols, two.frames, width).astype(BF16)
             k.grad_border[0, 1 : two.rows + 1, 1 : two.cols + 1, :, a : a + width] = part
         start_halo(two, k.grad_border.at[0], 4)
 
+    def nothing():
+        return None
+
     def split(value):
         a, b_, c, d = B0, B0 + B1, B0 + B1 + B2, B0 + B1 + B2 + BP
         return [value[:, :a], value[:, a:b_], value[:, b_:c], value[:, c:d]]
 
     def slope_two(i):
-        value = k.v_out_grad[...].astype(F32)
-        return split(value.reshape(two.cells, value.shape[-1]))
-
-    first_one, second_one, count_one = forward(one, 0, None, cubes_one, wait_barrier, spread_two)
+        return split(k.slopes[...].astype(F32))
+
+    first_one, second_one, count_one = forward(
+        one, 0, None, cubes_one, wait_barrier, nothing, nothing, spread_two, nothing
+    )
 
     def halve(row, carry):
         begin = 0
@@ -878,20 +998,27 @@
             two.s.block_in[row, col] = mean.astype(BF16)
         return carry
 
+    put_normed(one, second_one)
+    start_normed(*NORMED_AT[0])
     lax.fori_loop(0, two.rows, halve, 0)
 
     for copy in flat_two:
         copy.wait()
 
     def share_normed():
-        put_normed(one, second_one)
-        start_halo(one, one.s.normed, 1)
+        start_normed(*NORMED_AT[1])
+
+    def share_third():
+        start_normed(*NORMED_AT[2])
+
+    def share_rest():
+        start_normed(*NORMED_AT[3])
 
     first_two, second_two, count_two = forward(
-        two, 2, count_one * 0.125, cubes_two, lambda: None, share_normed
+        two, 2, count_one * 0.125, cubes_two, nothing, share_normed, share_third, nothing, share_rest
     )
 
-    def backward(lay, out_slope, border_slope, at, first, second, count, before_end):
+    def backward(lay, out_slope, border_slope, at, first, second, count, before_end, after_end, before_low):
         s, index, step = lay.s, lay.index, lay.step
         chunks = lay.rows // step
         per_cell = 1.0 / count
@@ -919,11 +1046,12 @@
         before_end()
         progress(index, 0)
         summed = end_sum(at)
+        after_end()
         totals = list(zip(get_second(summed, 0), get_second(summed, 1)))
         begin = REDUCE
         for (bias_grad, gain_grad), width in zip(totals, SECOND):
-            k.bias_grad[index, :, begin : begin + width] = bias_grad
-            k.gain_grad[index, :, begin : begin + width] = gain_grad
+            k.bias_grad[index : index + 1, begin : begin + width] = bias_grad
+            k.gain_grad[index : index + 1, begin : begin + width] = gain_grad
             begin += width
         totals = [(t * per_cell, q * per_cell) for t, q in totals]
 
@@ -960,6 +1088,21 @@
             border_cells((slice(1, lay.rows + 1), col), border_slope(False, col > 0))
 
         progress(index, 1)
+
+        center = s.normed[1 : lay.rows + 1, 1 : lay.cols + 1].reshape(lay.cells, SECOND_WIDTH)
+        turned_mid = center[:, 0:B1].T
+        turned_small = center[:, 384:512].T
+
+        def tap_body(tap, carry):
+            row, col = tap_at(tap)
+            mid = dot(turned_mid, window(lay, s.mid_in, row, col, 3 * B1R)).astype(BF16)
+            small = dot(turned_small, window(lay, s.small_in, row, col, 3 * B2R)).astype(BF16)
+            store_blocks(index, tap * TAP_BLOCKS, mid)
+            store_blocks(index, tap * TAP_BLOCKS + 80, small)
+            return carry
+
+        taps(lay, tap_body, 5, 0, EARLY_TAPS[index])
+
         s.mid[...] = jnp.zeros(s.mid.shape, F32)
         s.small[:, 0 : 3 * B2R] = jnp.zeros((lay.cells, 3 * B2R), F32)
 
@@ -1011,40 +1154,25 @@
 
         progress(index, 4)
 
-        center = s.normed[1 : lay.rows + 1, 1 : lay.cols + 1].reshape(lay.cells, SECOND_WIDTH)
-        turned_mid = center[:, 0:B1].T
-        turned_small = center[:, 384:512].T
-
-        def tap_body(tap, carry):
-            row, col = tap_at(tap)
-            mid = dot(turned_mid, window(lay, s.mid_in, row, col, 3 * B1R)).astype(BF16)
-            small = dot(turned_small, window(lay, s.small_in, row, col, 3 * B2R)).astype(BF16)
-            store_blocks(index, tap * TAP_BLOCKS, mid)
-            store_blocks(index, tap * TAP_BLOCKS + 80, small)
-            return carry
-
-        taps(lay, tap_body, 5)
+        taps(lay, tap_body, 5, EARLY_TAPS[index])
         store_blocks(index, LOW_AT + 196, dot(s.projected_slope[...].T, flat_block(lay)).astype(BF16))
         progress(index, 6)
         summed = end_sum(at + 1)
         total = (get_first(summed, 0), get_first(summed, 1))
-        k.bias_grad[index, :, 0:REDUCE] = total[0]
-        k.gain_grad[index, :, 0:REDUCE] = total[1]
+        k.bias_grad[index : index + 1, 0:REDUCE] = total[0]
+        k.gain_grad[index : index + 1, 0:REDUCE] = total[1]
 
         total = (total[0] * per_cell, total[1] * per_cell)
 
         def low_body(i, carry):
             cells = cells_of(lay, i)
             mask = center_mask(lay, i * step, step)
-            normed = first_normed(i)
-            value = (pre_slope(s.mid[cells, 0:REDUCE], normed, first, total) * mask).astype(BF16)
-            s.low[cells, :] = value
-            slope = dot(value, k.v_w_reduce[index])
-            slope = slope + dot(s.projected_slope[cells, :], k.v_w_pool[index], NT)
-            lay.put_slope(i, slope * mask)
+            value = pre_slope(s.mid[cells, 0:REDUCE], first_normed(i), first, total) * mask
+            s.low[cells, :] = value.astype(BF16)
             return carry
 
         loop(chunks, low_body, 0)
+        before_low()
         progress(index, 7)
         store_blocks(index, LOW_AT, dot(s.low[...].T, flat_block(lay)).astype(BF16))
         progress(index, 8)
@@ -1074,7 +1202,13 @@
                 inner = (slice(1, two.rows + 1), slice(1, two.cols + 1), slice(None))
                 k.grad_border[(1,) + inner + (slice(a - B0, a - B0 + width),)] = part.astype(BF16)
 
-    two.put_slope = put_two
+    def input_slope(lay, low, projected):
+        slope = dot(low, k.v_w_reduce[lay.index])
+        return slope + dot(projected, k.v_w_pool[lay.index], NT)
+
+    def low_two():
+        mask = center_mask(two, 0, two.rows)
+        put_two(0, input_slope(two, two.s.low[...], two.s.projected_slope[...]) * mask)
 
     def side(lay, across, last):
         if across:
@@ -1090,11 +1224,16 @@
         put_normed(two, second_two)
         start_halo(two, two.s.normed, 3)
         value = jnp.concatenate(outputs(two, 0, first_two, second_two), axis=1).astype(BF16)
-        k.block_output[...] = value.reshape(k.block_output.shape)
+        for row in range(two.rows):
+            part = reorder(two, value[row * two.row_cells : (row + 1) * two.row_cells], False)
+            k.block_output[:, row] = part.reshape(two.frames, two.cols, -1).astype(BF16)
         end_halo(two, two.s.normed, 3)
         end_halo(two, k.grad_border.at[0], 4)
 
-    backward(two, slope_two, border_two, 4, first_two, second_two, count_two, end_two)
+    def after_two():
+        start_normed(*NORMED_AT[4])
+
+    backward(two, slope_two, border_two, 4, first_two, second_two, count_two, end_two, after_two, low_two)
     start_halo(two, k.grad_border.at[1], 5)
 
     def slope_one(i):
@@ -1117,76 +1256,78 @@
         return out
 
     def end_one():
-        end_halo(one, one.s.normed, 1)
+        end_normed()
         end_halo(two, k.grad_border.at[1], 5)
         places = [(side(two, True, None)[0], col) for col in range(two.cols + 2)]
         places += [(row, col) for row in range(1, two.rows + 1) for col in (0, two.cols + 1)]
         for row, col in places:
             widen(k.border_spread.at[row, col], 0, k.grad_border[1, row, col].astype(F32))
 
-    def put_one(i, slope):
-        shape = (one.step, one.cols, one.frames, slope.shape[-1])
-        k.input_grad[pl.ds(i * one.step, one.step)] = slope.astype(BF16).reshape(shape)
-
-    one.put_slope = put_one
-    backward(one, slope_one, border_one, 6, first_one, second_one, count_one, end_one)
+    backward(one, slope_one, border_one, 6, first_one, second_one, count_one, end_one, nothing, nothing)
+
+    def input_row(row, carry):
+        cells = pl.ds(pl.multiple_of(row * one.row_cells, one.row_cells), one.row_cells)
+        low = reorder(one, one.s.low[cells, :], False).astype(BF16)
+        projected = one.s.projected_slope[cells, :].astype(F32) * center_mask(one, row)
+        projected = reorder(one, projected.astype(BF16), False).astype(BF16)
+        slope = input_slope(one, low, projected)
+        k.input_grad[:, row] = slope.reshape(one.frames, one.cols, -1).astype(BF16)
+        return carry
+
+    lax.fori_loop(0, one.rows, input_row, 0)
     for step in plan[None]:
         step()
 
 
-def unpack_body(taps, low, mid_out, small_out, reduce_out, pool_out, unit):
+UNPACK_TAPS = 3
+
+
+def unpack_body(taps, low, mid_out, small_out, reduce_out, pool_out):
     def lanes(blocks, tiles, rows, width):
         parts = []
         for tile in range(tiles):
             size = min(128, width - 128 * tile)
             part = blocks[tile * (rows // 16) : (tile + 1) * (rows // 16), :, 0:size]
             parts.append(part.reshape(rows, size))
-        return parts
-
-    @pl.when((pl.program_id(0) == 0) & (pl.program_id(1) == 0))
-    def _():
-        shape = unit.shape
-        same = lax.broadcasted_iota(jnp.int32, shape, 0) == lax.broadcasted_iota(jnp.int32, shape, 1)
-        unit[...] = same.astype(F32).astype(BF16)
-
-    mid = jnp.concatenate(lanes(taps.at[0], 4, B1, 3 * B1R), axis=1)
-    mid = dot(unit[...], mid, NT)
-    small = lanes(taps.at[0, 80:88], 1, B2, 3 * B2R)[0]
-    small = dot(unit[0 : 3 * B2R, 0 : 3 * B2R], small, NT)
-    for t in range(3):
-        mid_out[0, t, 0] = mid[B1R * t : B1R * (t + 1)]
-        small_out[0, t, 0] = small[B2R * t : B2R * (t + 1)]
+        return jnp.concatenate(parts, axis=1)
+
+    def tap_body(tap, carry):
+        blocks = taps.at[0, pl.ds(tap * TAP_BLOCKS, TAP_BLOCKS)]
+        mid = lanes(blocks, 4, B1, 3 * B1R).T.astype(F32)
+        small = lanes(blocks.at[80:88], 1, B2, 3 * B2R).T.astype(F32)
+        for t in range(3):
+            mid_out[0, t, tap] = mid[B1R * t : B1R * (t + 1)]
+            small_out[0, t, tap] = small[B2R * t : B2R * (t + 1)]
+        return carry
+
+    lax.fori_loop(0, UNPACK_TAPS, tap_body, 0)
 
     @pl.when(pl.program_id(1) == 0)
     def _():
         channels = reduce_out.shape[-1]
         tiles = -(-channels // 128)
-        for at, part in enumerate(lanes(low.at[0, 0:196], tiles, REDUCE, channels)):
-            reduce_out[0, :, 128 * at : 128 * at + part.shape[1]] = part.astype(F32)
-        for at, part in enumerate(lanes(low.at[0, 196:252], tiles, BP, channels)):
-            size = part.shape[1]
-            pool_out[0, 128 * at : 128 * at + size, :] = dot(unit[0:size, 0:size], part, NT)
+        reduce_out[0] = lanes(low.at[0, 0:196], tiles, REDUCE, channels).astype(F32)
+        pool_out[0] = lanes(low.at[0, 196:252], tiles, BP, channels).T.astype(F32)
 
 
 def unpack(grads, channels):
-    grid = (2, 9)
+    n = UNPACK_TAPS
     shapes = ((2, 3, 9, B1R, B1), (2, 3, 9, B2R, B2), (2, REDUCE, channels), (2, channels, BP))
     mid_grad, small_grad, reduce_grad, pool_grad = pl.pallas_call(
         unpack_body,
-        grid=grid,
+        grid=(2, 9 // n),
         out_shape=[jax.ShapeDtypeStruct(shape, F32) for shape in shapes],
         in_specs=[
-            pl.BlockSpec((1, TAP_BLOCKS, 16, 128), lambda i, j: (i, j, 0, 0)),
+            pl.BlockSpec((1, n * TAP_BLOCKS, 16, 128), lambda i, j: (i, j, 0, 0)),
             pl.BlockSpec((1, 256, 16, 128), lambda i, j: (i, LOW_OUT // 256, 0, 0)),
         ],
         out_specs=[
-            pl.BlockSpec((1, 3, 1, B1R, B1), lambda i, j: (i, 0, j, 0, 0)),
-            pl.BlockSpec((1, 3, 1, B2R, B2), lambda i, j: (i, 0, j, 0, 0)),
+            pl.BlockSpec((1, 3, n, B1R, B1), lambda i, j: (i, 0, j, 0, 0)),
+            pl.BlockSpec((1, 3, n, B2R, B2), lambda i, j: (i, 0, j, 0, 0)),
             pl.BlockSpec((1, REDUCE, channels), lambda i, j: (i, 0, 0)),
             pl.BlockSpec((1, channels, BP), lambda i, j: (i, 0, 0)),
         ],
-        scratch_shapes=[pltpu.VMEM((3 * B1R, 3 * B1R), BF16)],
-        compiler_params=pltpu.CompilerParams(vmem_limit_bytes=40 * 1024 * 1024),
+        compiler_params=pltpu.CompilerParams(vmem_limit_bytes=60 * 1024 * 1024),
         name="unpack",
     )(grads, grads)
     return (
@@ -1210,28 +1351,25 @@
     one, two = layers
     chips = n_batch * n_wa
 
-    def cells_first(array):
-        return array.transpose(1, 2, 0, 3)
-
     operands = dict(
-        features=cells_first(clip_features),
+        features=clip_features,
         frame_counts=frame_counts,
         w_reduce=jnp.swapaxes(w_reduce, 1, 2),
         w_mid=w_mid.reshape(2, 3, 9, B1R, B1),
         w_small=w_small.reshape(2, 3, 9, B2R, B2),
         w_pool=w_pool,
-        gain=norm_gain.reshape(2, 1, -1),
-        bias=norm_bias.reshape(2, 1, -1),
-        out_grad=cells_first(out_grad),
+        gain=norm_gain,
+        bias=norm_bias,
+        out_grad=out_grad,
     )
     in_space = dict(frame_counts=pltpu.SMEM, gain=pltpu.VMEM, bias=pltpu.VMEM)
     out_space = dict(weight_grads=pl.ANY)
     results = dict(
-        block_output=jax.ShapeDtypeStruct((two.rows, two.cols, two.frames, channels), BF16),
-        input_grad=jax.ShapeDtypeStruct((rows, cols, frames, channels), BF16),
+        block_output=jax.ShapeDtypeStruct(out_grad.shape, BF16),
+        input_grad=jax.ShapeDtypeStruct(clip_features.shape, BF16),
         weight_grads=jax.ShapeDtypeStruct((2, LOW_OUT + 256, 16, 128), BF16),
-        gain_grad=jax.ShapeDtypeStruct(norm_gain[:, None].shape, F32),
-        bias_grad=jax.ShapeDtypeStruct(norm_bias[:, None].shape, F32),
+        gain_grad=jax.ShapeDtypeStruct(norm_gain.shape, F32),
+        bias_grad=jax.ShapeDtypeStruct(norm_bias.shape, F32),
     )
     scratch = {}
     for name in ("w_reduce", "w_pool", "out_grad"):
@@ -1242,6 +1380,7 @@
     )
     small_pad = (two.rows + 2, two.cols + 2)
     scratch.update(
+        slopes=pltpu.VMEM((two.cells, channels), BF16),
         pairs=pltpu.VMEM((two.cols, (B0 + SECOND_WIDTH) // 128, one.frames, 128), F32),
         spread=pltpu.VMEM(
             (two.rows, two.cols, (B0 + SECOND_WIDTH) // 128, one.frames, 128), F32
@@ -1255,6 +1394,7 @@
         feature_sem=pltpu.SemaphoreType.DMA((one.rows // one.step,)),
         pair_sem=pltpu.SemaphoreType.DMA((2, 8)),
         chip_sem=pltpu.SemaphoreType.DMA((2, 8)),
+        normed_sem=pltpu.SemaphoreType.DMA((2, 4, 3)),
         halo_sem=pltpu.SemaphoreType.DMA((2, 6, 5)),
         grads=pltpu.VMEM((2, GRAD_BLOCKS, 16, 128), BF16),
         got_half=pltpu.VMEM((2, GRAD_BLOCKS // 2, 16, 128), BF16),
@@ -1292,14 +1432,14 @@
     reduce_grad, mid_grad, small_grad, pool_grad = unpack(out["weight_grads"], channels)
 
     return (
-        out["block_output"].transpose(2, 0, 1, 3),
-        out["input_grad"].transpose(2, 0, 1, 3),
+        out["block_output"],
+        out["input_grad"],
         reduce_grad,
         mid_grad,
         small_grad,
         pool_grad,
-        out["gain_grad"].reshape(norm_gain.shape),
-        out["bias_grad"].reshape(norm_bias.shape),
+        out["gain_grad"],
+        out["bias_grad"],
     )
 
 

time: 220 us -> 186 us (0.85)
  Pallas kernels: 201 us -> 181 us
  local copies, waits for them, and re-layouts: 17.6 us -> 3.13 us
    pallas_call x1, Pallas kernels: 187 us -> 170 us  [on_device(): pl.pallas_call(body, out_shape=list(results.values()), in_specs=[pl.Block...]
    unnamed x11 -> x12, local copies, waits for them, and re-layouts: 15 us -> 3.13 us
    reshape x2 -> x0, local copies, waits for them, and re-layouts: 2.6 us -> none  [the longest x1 1.3 us: on_device(): norm_gain.reshape(2, 1, -1)]
where the time goes in v3:
time: 186 us; the launch traced here: 185 us
  Pallas kernels  181 us (97%)
  local copies, waits for them, and re-layouts  3.13 us (2%)
    pallas_call x1, Pallas kernels, on_device(): pl.pallas_call(body, out_shape=list(results.values()), in_specs=[pl.Block...  170 us
    pallas_call x1, Pallas kernels, unpack(): pl.pallas_call(unpack_body, grid=(2, 9 // n), out_shape=[jax.ShapeDtypeSt...  11.8 us

profile of v3, /device:TPU:0, one launch (start us, length us, event | category | flops | bytes accessed | tf_op | source)
XLA Modules:
  0.0 185.3 jit_solution(2464938029670445939)
XLA Ops:
  0.6 169.7 %layers.1 = (bf16[16,4,2,832]{3,2,1,0:T(2,128)(2,1)}, bf16[32,8,4,832]{3,2,1,0:T(4,128)(2,1)}, bf16[2,1280,16,128]{3,2,1,0:T(8,128)(2,1)}, f32[2,1024]{1,0:T(2,128)}, f32[2,1024]{1,0:T(2,128)}) custom-call(bf16[32,8,4,832]{3,2,1,0:T(4,128)(2,1)} %refs_0_.1, s32[2]{0:T(128)} %refs_1_.1, bf16[2,448,832]{2,1,0:T(8,128)(2,1)} %bitcast.7, ...), custom_call_target="tpu_custom_call" | custom-call | tf_op jit(solution)/shard_map/layers/pallas_call | solution.py:1419
  170.3 0.0 copy-start.1
  170.3 0.0 copy-start
  170.4 11.8 %unpack.1 = (f32[2,3,9,160,320]{4,3,2,1,0:T(8,128)}, f32[2,3,9,32,128]{4,3,2,1,0:T(8,128)}, f32[2,448,832]{2,1,0:T(8,128)}, f32[2,832,128]{2,1,0:T(8,128)}) custom-call(bf16[2,1280,16,128]{3,2,1,0:T(8,128)(2,1)} %get-tuple-element.19.taps.low, bf16[2,1280,16,128]{3,2,1,0:T(8,128)(2,1)} %get-tuple-element.19.taps.low), custom_call_target="tpu_custom_call" | custom-call | tf_op jit(solution)/shard_map/unpack/pallas_call | solution.py:1316
  182.1 0.0 copy-start.3
  182.1 0.0 copy-start.2
  182.1 0.0 copy-done.1
  182.1 0.7 copy.21
  182.8 0.0 copy-done
  182.8 1.2 copy.22
  184.0 0.0 copy-done.3
  184.1 0.6 copy.23
  184.7 0.0 copy-done.2
  184.7 0.6 copy.24
Async XLA Ops:
  170.3 11.8 %copy-start.1 = (bf16[16,4,2,832]{3,2,1,0:T(2,128)(2,1)S(1)}, bf16[16,4,2,832]{3,2,1,0:T(2,128)(2,1)}, u32[]{:S(2)}) copy-start(bf16[16,4,2,832]{3,2,1,0:T(2,128)(2,1)} %get-tuple-element.34) | copy-start | bytes 638980
  170.3 12.5 %copy-start = (bf16[32,8,4,832]{3,2,1,0:T(4,128)(2,1)S(1)}, bf16[32,8,4,832]{3,2,1,0:T(4,128)(2,1)}, u32[]{:S(2)}) copy-start(bf16[32,8,4,832]{3,2,1,0:T(4,128)(2,1)} %get-tuple-element.35) | copy-start | bytes 5111812
  182.1 1.9 %copy-start.3 = (f32[2,1024]{1,0:T(2,128)S(1)}, f32[2,1024]{1,0:T(2,128)}, u32[]{:S(2)}) copy-start(f32[2,1024]{1,0:T(2,128)} %get-tuple-element.40) | copy-start | bytes 24580
  182.1 2.5 %copy-start.2 = (f32[2,1024]{1,0:T(2,128)S(1)}, f32[2,1024]{1,0:T(2,128)}, u32[]{:S(2)}) copy-start(f32[2,1024]{1,0:T(2,128)} %get-tuple-element.41) | copy-start | bytes 24580

commit v4 on v3

--- a/solution.py
+++ b/solution.py
@@ -35,54 +35,50 @@
     (1, (5, 8)): ((1, 1),),
     (1, 6): ((1, 0),),
     (1, 8): ((1, 2),),
-    (0, 0): ((1, 1), (1, 2), (1, 0),),
-    (0, 1): ((1, 1),),
-    (0, (5, 2)): ((1, 2),),
+    (0, 0): ((1, 1), (1, 0),),
+    (0, (5, 0)): ((1, 1),),
+    (0, (5, 1)): ((1, 2), (1, 0),),
     (0, (5, 3)): ((0, 0),),
-    (0, (5, 4)): ((1, 0),),
-    (0, (5, 6)): ((0, 0), (1, 1),),
+    (0, (5, 5)): ((1, 1),),
+    (0, (5, 6)): ((0, 0),),
     (0, (5, 8)): ((0, 1), (1, 2),),
-    (0, (2, 3)): ((0, 1), (1, 0),),
-    (0, (2, 4)): ((0, 0),),
-    (0, (2, 8)): ((1, 1),),
-    (0, 4): ((1, 2), (0, 1),),
-    (0, 6): ((0, 0), (1, 0),),
-    (0, 7): ((0, 1),),
-    (0, 8): ((0, 2),),
+    (0, (2, 0)): ((1, 0),),
+    (0, (2, 2)): ((0, 1),),
+    (0, (2, 5)): ((1, 1), (1, 2),),
+    (0, (2, 7)): ((0, 0),),
+    (0, (2, 8)): ((1, 0),),
+    (0, 4): ((0, 1),),
+    (0, 6): ((0, 0), (1, 1), (1, 0), (1, 2),),
+    (0, 8): ((0, 2), (0, 1), (0, 2), (1, 1), (0, 0),),
 }
 EARLY_TAPS = (9, 0)
 LAST_STEPS = (
+    (1, 2),
     (1, 0),
-    (1, 1),
+    (1, 0),
     (0, 2),
-    (1, 2),
-    (0, 0),
+    (0, 1),
     (1, 0),
-    (1, 1),
-    (1, 0),
-    (0, 1),
-    (0, 2),
-    (1, 0),
-    (1, 2),
     (0, 0),
     (1, 1),
+    (1, 2),
     (0, 2),
+    (1, 1),
     (0, 1),
-    (1, 1),
-    (1, 2),
-    (1, 1),
     (0, 0),
     (1, 2),
     (0, 2),
     (0, 1),
     (1, 2),
+    (1, 1),
     (0, 0),
     (0, 2),
     (0, 0),
+    (1, 2),
+    (0, 1),
+    (0, 2),
     (0, 1),
     (0, 0),
-    (0, 2),
-    (0, 1),
     (0, 1),
     (0, 2),
     (0, 2),
@@ -100,7 +96,7 @@
 
 
 def softplus(x):
-    return jnp.maximum(x, 0.0) + jnp.log1p(jnp.exp(-jnp.abs(x)))
+    return jnp.maximum(x, 0.0) + jnp.log(1.0 + jnp.exp(-jnp.abs(x)))
 
 
 def sigmoid(x):
@@ -1018,6 +1014,30 @@
         two, 2, count_one * 0.125, cubes_two, nothing, share_normed, share_third, nothing, share_rest
     )
 
+    def level(lay, begin, end):
+        return softplus(k.bias[lay.index : lay.index + 1, begin:end]).astype(BF16).astype(F32)
+
+    def center_windows(lay):
+        mid, small = level(lay, B0, B0 + B1R), level(lay, B0 + B1R, REDUCE)
+        mid, small = (jnp.concatenate([v] * 3, axis=1) for v in (mid, small))
+        s, step = lay.s, lay.pad_step
+
+        def body(i, carry):
+            at = pl.ds(i * step, step)
+            for ref, value in ((s.mid_in, mid), (s.small_in, small)):
+                shape = (step,) + ref.shape[1:]
+                part = ref[at].reshape(-1, shape[-1]).astype(F32) - value
+                ref[at] = part.astype(BF16).reshape(shape)
+            return carry
+
+        loop((lay.rows + 2) // step, body, 0)
+
+    def centered_block(lay):
+        if lay.index == 0:
+            return flat_block(lay)
+        value = jnp.concatenate([level(one, 0, B0), level(one, REDUCE, k.bias.shape[1])], axis=1)
+        return (flat_block(lay).astype(F32) - value).astype(BF16)
+
     def backward(lay, out_slope, border_slope, at, first, second, count, before_end, after_end, before_low):
         s, index, step = lay.s, lay.index, lay.step
         chunks = lay.rows // step
@@ -1044,6 +1064,7 @@
         put_second(at, loop(chunks, sum_body, zero))
         start_sum(at)
         before_end()
+        center_windows(lay)
         progress(index, 0)
         summed = end_sum(at)
         after_end()
@@ -1174,7 +1195,7 @@
         loop(chunks, low_body, 0)
         before_low()
         progress(index, 7)
-        store_blocks(index, LOW_AT, dot(s.low[...].T, flat_block(lay)).astype(BF16))
+        store_blocks(index, LOW_AT, dot(s.low[...].T, centered_block(lay)).astype(BF16))
         progress(index, 8)
 
     def widen(ref, begin, value):
@@ -1282,7 +1303,7 @@
 UNPACK_TAPS = 3
 
 
-def unpack_body(taps, low, mid_out, small_out, reduce_out, pool_out):
+def unpack_body(taps, low, gain, bias, mid_out, small_out, reduce_out, pool_out, gain_out, bias_out):
     def lanes(blocks, tiles, rows, width):
         parts = []
         for tile in range(tiles):
@@ -1308,33 +1329,41 @@
         tiles = -(-channels // 128)
         reduce_out[0] = lanes(low.at[0, 0:196], tiles, REDUCE, channels).astype(F32)
         pool_out[0] = lanes(low.at[0, 196:252], tiles, BP, channels).T.astype(F32)
-
-
-def unpack(grads, channels):
+        gain_out[...] = gain[...]
+        bias_out[...] = bias[...]
+
+
+def unpack(grads, gain, bias, channels):
     n = UNPACK_TAPS
     shapes = ((2, 3, 9, B1R, B1), (2, 3, 9, B2R, B2), (2, REDUCE, channels), (2, channels, BP))
-    mid_grad, small_grad, reduce_grad, pool_grad = pl.pallas_call(
+    shapes += (gain.shape, bias.shape)
+    norms = [pl.BlockSpec(gain.shape, lambda i, j: (0, 0))] * 2
+    mid_grad, small_grad, reduce_grad, pool_grad, gain, bias = pl.pallas_call(
         unpack_body,
         grid=(2, 9 // n),
         out_shape=[jax.ShapeDtypeStruct(shape, F32) for shape in shapes],
         in_specs=[
             pl.BlockSpec((1, n * TAP_BLOCKS, 16, 128), lambda i, j: (i, j, 0, 0)),
             pl.BlockSpec((1, 256, 16, 128), lambda i, j: (i, LOW_OUT // 256, 0, 0)),
-        ],
+        ]
+        + norms,
         out_specs=[
             pl.BlockSpec((1, 3, n, B1R, B1), lambda i, j: (i, 0, j, 0, 0)),
             pl.BlockSpec((1, 3, n, B2R, B2), lambda i, j: (i, 0, j, 0, 0)),
             pl.BlockSpec((1, REDUCE, channels), lambda i, j: (i, 0, 0)),
             pl.BlockSpec((1, channels, BP), lambda i, j: (i, 0, 0)),
-        ],
+        ]
+        + norms,
         compiler_params=pltpu.CompilerParams(vmem_limit_bytes=60 * 1024 * 1024),
         name="unpack",
-    )(grads, grads)
+    )(grads, grads, gain, bias)
     return (
         jnp.swapaxes(reduce_grad, 1, 2),
         mid_grad.reshape(2, 27, B1R, B1),
         small_grad.reshape(2, 27, B2R, B2),
         pool_grad,
+        gain,
+        bias,
     )
 
 
@@ -1429,17 +1458,12 @@
     )(*operands.values())
     out = dict(zip(results, out))
 
-    reduce_grad, mid_grad, small_grad, pool_grad = unpack(out["weight_grads"], channels)
+    kernels_and_norms = unpack(out["weight_grads"], out["gain_grad"], out["bias_grad"], channels)
 
     return (
         out["block_output"],
         out["input_grad"],
-        reduce_grad,
-        mid_grad,
-        small_grad,
-        pool_grad,
-        out["gain_grad"],
-        out["bias_grad"],
+        *kernels_and_norms,
     )
 
 

time: 186 us -> 175 us (0.941)
  Pallas kernels: 181 us -> 172 us
    pallas_call x1, Pallas kernels: 170 us -> 160 us  [on_device(): pl.pallas_call(body, out_shape=list(results.values()), in_specs=[pl.Block...]
where the time goes in v4:
time: 175 us
  Pallas kernels  172 us (98%)
  local copies, waits for them, and re-layouts  1.93 us (1%)
    pallas_call x1, Pallas kernels, on_device(): pl.pallas_call(body, out_shape=list(results.values()), in_specs=[pl.Block...  160 us
    pallas_call x1, Pallas kernels, unpack(): pl.pallas_call(unpack_body, grid=(2, 9 // n), out_shape=[jax.ShapeDtypeSt...  11.8 us

profile of v4, /device:TPU:0, one launch (start us, length us, event | category | flops | bytes accessed | tf_op | source)
XLA Modules:
  0.0 174.8 jit_solution(6534385312606475111)
XLA Ops:
  0.6 160.4 %layers.1 = (bf16[16,4,2,832]{3,2,1,0:T(2,128)(2,1)}, bf16[32,8,4,832]{3,2,1,0:T(4,128)(2,1)}, bf16[2,1280,16,128]{3,2,1,0:T(8,128)(2,1)}, f32[2,1024]{1,0:T(2,128)}, f32[2,1024]{1,0:T(2,128)}) custom-call(bf16[32,8,4,832]{3,2,1,0:T(4,128)(2,1)} %refs_0_.1, s32[2]{0:T(128)} %refs_1_.1, bf16[2,448,832]{2,1,0:T(8,128)(2,1)} %bitcast.7, ...), custom_call_target="tpu_custom_call" | custom-call | tf_op jit(solution)/shard_map/layers/pallas_call | solution.py:1448
  161.1 0.0 copy-start.1
  161.1 0.0 copy-start
  161.1 11.8 %unpack.1 = (f32[2,3,9,160,320]{4,3,2,1,0:T(8,128)}, f32[2,3,9,32,128]{4,3,2,1,0:T(8,128)}, f32[2,448,832]{2,1,0:T(8,128)}, f32[2,832,128]{2,1,0:T(8,128)}, f32[2,1024]{1,0:T(2,128)}, /*index=5*/f32[2,1024]{1,0:T(2,128)}) custom-call(bf16[2,1280,16,128]{3,2,1,0:T(8,128)(2,1)} %get-tuple-element.21.taps.low, ...), custom_call_target="tpu_custom_call" | custom-call | tf_op jit(solution)/shard_map/unpack/pallas_call | solution.py:1341
  172.9 0.0 copy-done.1
  172.9 0.7 copy.19
  173.6 0.0 copy-done
  173.6 1.2 copy.20
Async XLA Ops:
  161.1 11.8 %copy-start.1 = (bf16[16,4,2,832]{3,2,1,0:T(2,128)(2,1)S(1)}, bf16[16,4,2,832]{3,2,1,0:T(2,128)(2,1)}, u32[]{:S(2)}) copy-start(bf16[16,4,2,832]{3,2,1,0:T(2,128)(2,1)} %get-tuple-element.38) | copy-start | bytes 638980
  161.1 12.5 %copy-start = (bf16[32,8,4,832]{3,2,1,0:T(4,128)(2,1)S(1)}, bf16[32,8,4,832]{3,2,1,0:T(4,128)(2,1)}, u32[]{:S(2)}) copy-start(bf16[32,8,4,832]{3,2,1,0:T(4,128)(2,1)} %get-tuple-element.39) | copy-start | bytes 5111812

commit v5 on v4

--- a/solution.py
+++ b/solution.py
@@ -35,53 +35,55 @@
     (1, (5, 8)): ((1, 1),),
     (1, 6): ((1, 0),),
     (1, 8): ((1, 2),),
-    (0, 0): ((1, 1), (1, 0),),
+    (0, 0): ((1, 2), (1, 0),),
+    (0, 1): ((1, 0), (1, 2),),
     (0, (5, 0)): ((1, 1),),
-    (0, (5, 1)): ((1, 2), (1, 0),),
     (0, (5, 3)): ((0, 0),),
-    (0, (5, 5)): ((1, 1),),
+    (0, (5, 5)): ((1, 2),),
     (0, (5, 6)): ((0, 0),),
-    (0, (5, 8)): ((0, 1), (1, 2),),
-    (0, (2, 0)): ((1, 0),),
-    (0, (2, 2)): ((0, 1),),
-    (0, (2, 5)): ((1, 1), (1, 2),),
-    (0, (2, 7)): ((0, 0),),
-    (0, (2, 8)): ((1, 0),),
-    (0, 4): ((0, 1),),
-    (0, 6): ((0, 0), (1, 1), (1, 0), (1, 2),),
-    (0, 8): ((0, 2), (0, 1), (0, 2), (1, 1), (0, 0),),
+    (0, (5, 7)): ((1, 0),),
+    (0, (5, 8)): ((0, 1),),
+    (0, (2, 0)): ((1, 1),),
+    (0, (2, 4)): ((1, 2), (0, 0),),
+    (0, (2, 5)): ((0, 1), (1, 1),),
+    (0, (2, 8)): ((1, 0), (0, 0),),
+    (0, 3): ((1, 2),),
+    (0, 6): ((0, 1), (1, 1), (1, 0),),
+    (0, 7): ((1, 2),),
+    (0, 8): ((0, 2), (0, 1), (0, 0),),
 }
 EARLY_TAPS = (9, 0)
 LAST_STEPS = (
+    (1, 0),
+    (0, 2),
+    (1, 1),
     (1, 2),
     (1, 0),
     (1, 0),
+    (0, 1),
     (0, 2),
-    (0, 1),
-    (1, 0),
-    (0, 0),
+    (1, 2),
     (1, 1),
     (1, 2),
     (0, 2),
+    (0, 1),
+    (0, 2),
+    (0, 0),
+    (0, 1),
+    (0, 2),
+    (0, 0),
     (1, 1),
     (0, 1),
-    (0, 0),
-    (1, 2),
+    (1, 1),
     (0, 2),
+    (1, 1),
     (0, 1),
-    (1, 2),
-    (1, 1),
+    (0, 1),
     (0, 0),
     (0, 2),
     (0, 0),
-    (1, 2),
-    (0, 1),
     (0, 2),
-    (0, 1),
     (0, 0),
-    (0, 1),
-    (0, 2),
-    (0, 2),
     (0, 2),
 )
 
@@ -162,10 +164,13 @@
     def load(at, source, target):
         return pltpu.make_async_copy(source, target, k.load_sem.at[at])
 
+    output_store = pltpu.make_async_copy(k.v_block_output, k.block_output, k.result_sem.at[0])
+    input_store = pltpu.make_async_copy(k.v_input_grad, k.input_grad, k.result_sem.at[1])
+
     def load_features(i):
         rows = pl.ds(i * one.step, one.step)
         return pltpu.make_async_copy(
-            k.features.at[:, rows], k.input_grad.at[:, rows], k.feature_sem.at[i]
+            k.features.at[:, rows], k.v_input_grad.at[:, rows], k.feature_sem.at[i]
         )
 
     def load_cubes(at, layer):
@@ -246,7 +251,7 @@
             device_id_type=MESH,
         )
         pair.start()
-        pair.wait()
+        pair.wait_recv()
         k.chip_sums[at % 2, my_chip] = k.sums[at] + k.pair_sums[at]
 
         def send(i, carry):
@@ -265,6 +270,7 @@
                 send(i, 0)
         else:
             lax.fori_loop(1, chips, send, 0)
+        pair.wait_send()
 
     def end_sum(at):
         for way in (1, 0):
@@ -325,16 +331,16 @@
             way = w - 1 if left else w + 1
             run = pl.ds(1 if low else 1 + half, half)
             copies = [remote(part, 0, (run, src), (run, dst), (b, h, way))]
-            if low:
+            if not low:
                 copies.append(remote(part, 1, (src_row, src), (dst_row, dst), (b, 1 - h, way)))
             parts.append((w > 0 if left else w < n_wa - 1, w < n_wa - 1 if left else w > 0, copies))
         inner = pl.ds(1, cols)
-        row = remote(0, 2, (src_row, inner), (dst_row, inner), (b, 1 - h, w))
+        row = remote(1, 2, (src_row, inner), (dst_row, inner), (b, 1 - h, w))
         return row, parts
 
     def start_normed(*which):
         row, parts = normed_copies()
-        if 0 in which:
+        if 1 in which:
             row().start()
         for part in which:
             sends, _, copies = parts[part]
@@ -688,7 +694,7 @@
             if lay.index == 0:
                 load_features(i).wait()
             if lay.index == 0:
-                block = [reorder(lay, k.input_grad[:, i * step + row], True) for row in range(step)]
+                block = [reorder(lay, k.v_input_grad[:, i * step + row], True) for row in range(step)]
                 block = (jnp.concatenate(block, axis=0) * mask).astype(BF16)
                 shape = (step, lay.cols, lay.frames, block.shape[-1])
                 s.block_in[pl.ds(i * step, step)] = block.reshape(shape)
@@ -927,16 +933,23 @@
         parts += [softplus(affine(v, n)) * mask for v, n in zip(second_rows(lay, i), second)]
         return parts
 
-    def put_normed(lay, second):
+    def put_normed(lay, second, begin, end, cols):
+        step = min(lay.step, end - begin)
+        skipped, count = cols.start, cols.stop - cols.start
+
         def body(i, carry):
-            inner = pl.ds(i * lay.step + 1, lay.step)
-            for begin, width, v, n in zip(SECOND_AT, SECOND, second_rows(lay, i), second):
-                normed = normalised(v, n).astype(BF16)
-                normed = normed.reshape(lay.step, lay.cols, lay.frames, width)
-                lay.s.normed[inner, 1 : lay.cols + 1, :, begin : begin + width] = normed
+            row = begin + i * step
+            inner = (pl.ds(row + 1, step), pl.ds(skipped + 1, count))
+            size = lay.row_cells
+            cells = pl.ds(row * size if isinstance(i, int) else pl.multiple_of(row * size, size), step * size)
+            for a, width, ref, n in zip(SECOND_AT, SECOND, (lay.s.mid, lay.s.small, lay.s.pool), second):
+                value = ref[cells, 0:width].reshape(step, lay.cols, lay.frames, width)
+                value = value[:, cols].reshape(step * count * lay.frames, width)
+                normed = normalised(value, n).astype(BF16).reshape(step, count, lay.frames, width)
+                lay.s.normed[inner + (slice(None), slice(a, a + width))] = normed
             return carry
 
-        loop(lay.rows // lay.step, body, 0)
+        loop((end - begin) // step, body, 0)
 
     for copy in flat_one:
         copy.wait()
@@ -994,7 +1007,8 @@
             two.s.block_in[row, col] = mean.astype(BF16)
         return carry
 
-    put_normed(one, second_one)
+    half_rows = one.rows // 2
+    put_normed(one, second_one, 0, half_rows, slice(0, 1))
     start_normed(*NORMED_AT[0])
     lax.fori_loop(0, two.rows, halve, 0)
 
@@ -1002,6 +1016,8 @@
         copy.wait()
 
     def share_normed():
+        put_normed(one, second_one, 0, half_rows, slice(1, one.cols))
+        put_normed(one, second_one, half_rows, one.rows, slice(0, one.cols))
         start_normed(*NORMED_AT[1])
 
     def share_third():
@@ -1242,12 +1258,13 @@
         return [value[:, a : a + n] for a, n in zip(SECOND_AT, SECOND)]
 
     def end_two():
-        put_normed(two, second_two)
+        put_normed(two, second_two, 0, two.rows, slice(0, two.cols))
         start_halo(two, two.s.normed, 3)
         value = jnp.concatenate(outputs(two, 0, first_two, second_two), axis=1).astype(BF16)
         for row in range(two.rows):
             part = reorder(two, value[row * two.row_cells : (row + 1) * two.row_cells], False)
-            k.block_output[:, row] = part.reshape(two.frames, two.cols, -1).astype(BF16)
+            k.v_block_output[:, row] = part.reshape(two.frames, two.cols, -1).astype(BF16)
+        output_store.start()
         end_halo(two, two.s.normed, 3)
         end_halo(two, k.grad_border.at[0], 4)
 
@@ -1292,15 +1309,18 @@
         projected = one.s.projected_slope[cells, :].astype(F32) * center_mask(one, row)
         projected = reorder(one, projected.astype(BF16), False).astype(BF16)
         slope = input_slope(one, low, projected)
-        k.input_grad[:, row] = slope.reshape(one.frames, one.cols, -1).astype(BF16)
+        k.v_input_grad[:, row] = slope.reshape(one.frames, one.cols, -1).astype(BF16)
         return carry
 
     lax.fori_loop(0, one.rows, input_row, 0)
+    input_store.start()
     for step in plan[None]:
         step()
-
-
-UNPACK_TAPS = 3
+    output_store.wait()
+    input_store.wait()
+
+
+UNPACK_TAPS = 9
 
 
 def unpack_body(taps, low, gain, bias, mid_out, small_out, reduce_out, pool_out, gain_out, bias_out):
@@ -1392,7 +1412,7 @@
         out_grad=out_grad,
     )
     in_space = dict(frame_counts=pltpu.SMEM, gain=pltpu.VMEM, bias=pltpu.VMEM)
-    out_space = dict(weight_grads=pl.ANY)
+    out_space = dict(weight_grads=pl.ANY, block_output=pl.ANY, input_grad=pl.ANY)
     results = dict(
         block_output=jax.ShapeDtypeStruct(out_grad.shape, BF16),
         input_grad=jax.ShapeDtypeStruct(clip_features.shape, BF16),
@@ -1410,6 +1430,9 @@
     small_pad = (two.rows + 2, two.cols + 2)
     scratch.update(
         slopes=pltpu.VMEM((two.cells, channels), BF16),
+        v_block_output=pltpu.VMEM(out_grad.shape, BF16),
+        v_input_grad=pltpu.VMEM(clip_features.shape, BF16),
+        result_sem=pltpu.SemaphoreType.DMA((2,)),
         pairs=pltpu.VMEM((two.cols, (B0 + SECOND_WIDTH) // 128, one.frames, 128), F32),
         spread=pltpu.VMEM(
             (two.rows, two.cols, (B0 + SECOND_WIDTH) // 128, one.frames, 128), F32

time: 175 us -> 172 us (0.983)
  Pallas kernels: 172 us -> 169 us
where the time goes in v5:
time: 172 us
  Pallas kernels  169 us (98%)
  local copies, waits for them, and re-layouts  1.93 us (1%)
    pallas_call x1, Pallas kernels, on_device(): pl.pallas_call(body, out_shape=list(results.values()), in_specs=[pl.Block...  159 us
    pallas_call x1, Pallas kernels, unpack(): pl.pallas_call(unpack_body, grid=(2, 9 // n), out_shape=[jax.ShapeDtypeSt...  10.3 us

profile of v5, /device:TPU:0, one launch (start us, length us, event | category | flops | bytes accessed | tf_op | source)
XLA Modules:
  0.0 171.6 jit_solution(14029037722966931347)
XLA Ops:
  0.6 158.7 %layers.1 = (bf16[16,4,2,832]{3,2,1,0:T(2,128)(2,1)}, bf16[32,8,4,832]{3,2,1,0:T(4,128)(2,1)}, bf16[2,1280,16,128]{3,2,1,0:T(8,128)(2,1)}, f32[2,1024]{1,0:T(2,128)}, f32[2,1024]{1,0:T(2,128)}) custom-call(bf16[32,8,4,832]{3,2,1,0:T(4,128)(2,1)} %refs_0_.1, s32[2]{0:T(128)} %refs_1_.1, bf16[2,448,832]{2,1,0:T(8,128)(2,1)} %bitcast.7, ...), custom_call_target="tpu_custom_call" | custom-call | tf_op jit(solution)/shard_map/layers/pallas_call | solution.py:1471
  159.3 0.0 copy-start.1
  159.4 0.0 copy-start
  159.4 10.3 %unpack.1 = (f32[2,3,9,160,320]{4,3,2,1,0:T(8,128)}, f32[2,3,9,32,128]{4,3,2,1,0:T(8,128)}, f32[2,448,832]{2,1,0:T(8,128)}, f32[2,832,128]{2,1,0:T(8,128)}, f32[2,1024]{1,0:T(2,128)}, /*index=5*/f32[2,1024]{1,0:T(2,128)}) custom-call(bf16[2,1280,16,128]{3,2,1,0:T(8,128)(2,1)} %get-tuple-element.21.taps.low, ...), custom_call_target="tpu_custom_call" | custom-call | tf_op jit(solution)/shard_map/unpack/pallas_call | solution.py:1361
  169.6 0.0 copy-done.1
  169.6 0.7 copy.19
  170.3 0.0 copy-done
  170.3 1.2 copy.20
Async XLA Ops:
  159.3 10.3 %copy-start.1 = (bf16[16,4,2,832]{3,2,1,0:T(2,128)(2,1)S(1)}, bf16[16,4,2,832]{3,2,1,0:T(2,128)(2,1)}, u32[]{:S(2)}) copy-start(bf16[16,4,2,832]{3,2,1,0:T(2,128)(2,1)} %get-tuple-element.38) | copy-start | bytes 638980
  159.4 11.0 %copy-start = (bf16[32,8,4,832]{3,2,1,0:T(4,128)(2,1)S(1)}, bf16[32,8,4,832]{3,2,1,0:T(4,128)(2,1)}, u32[]{:S(2)}) copy-start(bf16[32,8,4,832]{3,2,1,0:T(4,128)(2,1)} %get-tuple-element.39) | copy-start | bytes 5111812

commit v6 on v5

--- a/solution.py
+++ b/solution.py
@@ -36,54 +36,57 @@
     (1, 6): ((1, 0),),
     (1, 8): ((1, 2),),
     (0, 0): ((1, 2), (1, 0),),
-    (0, 1): ((1, 0), (1, 2),),
-    (0, (5, 0)): ((1, 1),),
+    (0, 1): ((1, 2),),
+    (0, (5, 0)): ((1, 0),),
+    (0, (5, 1)): ((1, 1),),
     (0, (5, 3)): ((0, 0),),
-    (0, (5, 5)): ((1, 2),),
+    (0, (5, 4)): ((1, 2),),
     (0, (5, 6)): ((0, 0),),
-    (0, (5, 7)): ((1, 0),),
     (0, (5, 8)): ((0, 1),),
-    (0, (2, 0)): ((1, 1),),
-    (0, (2, 4)): ((1, 2), (0, 0),),
-    (0, (2, 5)): ((0, 1), (1, 1),),
-    (0, (2, 8)): ((1, 0), (0, 0),),
-    (0, 3): ((1, 2),),
-    (0, 6): ((0, 1), (1, 1), (1, 0),),
-    (0, 7): ((1, 2),),
-    (0, 8): ((0, 2), (0, 1), (0, 0),),
+    (0, (2, 0)): ((1, 0),),
+    (0, (2, 1)): ((1, 1),),
+    (0, (2, 3)): ((1, 2),),
+    (0, (2, 5)): ((0, 0),),
+    (0, (2, 6)): ((0, 1),),
+    (0, (2, 7)): ((1, 1),),
+    (0, (2, 8)): ((1, 0),),
+    (0, 4): ((1, 2),),
+    (0, 6): ((0, 0), (0, 1), (1, 1),),
+    (0, 7): ((1, 0),),
+    (0, 8): ((0, 2), (0, 0), (0, 2), (1, 2),),
 }
 EARLY_TAPS = (9, 0)
 LAST_STEPS = (
+    (0, 1),
+    (0, 2),
+    (1, 1),
+    (0, 0),
+    (0, 2),
     (1, 0),
+    (0, 1),
+    (1, 1),
+    (1, 0),
+    (0, 0),
     (0, 2),
     (1, 1),
     (1, 2),
+    (0, 1),
     (1, 0),
-    (1, 0),
-    (0, 1),
+    (1, 1),
     (0, 2),
+    (0, 0),
     (1, 2),
     (1, 1),
+    (0, 1),
     (1, 2),
+    (0, 2),
+    (0, 0),
+    (0, 0),
+    (0, 1),
     (0, 2),
     (0, 1),
     (0, 2),
-    (0, 0),
     (0, 1),
-    (0, 2),
-    (0, 0),
-    (1, 1),
-    (0, 1),
-    (1, 1),
-    (0, 2),
-    (1, 1),
-    (0, 1),
-    (0, 1),
-    (0, 0),
-    (0, 2),
-    (0, 0),
-    (0, 2),
-    (0, 0),
     (0, 2),
 )
 

time: 172 us -> 169 us (0.983)
  Pallas kernels: 169 us -> 166 us
    pallas_call x1, Pallas kernels: 159 us -> 156 us  [on_device(): pl.pallas_call(body, out_shape=list(results.values()), in_specs=[pl.Block...]
where the time goes in v6:
time: 169 us
  Pallas kernels  166 us (98%)
  local copies, waits for them, and re-layouts  1.93 us (1%)
    pallas_call x1, Pallas kernels, on_device(): pl.pallas_call(body, out_shape=list(results.values()), in_specs=[pl.Block...  156 us
    pallas_call x1, Pallas kernels, unpack(): pl.pallas_call(unpack_body, grid=(2, 9 // n), out_shape=[jax.ShapeDtypeSt...  10.3 us

profile of v6, /device:TPU:0, one launch (start us, length us, event | category | flops | bytes accessed | tf_op | source)
XLA Modules:
  0.0 169.0 jit_solution(14623423036620036165)
XLA Ops:
  0.6 156.1 %layers.1 = (bf16[16,4,2,832]{3,2,1,0:T(2,128)(2,1)}, bf16[32,8,4,832]{3,2,1,0:T(4,128)(2,1)}, bf16[2,1280,16,128]{3,2,1,0:T(8,128)(2,1)}, f32[2,1024]{1,0:T(2,128)}, f32[2,1024]{1,0:T(2,128)}) custom-call(bf16[32,8,4,832]{3,2,1,0:T(4,128)(2,1)} %refs_0_.1, s32[2]{0:T(128)} %refs_1_.1, bf16[2,448,832]{2,1,0:T(8,128)(2,1)} %bitcast.7, ...), custom_call_target="tpu_custom_call" | custom-call | tf_op jit(solution)/shard_map/layers/pallas_call | solution.py:1474
  156.7 0.0 copy-start.1
  156.8 0.0 copy-start
  156.8 10.3 %unpack.1 = (f32[2,3,9,160,320]{4,3,2,1,0:T(8,128)}, f32[2,3,9,32,128]{4,3,2,1,0:T(8,128)}, f32[2,448,832]{2,1,0:T(8,128)}, f32[2,832,128]{2,1,0:T(8,128)}, f32[2,1024]{1,0:T(2,128)}, /*index=5*/f32[2,1024]{1,0:T(2,128)}) custom-call(bf16[2,1280,16,128]{3,2,1,0:T(8,128)(2,1)} %get-tuple-element.21.taps.low, ...), custom_call_target="tpu_custom_call" | custom-call | tf_op jit(solution)/shard_map/unpack/pallas_call | solution.py:1364
  167.0 0.0 copy-done.1
  167.0 0.7 copy.19
  167.7 0.0 copy-done
  167.7 1.2 copy.20
Async XLA Ops:
  156.7 10.3 %copy-start.1 = (bf16[16,4,2,832]{3,2,1,0:T(2,128)(2,1)S(1)}, bf16[16,4,2,832]{3,2,1,0:T(2,128)(2,1)}, u32[]{:S(2)}) copy-start(bf16[16,4,2,832]{3,2,1,0:T(2,128)(2,1)} %get-tuple-element.38) | copy-start | bytes 638980
  156.8 11.0 %copy-start = (bf16[32,8,4,832]{3,2,1,0:T(4,128)(2,1)S(1)}, bf16[32,8,4,832]{3,2,1,0:T(4,128)(2,1)}, u32[]{:S(2)}) copy-start(bf16[32,8,4,832]{3,2,1,0:T(4,128)(2,1)} %get-tuple-element.39) | copy-start | bytes 5111812
